TPU v7x, 256 devices: a whole 4x4x8 slice. The times are simulated.
256 devices in a mesh: grp: 4 (over z_lo), wide: 64 (over z_hi, y, x, core).
Axes of the slice: x: 4, y: 4, z: 8 (z_hi: 2, z_lo: 4; z = z_hi * 4 + z_lo), core: 2. Of those that a mesh axis runs over, the one named last changes fastest.
Arguments:
- plan: float32 [8192, 32768], P('grp', 'wide'), may hold values from 0.1 to 10
- cost_source: float32 [8192, 1536], P(('grp', 'wide')), may hold values from -52 to 52
- cost_target: float32 [32768, 1024], P('wide', 'grp'), may hold values from -42 to 42
- potential_col: float32 [1024], replicated, may hold values from -12 to 12
- row_mass: float32 [1536], P(('grp', 'wide')), may hold values from 0.5 to 2
Outputs:
- gradient: float32 [1536, 1024], P(('grp', 'wide'))
- potential_row: float32 [1536], P(('grp', 'wide'))
All inputs are finite; a program needn't handle non-finite values.
Results may differ from a plain program's by a relative error of at most 0.00012.
Values sent between devices are 32-bit elements; how exact they have to be, the bound alone decides.
No kernel may reach another device: no remote copies, remote signals or barrier semaphores. Data moves between devices by JAX's collectives and lax.ppermute only.
A program may use at most 64 MiB of HBM per device.

v0:
```python
import math

import jax
import jax.numpy as jnp
from jax import lax
from jax.sharding import PartitionSpec as P

entropy = 2.0


def body(plan, cost_source, cost_target, potential_col, row_mass):
    highest = lax.Precision.HIGHEST
    n_grp = lax.axis_size("grp")
    n_wide = lax.axis_size("wide")
    num_source = plan.shape[0] * n_grp
    num_target = plan.shape[1] * n_wide
    factor = -2.0 / math.sqrt(num_source * num_target)
    gathered = lax.all_gather(cost_target, "grp", axis=1, tiled=True)
    contract_lead = (((0,), (0,)), ((), ()))
    carried = lax.psum_scatter(
        jnp.dot(plan, gathered, precision=highest), "wide", scatter_dimension=0, tiled=True
    )
    gradient = lax.psum_scatter(
        factor * lax.dot_general(cost_source, carried, contract_lead, precision=highest),
        ("grp", "wide"),
        scatter_dimension=0,
        tiled=True,
    )
    scores = (potential_col[None, :] - gradient) / entropy
    peak = jnp.max(scores, axis=1, keepdims=True)
    log_total = peak[:, 0] + jnp.log(jnp.sum(jnp.exp(scores - peak), axis=1))
    potential_row = entropy * jnp.log(row_mass) - entropy * log_total
    return (gradient, potential_row)


def solution(mesh):
    placed = (P("grp", "wide"), P(("grp", "wide"), None), P("wide", "grp"), P(), P(("grp", "wide")))
    return jax.shard_map(
        body,
        mesh=mesh,
        in_specs=placed,
        out_specs=(P(("grp", "wide"), None), P(("grp", "wide"))),
        check_vma=False,
    )
```

profile of v0, /device:TPU:1, one launch (start us, length us, event | category | flops | bytes accessed | tf_op | source)
XLA Modules:
  0.0 790.7 jit_solution(2605685048633073887)
XLA Ops:
  7.2 0.0 copy-start
  7.2 0.0 all-gather.2.cloned.1.call-start
  7.2 0.7 all-gather.2.cloned.1.call-update
  7.9 0.0 reduce-scatter.3.cloned.1.call-start
  8.0 55.7 %all-gather.2.cloned.1.call-done = f32[512,1024]{1,0:T(8,128)} async-done(((f32[512,256]{1,0:T(8,128)}), f32[512,1024]{1,0:T(8,128)}) %all-gather.2.cloned.1.call-update) | async-done | bytes 2097168 | tf_op jit(solution)/shard_map/all_gather | solution.py:18
  63.7 17.9 %fusion.1 = f32[2048,1024]{1,0:T(8,128)} fusion(f32[2048,512]{1,0:T(8,128)} %param.5, f32[512,1024]{1,0:T(8,128)} %all-gather.2.cloned.1.call-done), kind=kOutput, calls=%fused_computation.6 | convolution fusion | flops 12884901888 | bytes 14680064 | tf_op jit(solution)/shard_map/dot_general | solution.py:21
  81.6 0.0 reduce-scatter.3.cloned.1.call-update
  81.7 0.0 copy-start.2
  81.7 0.0 copy-start.3
  81.7 0.0 all-reduce.3.cloned.1.call-start
  81.7 418.0 %reduce-scatter.3.cloned.1.call-done = f32[32,1024]{1,0:T(8,128)} async-done(((f32[2048,1024]{1,0:T(8,128)}), f32[32,1024]{1,0:T(8,128)}) %reduce-scatter.3.cloned.1.call-update) | async-done | bytes 131088 | tf_op jit(solution)/shard_map/reduce_scatter | solution.py:20
  499.7 0.0 copy-done
  499.7 8.0 %multiply_bitcast_fusion = f32[1536,1024]{0,1:T(8,128)} fusion(f32[32,1024]{1,0:T(8,128)} %reduce-scatter.3.cloned.1.call-done, f32[32,1536]{1,0:T(8,128)S(1)} %copy-done), kind=kOutput, calls=%fused_computation | convolution fusion | flops 605552640 | bytes 6619136 | tf_op jit(solution)/shard_map/dot_general | solution.py:24
  507.8 0.0 all-reduce.3.cloned.1.call-update
  507.8 273.8 %all-reduce.3.cloned.1.call-done = f32[1536,1024]{0,1:T(8,128)} async-done(((f32[1536,1024]{0,1:T(8,128)}), f32[1536,1024]{0,1:T(8,128)}) %all-reduce.3.cloned.1.call-update) | async-done | bytes 6291472
  781.6 1.4 constant_dynamic-slice_fusion
  783.1 0.2 copy.10
  783.3 0.0 copy-done.2
  783.3 0.0 copy-start.1
  783.3 0.1 fusion
  783.4 0.2 exponential_reduce_fusion
  783.6 0.0 copy-done.3
  783.6 0.5 multiply_subtract_fusion
  784.1 0.0 copy-done.1
Async XLA Ops:
  7.2 492.6 %copy-start = (f32[32,1536]{1,0:T(8,128)S(1)}, f32[32,1536]{1,0:T(8,128)}, u32[]{:S(2)}) copy-start(f32[32,1536]{1,0:T(8,128)} %param.6) | copy-start | bytes 589828
  7.2 56.5 %all-gather.2.cloned.1.call-start = ((), (), s32[]{:S(2)}) async-start(), calls=%async_computation.1 | async-start | bytes 2621440 | tf_op jit(solution)/shard_map/all_gather | solution.py:18
  7.9 491.8 %reduce-scatter.3.cloned.1.call-start = ((), (), s32[]{:S(2)}) async-start(), calls=%async_computation.2 | async-start | bytes 8519680 | tf_op jit(solution)/shard_map/reduce_scatter | solution.py:20
  81.7 701.6 %copy-start.2 = (f32[1024]{0:T(1024)S(1)}, f32[1024]{0:T(1024)}, u32[]{:S(2)}) copy-start(f32[1024]{0:T(1024)} %param.8) | copy-start | bytes 12292
  81.7 701.9 %copy-start.3 = (f32[6]{0:T(128)S(1)}, f32[6]{0:T(128)}, u32[]{:S(2)}) copy-start(f32[6]{0:T(128)} %param.9) | copy-start | bytes 76
  81.7 700.0 %all-reduce.3.cloned.1.call-start = ((), (), s32[]{:S(2)}) async-start(), calls=%async_computation.3 | async-start | bytes 12582912
  783.3 0.9 copy-start.1
Sparse Core Ops, SparseCore 0:
  9.8 53.8 all-gather.1
  81.8 417.9 reduce-scatter.2
  507.9 273.6 all-reduce.2
where the time goes:
time: 792 us; the launch traced here: 791 us
  waiting for transfers between devices  748 us (94%)
  matrix products  26 us (3%)
  between operations  13.8 us (2%)
    reduce_scatter x1, waiting for transfers between devices, body(): lax.psum_scatter(jnp.dot(plan, gathered, precision=highest), 'wide', scat...  418 us
    unnamed x4, waiting for transfers between devices  275 us
    all_gather x1, waiting for transfers between devices, body(): gathered = lax.all_gather(cost_target, 'grp', axis=1, tiled=True)  55.7 us
    dot_general x1, matrix products, body(): jnp.dot(plan, gathered, precision=highest)  17.9 us
  transfers between devices with their start and end apart: 3, of which 3 were waited for; matrix products, arithmetic and copies ran while one was open for 0% of the time, Pallas kernels for 0%

commit v1 on v0

v1 whole, which is shorter than its diff:
```python
import math

import jax
import jax.numpy as jnp
from jax import lax
from jax.experimental import pallas as pl
from jax.experimental.pallas import tpu as pltpu
from jax.sharding import PartitionSpec as P

entropy = 2.0
NX = NY = 4
NC = 2
NH = 2
NG = 4
WIDE = NH * NY * NX * NC


def coords(w):
    return w // (NY * NX * NC), (w // (NX * NC)) % NY, (w // NC) % NX, w % NC


def wide_index(h, y, x, c):
    return ((h * NY + y % NY) * NX + x % NX) * NC + c


def wide_pairs(move):
    return [(w, wide_index(*move(*coords(w)))) for w in range(WIDE)]


def first_pairs(d):
    return wide_pairs(lambda h, y, x, c: (h, y, x + d, c) if c == 0 else (h, y + d, x, c))


def second_pairs(d):
    return wide_pairs(lambda h, y, x, c: (h, y + d, x, c) if c == 0 else (h, y, x + d, c))


CORE_SWAP = wide_pairs(lambda h, y, x, c: (h, y, x, 1 - c))
H_SWAP = wide_pairs(lambda h, y, x, c: (1 - h, y, x, c))


def y_pairs(d):
    return wide_pairs(lambda h, y, x, c: (h, y + d, x, c))


def halves(v):
    hi = v.astype(jnp.bfloat16)
    return hi, (v - hi.astype(jnp.float32)).astype(jnp.bfloat16)


def dot3(a, b):
    (ah, al), (bh, bl) = a, b

    def dot(u, v):
        return jnp.dot(u, v, preferred_element_type=jnp.float32)

    return dot(ah, bh) + (dot(ah, bl) + dot(al, bh))


def carry_kernel(place, *refs, n_blocks):
    plan_ref, blocks, (own_ref, send_ref) = refs[0], refs[1 : 1 + n_blocks], refs[1 + n_blocks :]
    c, x, y = place[0], place[1], place[2]
    xx = pl.program_id(0)
    rows = plan_ref[...].reshape(-1, plan_ref.shape[-1])
    block = blocks[0][...]
    for other in blocks[1:]:
        block = block + other[...]
    out = dot3(halves(rows), halves(block)).T
    part = out.shape[0] // (NC * NY)
    for cc in range(NC):
        for yy in range(NY):
            chunk = out[(cc * NY + yy) * part : (cc * NY + yy + 1) * part, :]
            dx, dy = lax.rem(xx - x + NX, NX), lax.rem(yy - y + NY, NY)
            d1, d2 = (dx, dy) if cc == 0 else (dy, dx)

            @pl.when(c == cc)
            def _():
                own_ref[d1, d2] = chunk

            @pl.when(c != cc)
            def _():
                send_ref[d1, d2] = chunk


def carry(place, plan5, blocks):
    groups, nx, run, depth = plan5.shape
    cols = blocks[0].shape[1]
    part = cols // (NC * NY)
    out = jax.ShapeDtypeStruct((4, 4, part, groups * run), jnp.float32)
    whole = pl.BlockSpec(out.shape, lambda i, s: (0, 0, 0, 0))
    return pl.pallas_call(
        lambda place, *refs: carry_kernel(place, *refs, n_blocks=len(blocks)),
        grid_spec=pltpu.PrefetchScalarGridSpec(
            num_scalar_prefetch=1,
            grid=(nx,),
            in_specs=[pl.BlockSpec((groups, 1, run, depth), lambda i, s: (0, i, 0, 0))]
            + [pl.BlockSpec(b.shape, lambda i, s: (0, 0)) for b in blocks],
            out_specs=[whole, whole],
        ),
        out_shape=[out, out],
        compiler_params=pltpu.CompilerParams(vmem_limit_bytes=32 * 1024 * 1024),
        cost_estimate=pl.CostEstimate(
            flops=6 * groups * nx * run * depth * cols, bytes_accessed=4 * 1024 * 1024, transcendentals=0
        ),
        name="carry",
    )(place, plan5, *blocks)


def grad_kernel(place, *refs, factor):
    pieces, blocks, out_ref, cost, held = refs[:4], refs[4:8], refs[8], refs[9], refs[10]
    c, y, h, g = place[0], place[2], place[3], place[4]
    run = pieces[0].shape[1]
    for dh in range(NH):
        for dc in range(NC):
            for d in range(NY):
                hh = lax.rem(h + dh, NH)
                cc = lax.rem(c + dc, NC)
                yy = lax.rem(y - d + NY, NY)
                at = pl.multiple_of(((hh * NY + yy) * NC + cc) * run, run)
                cost[pl.ds(at, run), :] = pieces[dh * NC + dc][d]
    part = blocks[0].shape[0]
    low = g < 2
    order = [g, g + 1 - 2 * lax.rem(g, 2), jnp.where(low, 2, 1), jnp.where(low, 3, 0)]
    for j, block in zip(order, blocks, strict=True):
        held[pl.ds(pl.multiple_of(j * part, part), part), :] = block[...]
    left = halves(held[...])
    step = 512
    for at in range(0, cost.shape[1], step):
        out = dot3(left, halves(cost[:, at : at + step]))
        out_ref[at : at + step, :] = factor * out.T


def grad(place, pieces, blocks, factor):
    rows = NH * NC * NY * pieces[0].shape[1]
    width = pieces[0].shape[2]
    cols = 4 * blocks[0].shape[0]
    vmem = pl.BlockSpec(memory_space=pltpu.VMEM)
    return pl.pallas_call(
        lambda place, *refs: grad_kernel(place, *refs, factor=factor),
        in_specs=[pl.BlockSpec(memory_space=pltpu.SMEM)] + [vmem] * 8,
        out_specs=vmem,
        out_shape=jax.ShapeDtypeStruct((width, cols), jnp.float32),
        scratch_shapes=[pltpu.VMEM((rows, width), jnp.float32), pltpu.VMEM((cols, rows), jnp.float32)],
        compiler_params=pltpu.CompilerParams(vmem_limit_bytes=32 * 1024 * 1024),
        cost_estimate=pl.CostEstimate(flops=6 * rows * width * cols, bytes_accessed=4 * 1024 * 1024, transcendentals=0),
        name="grad",
    )(place, *pieces, *blocks)


def after(value, *others):
    return lax.optimization_barrier((value, *others))[0]


def body(plan, cost_source, cost_target, potential_col, row_mass):
    num_source = plan.shape[0] * NG
    num_target = plan.shape[1] * WIDE
    factor = -2.0 / math.sqrt(num_source * num_target)
    g = lax.axis_index("grp")
    w = lax.axis_index("wide")
    h, y, x, c = coords(w)
    place = jnp.stack([c, x, y, h, g]).astype(jnp.int32)
    run = NC * cost_source.shape[0]
    plan5 = plan.reshape(NH * NY, NX, run, plan.shape[1])

    def wide(v, pairs):
        return lax.ppermute(v, "wide", pairs)

    pair = lax.ppermute(cost_target, "grp", [(0, 1), (1, 0), (2, 3), (3, 2)])
    mid1 = lax.ppermute(cost_target, "grp", [(1, 2), (2, 1)])
    mid2 = lax.ppermute(pair, "grp", [(1, 2), (2, 1)])
    end1 = lax.ppermute(mid1, "grp", [(1, 0), (2, 3)])
    end2 = lax.ppermute(mid2, "grp", [(1, 0), (2, 3)])

    def gather_y(v):
        piece = jnp.stack([v] + [wide(v, y_pairs(d)) for d in (1, 2, 3)])
        return piece, wide(piece, CORE_SWAP)

    def exchange(blocks):
        own, send = carry(place, plan5, blocks)
        got = wide(send, CORE_SWAP)
        parts = [own[d] + got[d] for d in range(4)]
        return parts[0] + sum(wide(parts[d], first_pairs(d)) for d in (1, 2, 3))

    def finish(total):
        return total[0] + sum(wide(total[d], second_pairs(d)) for d in (1, 2, 3))

    pieces = gather_y(cost_source)
    done = [finish(exchange(blocks)) for blocks in ((cost_target,), (pair,), (mid1, end1), (mid2, end2))]
    far = wide(after(cost_source, end2), H_SWAP)
    pieces += gather_y(far)
    partial = grad(place, pieces, done, factor)

    n_all = NG * WIDE
    rows = partial.shape[0] // n_all
    parts = lax.all_to_all(partial.reshape(n_all, rows, -1), ("grp", "wide"), 0, 0, tiled=True)
    parts = parts.reshape(NG, NH, NY, NX, NC, rows, 4, -1)
    summed = parts.sum(axis=(0, 1, 3))
    gradient = summed.transpose(2, 3, 1, 0, 4).reshape(rows, -1)

    scores = (potential_col[None, :] - gradient) / entropy
    peak = jnp.max(scores, axis=1, keepdims=True)
    log_total = peak[:, 0] + jnp.log(jnp.sum(jnp.exp(scores - peak), axis=1))
    potential_row = entropy * jnp.log(row_mass) - entropy * log_total
    return (gradient, potential_row)


def solution(mesh):
    placed = (P("grp", "wide"), P(("grp", "wide"), None), P("wide", "grp"), P(), P(("grp", "wide")))
    return jax.shard_map(
        body,
        mesh=mesh,
        in_specs=placed,
        out_specs=(P(("grp", "wide"), None), P(("grp", "wide"))),
        check_vma=False,
    )
```

time: 792 us -> 191 us (0.24)
  waiting for transfers between devices: 748 us -> 81.6 us
  starting transfers between devices: 0.12 us -> 79.1 us
  matrix products: 26 us -> 0 us
  Pallas kernels: 0 us -> 17.2 us
  between operations: 13.8 us -> 1.03 us
    reduce_scatter x1 -> x0, waiting for transfers between devices: 418 us -> none  [body(): lax.psum_scatter(jnp.dot(plan, gathered, precision=highest), 'wide', scat...]
    unnamed x4 -> x0, waiting for transfers between devices: 275 us -> none
    ppermute x0 -> x42, starting transfers between devices: none -> 61.2 us  [the longest x37 54.4 us: wide(): return lax.ppermute(v, 'wide', pairs)]
    all_gather x1 -> x0, waiting for transfers between devices: 55.7 us -> none  [body(): gathered = lax.all_gather(cost_target, 'grp', axis=1, tiled=True)]
    ppermute x0 -> x42, waiting for transfers between devices: none -> 49.1 us  [the longest x37 29.5 us: wide(): return lax.ppermute(v, 'wide', pairs)]
    all_to_all x0 -> x1, waiting for transfers between devices: none -> 32.5 us  [body(): lax.all_to_all(partial.reshape(n_all, rows, -1), ('grp', 'wide'), 0, 0, t...]
    dot_general x2 -> x0, matrix products: 26 us -> none  [the longest x1 17.9 us: body(): jnp.dot(plan, gathered, precision=highest)]
    all_to_all x0 -> x1, starting transfers between devices: none -> 17.9 us  [body(): lax.all_to_all(partial.reshape(n_all, rows, -1), ('grp', 'wide'), 0, 0, t...]
  transfers between devices with their start and end apart: 3 -> 43, of which waited for: 3 -> 14; matrix products, arithmetic and copies ran while one was open for 0% -> 1% of each run, Pallas kernels for 0% -> 6%
where the time goes in v1:
time: 191 us
  waiting for transfers between devices  81.6 us (43%)
  starting transfers between devices  79.1 us (41%)
  Pallas kernels  17.2 us (9%)
  local copies, waits for them, and re-layouts  8.91 us (5%)
  other arithmetic  2.93 us (2%)
    ppermute x37, starting transfers between devices, wide(): return lax.ppermute(v, 'wide', pairs)  54.4 us
    all_to_all x1, waiting for transfers between devices, body(): lax.all_to_all(partial.reshape(n_all, rows, -1), ('grp', 'wide'), 0, 0, t...  32.5 us
    ppermute x37, waiting for transfers between devices, wide(): return lax.ppermute(v, 'wide', pairs)  29.5 us
    all_to_all x1, starting transfers between devices, body(): lax.all_to_all(partial.reshape(n_all, rows, -1), ('grp', 'wide'), 0, 0, t...  17.9 us
    pallas_call x4, Pallas kernels, carry(): pl.pallas_call(lambda place, *refs: carry_kernel(place, *refs, n_blocks=l...  15.5 us
    ppermute x1, waiting for transfers between devices, body(): end2 = lax.ppermute(mid2, 'grp', [(1, 0), (2, 3)])  10.1 us
    ppermute x1, waiting for transfers between devices, body(): pair = lax.ppermute(cost_target, 'grp', [(0, 1), (1, 0), (2, 3), (3, 2)])  9.49 us
  transfers between devices with their start and end apart: 43, of which 14 were waited for; matrix products, arithmetic and copies ran while one was open for 1% of the time, Pallas kernels for 6%

profile of v1, /device:TPU:1, one launch (start us, length us, event | category | flops | bytes accessed | tf_op | source)
XLA Modules:
  0.0 190.7 jit_solution(6062859687821754467)
XLA Ops:
  0.8 2.2 %copy-done = f32[2048,512]{1,0:T(8,128)S(1)} copy-done((f32[2048,512]{1,0:T(8,128)S(1)}, f32[2048,512]{1,0:T(8,128)}, u32[]{:S(2)}) %copy-start) | copy-done | bytes 4194328
  3.0 1.0 copy-done.1
  4.0 3.8 %carry.4 = (f32[4,4,32,512]{3,2,1,0:T(8,128)S(1)}, f32[4,4,32,512]{3,2,1,0:T(8,128)S(1)}) custom-call(s32[5]{0:T(128)S(1)} %stack.53.place, f32[8,4,64,512]{3,2,1,0:T(8,128)S(1)} %bitcast.99, f32[512,256]{1,0:T(8,128)S(1)} %copy-done.1), custom_call_target="tpu_custom_call" | custom-call | flops 1610612736 | bytes 4194304 | tf_op jit(solution)/shard_map/carry/pallas_call | solution.py:91
  7.9 3.4 %collective-permute-start.12 = (f32[4,4,32,512]{3,2,1,0:T(8,128)S(1)}, f32[4,4,32,512]{3,2,1,0:T(8,128)S(1)}, u32[]{:S(2)}, u32[]{:S(2)}) collective-permute-start(f32[4,4,32,512]{3,2,1,0:T(8,128)S(1)} %get-tuple-element.13), channel_id=1, source_target_pairs={{0,1},{1,0},{2,3},{3,2},{4,5},{5,4},{6,7},{7,6},{8,9},{9,8},{10,11... | collective-permute-start | bytes 3145736 | tf_op jit(solution)/shard_map/ppermute | solution.py:166
  11.2 0.7 collective-permute-start.26
  11.9 2.8 %collective-permute-start.4 = (f32[512,256]{1,0:T(8,128)S(1)}, f32[512,256]{1,0:T(8,128)S(1)}, u32[]{:S(2)}, u32[]{:S(2)}) collective-permute-start(f32[512,256]{1,0:T(8,128)S(1)} %copy-done.1), channel_id=1, source_target_pairs={{0,64},{64,0},{128,192},{192,128},{1,65},{65,1},{129,193},{193,129... | collective-permute-start | bytes 1572872 | tf_op jit(solution)/shard_map/ppermute | solution.py:168
  14.8 1.3 collective-permute-start
  16.0 1.3 collective-permute-start.27
  17.3 9.5 %collective-permute-done.4.refs_1_ = f32[512,256]{1,0:T(8,128)S(1)} collective-permute-done((f32[512,256]{1,0:T(8,128)S(1)}, f32[512,256]{1,0:T(8,128)S(1)}, u32[]{:S(2)}, u32[]{:S(2)}) %collective-permute-start.4) | collective-permute-done | bytes 524320 | tf_op jit(solution)/shard_map/ppermute | solution.py:168
  26.8 3.8 %carry.5 = (f32[4,4,32,512]{3,2,1,0:T(8,128)S(1)}, f32[4,4,32,512]{3,2,1,0:T(8,128)S(1)}) custom-call(s32[5]{0:T(128)S(1)} %stack.53.place, f32[8,4,64,512]{3,2,1,0:T(8,128)S(1)} %bitcast.100, f32[512,256]{1,0:T(8,128)S(1)} %collective-permute-done.4.refs_1_), custom_call_target="tpu_custom_call" | custom-call | flops 1610612736 | bytes 4194304 | tf_op jit(solution)/shard_map/carry/pallas_call | solution.py:91
  30.7 0.9 collective-permute-start.19
  31.6 2.9 %collective-permute-start.1 = (f32[32,1536]{1,0:T(8,128)S(1)}, f32[32,1536]{1,0:T(8,128)S(1)}, u32[]{:S(2)}, u32[]{:S(2)}) collective-permute-start(f32[32,1536]{1,0:T(8,128)S(1)} %copy-done.2), channel_id=1, source_target_pairs={{0,16},{1,17},{2,18},{3,19},{4,20},{5,21},{6,22},{7,23},{8,24},{9,... | collective-permute-start | bytes 589832 | tf_op jit(solution)/shard_map/ppermute | solution.py:166
  34.5 0.8 collective-permute-start.2
  35.3 0.7 collective-permute-start.5
  36.1 3.4 %collective-permute-done.1 = f32[32,1536]{1,0:T(8,128)S(1)} collective-permute-done((f32[32,1536]{1,0:T(8,128)S(1)}, f32[32,1536]{1,0:T(8,128)S(1)}, u32[]{:S(2)}, u32[]{:S(2)}) %collective-permute-start.1) | collective-permute-done | bytes 196640 | tf_op jit(solution)/shard_map/ppermute | solution.py:166
  39.6 1.3 collective-permute-start.13
  40.9 3.3 %collective-permute-done.2 = f32[32,1536]{1,0:T(8,128)S(1)} collective-permute-done((f32[32,1536]{1,0:T(8,128)S(1)}, f32[32,1536]{1,0:T(8,128)S(1)}, u32[]{:S(2)}, u32[]{:S(2)}) %collective-permute-start.2) | collective-permute-done | bytes 196640 | tf_op jit(solution)/shard_map/ppermute | solution.py:166
  44.2 1.6 collective-permute-start.14
  45.7 2.1 %collective-permute-start.15 = (f32[4,32,512]{2,1,0:T(8,128)S(1)}, f32[4,32,512]{2,1,0:T(8,128)S(1)}, u32[]{:S(2)}, u32[]{:S(2)}) collective-permute-start(f32[4,32,512]{2,1,0:T(8,128)S(1)} %get-tuple-element.30), channel_id=1, source_target_pairs={{0,6},{1,25},{2,0},{3,27},{4,2},{5,29},{6,4},{7,31},{8,14},{9,1},{... | collective-permute-start | bytes 786440 | tf_op jit(solution)/shard_map/ppermute | solution.py:166
  47.9 3.9 %carry.6 = (f32[4,4,32,512]{3,2,1,0:T(8,128)S(1)}, f32[4,4,32,512]{3,2,1,0:T(8,128)S(1)}) custom-call(s32[5]{0:T(128)S(1)} %stack.53.place, f32[8,4,64,512]{3,2,1,0:T(8,128)S(1)} %bitcast.101, f32[512,256]{1,0:T(8,128)S(1)} %collective-permute-done.26.refs_1_, f32[512,256]{1,0:T(8,128)S(1)} %collective-permute-done.27.refs_2_), custom_call_target="tpu_custom_call" | custom-call | flops 1610612736 | bytes 4194304 | tf_op jit(solution)/shard_map/carry/pallas_call | solution.py:91
  51.8 1.4 collective-permute-start.28
  53.3 1.3 collective-permute-start.6
  54.9 1.0 collective-permute-start.20
  55.9 2.6 %collective-permute-start.21 = (f32[4,32,512]{2,1,0:T(8,128)S(1)}, f32[4,32,512]{2,1,0:T(8,128)S(1)}, u32[]{:S(2)}, u32[]{:S(2)}) collective-permute-start(f32[4,32,512]{2,1,0:T(8,128)S(1)} %get-tuple-element.26), channel_id=1, source_target_pairs={{0,4},{1,17},{2,6},{3,19},{4,0},{5,21},{6,2},{7,23},{8,12},{9,25},... | collective-permute-start | bytes 786440 | tf_op jit(solution)/shard_map/ppermute | solution.py:166
  58.6 10.1 %collective-permute-done.6.refs_2_ = f32[512,256]{1,0:T(8,128)S(1)} collective-permute-done((f32[512,256]{1,0:T(8,128)S(1)}, f32[512,256]{1,0:T(8,128)S(1)}, u32[]{:S(2)}, u32[]{:S(2)}) %collective-permute-start.6) | collective-permute-done | bytes 524320 | tf_op jit(solution)/shard_map/ppermute | solution.py:172
  68.7 0.6 collective-permute-start.16
  69.3 3.9 %carry.7 = (f32[4,4,32,512]{3,2,1,0:T(8,128)S(1)}, f32[4,4,32,512]{3,2,1,0:T(8,128)S(1)}) custom-call(s32[5]{0:T(128)S(1)} %stack.53.place, f32[8,4,64,512]{3,2,1,0:T(8,128)S(1)} %bitcast.102, f32[512,256]{1,0:T(8,128)S(1)} %collective-permute-done.5.refs_1_, f32[512,256]{1,0:T(8,128)S(1)} %collective-permute-done.6.refs_2_), custom_call_target="tpu_custom_call" | custom-call | flops 1610612736 | bytes 4194304 | tf_op jit(solution)/shard_map/carry/pallas_call | solution.py:91
  73.2 1.3 collective-permute-start.17
  74.5 1.2 collective-permute-start.18
  75.7 2.3 %collective-permute-start.35 = (f32[4,4,32,512]{3,2,1,0:T(8,128)S(1)}, f32[4,4,32,512]{3,2,1,0:T(8,128)S(1)}, u32[]{:S(2)}, u32[]{:S(2)}) collective-permute-start(f32[4,4,32,512]{3,2,1,0:T(8,128)S(1)} %get-tuple-element.19), channel_id=1, source_target_pairs={{0,1},{1,0},{2,3},{3,2},{4,5},{5,4},{6,7},{7,6},{8,9},{9,8},{10,11... | collective-permute-start | bytes 3145736 | tf_op jit(solution)/shard_map/ppermute | solution.py:166
  78.1 5.2 %collective-permute-start.7 = (f32[32,1536]{1,0:T(8,128)S(1)}, f32[32,1536]{1,0:T(8,128)S(1)}, u32[]{:S(2)}, u32[]{:S(2)}) collective-permute-start(f32[32,1536]{1,0:T(8,128)S(1)} %copy-done.2), channel_id=1, source_target_pairs={{0,32},{1,33},{2,34},{3,35},{4,36},{5,37},{6,38},{7,39},{8,40},{9,... | collective-permute-start | bytes 589832 | tf_op jit(solution)/shard_map/ppermute | solution.py:166
  83.4 0.7 collective-permute-start.23
  84.0 1.6 collective-permute-start.24
  85.6 5.6 %collective-permute-done.7 = f32[32,1536]{1,0:T(8,128)S(1)} collective-permute-done((f32[32,1536]{1,0:T(8,128)S(1)}, f32[32,1536]{1,0:T(8,128)S(1)}, u32[]{:S(2)}, u32[]{:S(2)}) %collective-permute-start.7) | collective-permute-done | bytes 196640 | tf_op jit(solution)/shard_map/ppermute | solution.py:166
  91.2 1.0 collective-permute-start.25
  92.3 0.7 collective-permute-start.3
  93.0 0.9 collective-permute-start.8
  94.3 1.4 collective-permute-start.9
  95.8 2.4 %collective-permute-start.10 = (f32[32,1536]{1,0:T(8,128)S(1)}, f32[32,1536]{1,0:T(8,128)S(1)}, u32[]{:S(2)}, u32[]{:S(2)}) collective-permute-start(f32[32,1536]{1,0:T(8,128)S(1)} %collective-permute-done.7), channel_id=1, source_target_pairs={{0,24},{1,25},{2,26},{3,27},{4,28},{5,29},{6,30},{7,31},{8,0},{9,1... | collective-permute-start | bytes 589832 | tf_op jit(solution)/shard_map/ppermute | solution.py:166
  98.4 2.3 %collective-permute-done.8 = f32[32,1536]{1,0:T(8,128)S(1)} collective-permute-done((f32[32,1536]{1,0:T(8,128)S(1)}, f32[32,1536]{1,0:T(8,128)S(1)}, u32[]{:S(2)}, u32[]{:S(2)}) %collective-permute-start.8) | collective-permute-done | bytes 196640 | tf_op jit(solution)/shard_map/ppermute | solution.py:166
  100.7 4.3 %collective-permute-done.9 = f32[32,1536]{1,0:T(8,128)S(1)} collective-permute-done((f32[32,1536]{1,0:T(8,128)S(1)}, f32[32,1536]{1,0:T(8,128)S(1)}, u32[]{:S(2)}, u32[]{:S(2)}) %collective-permute-start.9) | collective-permute-done | bytes 196640 | tf_op jit(solution)/shard_map/ppermute | solution.py:166
  105.0 1.1 collective-permute-start.30
  106.1 0.6 collective-permute-start.31
  106.8 3.7 %collective-permute-start.11 = (f32[4,32,1536]{2,1,0:T(8,128)S(1)}, f32[4,32,1536]{2,1,0:T(8,128)S(1)}, u32[]{:S(2)}, u32[]{:S(2)}) collective-permute-start(f32[4,32,1536]{2,1,0:T(8,128)S(1)} %pad_maximum_fusion.1.refs_2_), channel_id=1, source_target_pairs={{0,1},{1,0},{2,3},{3,2},{4,5},{5,4},{6,7},{7,6},{8,9},{9,8},{10,11... | collective-permute-start | bytes 2359304 | tf_op jit(solution)/shard_map/ppermute | solution.py:166
  110.7 1.3 collective-permute-done.30
  112.0 1.2 collective-permute-start.37
  113.2 1.0 collective-permute-start.38
  114.4 5.6 %collective-permute-done.36 = f32[4,32,512]{2,1,0:T(8,128)S(1)} collective-permute-done((f32[4,32,512]{2,1,0:T(8,128)S(1)}, f32[4,32,512]{2,1,0:T(8,128)S(1)}, u32[]{:S(2)}, u32[]{:S(2)}) %collective-permute-start.36) | collective-permute-done | bytes 262176 | tf_op jit(solution)/shard_map/ppermute | solution.py:166
  119.9 2.5 %collective-permute-start.33 = (f32[32,512]{1,0:T(8,128)S(1)}, f32[32,512]{1,0:T(8,128)S(1)}, u32[]{:S(2)}, u32[]{:S(2)}) collective-permute-start(f32[32,512]{1,0:T(8,128)S(1)} %get-tuple-element.35), channel_id=1, source_target_pairs={{0,16},{1,5},{2,18},{3,7},{4,20},{5,1},{6,22},{7,3},{8,24},{9,13},... | collective-permute-start | bytes 196616 | tf_op jit(solution)/shard_map/ppermute | solution.py:166
  122.5 1.5 collective-permute-start.34
  124.1 1.3 collective-permute-done.32
  125.4 1.7 collective-permute-start.40
  127.1 2.2 %collective-permute-start.41 = (f32[32,512]{1,0:T(8,128)S(1)}, f32[32,512]{1,0:T(8,128)S(1)}, u32[]{:S(2)}, u32[]{:S(2)}) collective-permute-start(f32[32,512]{1,0:T(8,128)S(1)} %get-tuple-element.33), channel_id=1, source_target_pairs={{0,24},{1,7},{2,26},{3,1},{4,28},{5,3},{6,30},{7,5},{8,0},{9,15},{... | collective-permute-start | bytes 196616 | tf_op jit(solution)/shard_map/ppermute | solution.py:166
  129.4 1.1 collective-permute-done.39
  130.4 0.9 collective-permute-done.41
  131.4 1.8 grad.1
  133.1 1.1 reshape.49
  134.2 17.9 %all-to-all-start = ((f32[256,6,128]{2,1,0:T(8,128)}), f32[256,6,128]{2,1,0:T(8,128)S(1)}, u32[]{:S(2)}, u32[]{:S(2)}) async-start(f32[256,6,128]{2,1,0:T(8,128)} %reshape.49), calls=%async_computation | async-start | bytes 2097152 | tf_op jit(solution)/shard_map/all_to_all | solution.py:195
  152.2 32.5 %all-to-all-done = f32[256,6,128]{2,1,0:T(8,128)S(1)} async-done(((f32[256,6,128]{2,1,0:T(8,128)}), f32[256,6,128]{2,1,0:T(8,128)S(1)}, u32[]{:S(2)}, u32[]{:S(2)}) %all-to-all-start) | async-done | bytes 786464 | tf_op jit(solution)/shard_map/all_to_all | solution.py:195
  184.7 1.0 copy.9
  185.7 2.5 %reshape.50 = f32[4,2,4,4,2,6,4,32]{7,6,4,3,2,1,0,5:T(4,128)S(1)} reshape(f32[256,6,128]{2,0,1:T(8,128)} %copy.9) | data formatting | bytes 1572864 | tf_op jit(solution)/shard_map/reshape | solution.py:196
  188.3 0.8 reduce_sum.18
  189.5 0.7 reshape.51
  190.2 0.5 multiply_subtract_fusion
  (67 shorter events, 2.5 us)
Async XLA Ops:
  0.8 2.2 %copy-start = (f32[2048,512]{1,0:T(8,128)S(1)}, f32[2048,512]{1,0:T(8,128)}, u32[]{:S(2)}) copy-start(f32[2048,512]{1,0:T(8,128)} %param.5) | copy-start | bytes 12582916
  3.0 1.0 copy-start.1
  4.0 10.7 %copy-start.2 = (f32[32,1536]{1,0:T(8,128)S(1)}, f32[32,1536]{1,0:T(8,128)}, u32[]{:S(2)}) copy-start(f32[32,1536]{1,0:T(8,128)} %param.6) | copy-start | bytes 589828
  7.9 27.4 %collective-permute-start.12 = (f32[4,4,32,512]{3,2,1,0:T(8,128)S(1)}, f32[4,4,32,512]{3,2,1,0:T(8,128)S(1)}, u32[]{:S(2)}, u32[]{:S(2)}) collective-permute-start(f32[4,4,32,512]{3,2,1,0:T(8,128)S(1)} %get-tuple-element.13), channel_id=1, source_target_pairs={{0,1},{1,0},{2,3},{3,2},{4,5},{5,4},{6,7},{7,6},{8,9},{9,8},{10,11... | collective-permute-start | bytes 3145736 | tf_op jit(solution)/shard_map/ppermute | solution.py:166
  11.2 4.8 %collective-permute-start.26 = (f32[512,256]{1,0:T(8,128)S(1)}, f32[512,256]{1,0:T(8,128)S(1)}, u32[]{:S(2)}, u32[]{:S(2)}) collective-permute-start(f32[512,256]{1,0:T(8,128)S(1)} %copy-done.1), channel_id=1, source_target_pairs={{64,128},{128,64},{65,129},{129,65},{66,130},{130,66},{67,131},{13... | collective-permute-start | bytes 1572872 | tf_op jit(solution)/shard_map/ppermute | solution.py:169
  11.9 14.9 %collective-permute-start.4 = (f32[512,256]{1,0:T(8,128)S(1)}, f32[512,256]{1,0:T(8,128)S(1)}, u32[]{:S(2)}, u32[]{:S(2)}) collective-permute-start(f32[512,256]{1,0:T(8,128)S(1)} %copy-done.1), channel_id=1, source_target_pairs={{0,64},{64,0},{128,192},{192,128},{1,65},{65,1},{129,193},{193,129... | collective-permute-start | bytes 1572872 | tf_op jit(solution)/shard_map/ppermute | solution.py:168
  14.8 19.8 %collective-permute-start = (f32[32,1536]{1,0:T(8,128)S(1)}, f32[32,1536]{1,0:T(8,128)S(1)}, u32[]{:S(2)}, u32[]{:S(2)}) collective-permute-start(f32[32,1536]{1,0:T(8,128)S(1)} %copy-done.2), channel_id=1, source_target_pairs={{0,8},{1,9},{2,10},{3,11},{4,12},{5,13},{6,14},{7,15},{8,16},{9,17... | collective-permute-start | bytes 589832 | tf_op jit(solution)/shard_map/ppermute | solution.py:166
  16.0 29.7 %collective-permute-start.27 = (f32[512,256]{1,0:T(8,128)S(1)}, f32[512,256]{1,0:T(8,128)S(1)}, u32[]{:S(2)}, u32[]{:S(2)}) collective-permute-start(f32[512,256]{1,0:T(8,128)S(1)} %collective-permute-done.26.refs_1_), channel_id=1, source_target_pairs={{64,0},{128,192},{65,1},{129,193},{66,2},{130,194},{67,3},{131,195... | collective-permute-start | bytes 1572872 | tf_op jit(solution)/shard_map/ppermute | solution.py:171
  30.7 24.0 %collective-permute-start.19 = (f32[4,4,32,512]{3,2,1,0:T(8,128)S(1)}, f32[4,4,32,512]{3,2,1,0:T(8,128)S(1)}, u32[]{:S(2)}, u32[]{:S(2)}) collective-permute-start(f32[4,4,32,512]{3,2,1,0:T(8,128)S(1)} %get-tuple-element.15), channel_id=1, source_target_pairs={{0,1},{1,0},{2,3},{3,2},{4,5},{5,4},{6,7},{7,6},{8,9},{9,8},{10,11... | collective-permute-start | bytes 3145736 | tf_op jit(solution)/shard_map/ppermute | solution.py:166
  31.6 8.0 %collective-permute-start.1 = (f32[32,1536]{1,0:T(8,128)S(1)}, f32[32,1536]{1,0:T(8,128)S(1)}, u32[]{:S(2)}, u32[]{:S(2)}) collective-permute-start(f32[32,1536]{1,0:T(8,128)S(1)} %copy-done.2), channel_id=1, source_target_pairs={{0,16},{1,17},{2,18},{3,19},{4,20},{5,21},{6,22},{7,23},{8,24},{9,... | collective-permute-start | bytes 589832 | tf_op jit(solution)/shard_map/ppermute | solution.py:166
  34.5 9.6 %collective-permute-start.2 = (f32[32,1536]{1,0:T(8,128)S(1)}, f32[32,1536]{1,0:T(8,128)S(1)}, u32[]{:S(2)}, u32[]{:S(2)}) collective-permute-start(f32[32,1536]{1,0:T(8,128)S(1)} %copy-done.2), channel_id=1, source_target_pairs={{0,24},{1,25},{2,26},{3,27},{4,28},{5,29},{6,30},{7,31},{8,0},{9,1... | collective-permute-start | bytes 589832 | tf_op jit(solution)/shard_map/ppermute | solution.py:166
  35.3 16.5 %collective-permute-start.5 = (f32[512,256]{1,0:T(8,128)S(1)}, f32[512,256]{1,0:T(8,128)S(1)}, u32[]{:S(2)}, u32[]{:S(2)}) collective-permute-start(f32[512,256]{1,0:T(8,128)S(1)} %collective-permute-done.4.refs_1_), channel_id=1, source_target_pairs={{64,128},{128,64},{65,129},{129,65},{66,130},{130,66},{67,131},{13... | collective-permute-start | bytes 1572872 | tf_op jit(solution)/shard_map/ppermute | solution.py:170
  39.6 13.7 %collective-permute-start.13 = (f32[4,32,512]{2,1,0:T(8,128)S(1)}, f32[4,32,512]{2,1,0:T(8,128)S(1)}, u32[]{:S(2)}, u32[]{:S(2)}) collective-permute-start(f32[4,32,512]{2,1,0:T(8,128)S(1)} %get-tuple-element.31), channel_id=1, source_target_pairs={{0,2},{1,9},{2,4},{3,11},{4,6},{5,13},{6,0},{7,15},{8,10},{9,17},{... | collective-permute-start | bytes 786440 | tf_op jit(solution)/shard_map/ppermute | solution.py:166
  44.2 10.4 %collective-permute-start.14 = (f32[4,32,512]{2,1,0:T(8,128)S(1)}, f32[4,32,512]{2,1,0:T(8,128)S(1)}, u32[]{:S(2)}, u32[]{:S(2)}) collective-permute-start(f32[4,32,512]{2,1,0:T(8,128)S(1)} %get-tuple-element.29), channel_id=1, source_target_pairs={{0,4},{1,17},{2,6},{3,19},{4,0},{5,21},{6,2},{7,23},{8,12},{9,25},... | collective-permute-start | bytes 786440 | tf_op jit(solution)/shard_map/ppermute | solution.py:166
  45.7 8.9 %collective-permute-start.15 = (f32[4,32,512]{2,1,0:T(8,128)S(1)}, f32[4,32,512]{2,1,0:T(8,128)S(1)}, u32[]{:S(2)}, u32[]{:S(2)}) collective-permute-start(f32[4,32,512]{2,1,0:T(8,128)S(1)} %get-tuple-element.30), channel_id=1, source_target_pairs={{0,6},{1,25},{2,0},{3,27},{4,2},{5,29},{6,4},{7,31},{8,14},{9,1},{... | collective-permute-start | bytes 786440 | tf_op jit(solution)/shard_map/ppermute | solution.py:166
  51.8 43.9 %collective-permute-start.28 = (f32[4,4,32,512]{3,2,1,0:T(8,128)S(1)}, f32[4,4,32,512]{3,2,1,0:T(8,128)S(1)}, u32[]{:S(2)}, u32[]{:S(2)}) collective-permute-start(f32[4,4,32,512]{3,2,1,0:T(8,128)S(1)} %get-tuple-element.17), channel_id=1, source_target_pairs={{0,1},{1,0},{2,3},{3,2},{4,5},{5,4},{6,7},{7,6},{8,9},{9,8},{10,11... | collective-permute-start | bytes 3145736 | tf_op jit(solution)/shard_map/ppermute | solution.py:166
  53.3 15.4 %collective-permute-start.6 = (f32[512,256]{1,0:T(8,128)S(1)}, f32[512,256]{1,0:T(8,128)S(1)}, u32[]{:S(2)}, u32[]{:S(2)}) collective-permute-start(f32[512,256]{1,0:T(8,128)S(1)} %collective-permute-done.5.refs_1_), channel_id=1, source_target_pairs={{64,0},{128,192},{65,1},{129,193},{66,2},{130,194},{67,3},{131,195... | collective-permute-start | bytes 1572872 | tf_op jit(solution)/shard_map/ppermute | solution.py:172
  54.9 18.3 %collective-permute-start.20 = (f32[4,32,512]{2,1,0:T(8,128)S(1)}, f32[4,32,512]{2,1,0:T(8,128)S(1)}, u32[]{:S(2)}, u32[]{:S(2)}) collective-permute-start(f32[4,32,512]{2,1,0:T(8,128)S(1)} %get-tuple-element.28), channel_id=1, source_target_pairs={{0,2},{1,9},{2,4},{3,11},{4,6},{5,13},{6,0},{7,15},{8,10},{9,17},{... | collective-permute-start | bytes 786440 | tf_op jit(solution)/shard_map/ppermute | solution.py:166
  55.9 18.6 %collective-permute-start.21 = (f32[4,32,512]{2,1,0:T(8,128)S(1)}, f32[4,32,512]{2,1,0:T(8,128)S(1)}, u32[]{:S(2)}, u32[]{:S(2)}) collective-permute-start(f32[4,32,512]{2,1,0:T(8,128)S(1)} %get-tuple-element.26), channel_id=1, source_target_pairs={{0,4},{1,17},{2,6},{3,19},{4,0},{5,21},{6,2},{7,23},{8,12},{9,25},... | collective-permute-start | bytes 786440 | tf_op jit(solution)/shard_map/ppermute | solution.py:166
  58.5 17.2 %collective-permute-start.22 = (f32[4,32,512]{2,1,0:T(8,128)S(1)}, f32[4,32,512]{2,1,0:T(8,128)S(1)}, u32[]{:S(2)}, u32[]{:S(2)}) collective-permute-start(f32[4,32,512]{2,1,0:T(8,128)S(1)} %get-tuple-element.27), channel_id=1, source_target_pairs={{0,6},{1,25},{2,0},{3,27},{4,2},{5,29},{6,4},{7,31},{8,14},{9,1},{... | collective-permute-start | bytes 786440 | tf_op jit(solution)/shard_map/ppermute | solution.py:166
  68.7 9.4 %collective-permute-start.16 = (f32[32,512]{1,0:T(8,128)S(1)}, f32[32,512]{1,0:T(8,128)S(1)}, u32[]{:S(2)}, u32[]{:S(2)}) collective-permute-start(f32[32,512]{1,0:T(8,128)S(1)} %get-tuple-element.43), channel_id=1, source_target_pairs={{0,8},{1,3},{2,10},{3,5},{4,12},{5,7},{6,14},{7,1},{8,16},{9,11},{... | collective-permute-start | bytes 196616 | tf_op jit(solution)/shard_map/ppermute | solution.py:166
  73.2 10.1 %collective-permute-start.17 = (f32[32,512]{1,0:T(8,128)S(1)}, f32[32,512]{1,0:T(8,128)S(1)}, u32[]{:S(2)}, u32[]{:S(2)}) collective-permute-start(f32[32,512]{1,0:T(8,128)S(1)} %get-tuple-element.41), channel_id=1, source_target_pairs={{0,16},{1,5},{2,18},{3,7},{4,20},{5,1},{6,22},{7,3},{8,24},{9,13},... | collective-permute-start | bytes 196616 | tf_op jit(solution)/shard_map/ppermute | solution.py:166
  74.5 9.5 %collective-permute-start.18 = (f32[32,512]{1,0:T(8,128)S(1)}, f32[32,512]{1,0:T(8,128)S(1)}, u32[]{:S(2)}, u32[]{:S(2)}) collective-permute-start(f32[32,512]{1,0:T(8,128)S(1)} %get-tuple-element.42), channel_id=1, source_target_pairs={{0,24},{1,7},{2,26},{3,1},{4,28},{5,3},{6,30},{7,5},{8,0},{9,15},{... | collective-permute-start | bytes 196616 | tf_op jit(solution)/shard_map/ppermute | solution.py:166
  75.7 31.1 %collective-permute-start.35 = (f32[4,4,32,512]{3,2,1,0:T(8,128)S(1)}, f32[4,4,32,512]{3,2,1,0:T(8,128)S(1)}, u32[]{:S(2)}, u32[]{:S(2)}) collective-permute-start(f32[4,4,32,512]{3,2,1,0:T(8,128)S(1)} %get-tuple-element.19), channel_id=1, source_target_pairs={{0,1},{1,0},{2,3},{3,2},{4,5},{5,4},{6,7},{7,6},{8,9},{9,8},{10,11... | collective-permute-start | bytes 3145736 | tf_op jit(solution)/shard_map/ppermute | solution.py:166
  78.1 13.1 %collective-permute-start.7 = (f32[32,1536]{1,0:T(8,128)S(1)}, f32[32,1536]{1,0:T(8,128)S(1)}, u32[]{:S(2)}, u32[]{:S(2)}) collective-permute-start(f32[32,1536]{1,0:T(8,128)S(1)} %copy-done.2), channel_id=1, source_target_pairs={{0,32},{1,33},{2,34},{3,35},{4,36},{5,37},{6,38},{7,39},{8,40},{9,... | collective-permute-start | bytes 589832 | tf_op jit(solution)/shard_map/ppermute | solution.py:166
  83.4 8.9 %collective-permute-start.23 = (f32[32,512]{1,0:T(8,128)S(1)}, f32[32,512]{1,0:T(8,128)S(1)}, u32[]{:S(2)}, u32[]{:S(2)}) collective-permute-start(f32[32,512]{1,0:T(8,128)S(1)} %get-tuple-element.40), channel_id=1, source_target_pairs={{0,8},{1,3},{2,10},{3,5},{4,12},{5,7},{6,14},{7,1},{8,16},{9,11},{... | collective-permute-start | bytes 196616 | tf_op jit(solution)/shard_map/ppermute | solution.py:166
  84.0 8.9 %collective-permute-start.24 = (f32[32,512]{1,0:T(8,128)S(1)}, f32[32,512]{1,0:T(8,128)S(1)}, u32[]{:S(2)}, u32[]{:S(2)}) collective-permute-start(f32[32,512]{1,0:T(8,128)S(1)} %get-tuple-element.38), channel_id=1, source_target_pairs={{0,16},{1,5},{2,18},{3,7},{4,20},{5,1},{6,22},{7,3},{8,24},{9,13},... | collective-permute-start | bytes 196616 | tf_op jit(solution)/shard_map/ppermute | solution.py:166
  91.2 3.1 %collective-permute-start.25 = (f32[32,512]{1,0:T(8,128)S(1)}, f32[32,512]{1,0:T(8,128)S(1)}, u32[]{:S(2)}, u32[]{:S(2)}) collective-permute-start(f32[32,512]{1,0:T(8,128)S(1)} %get-tuple-element.39), channel_id=1, source_target_pairs={{0,24},{1,7},{2,26},{3,1},{4,28},{5,3},{6,30},{7,5},{8,0},{9,15},{... | collective-permute-start | bytes 196616 | tf_op jit(solution)/shard_map/ppermute | solution.py:166
  92.3 39.1 %collective-permute-start.3 = (f32[4,32,1536]{2,1,0:T(8,128)S(1)}, f32[4,32,1536]{2,1,0:T(8,128)S(1)}, u32[]{:S(2)}, u32[]{:S(2)}) collective-permute-start(f32[4,32,1536]{2,1,0:T(8,128)S(1)} %pad_maximum_fusion.refs_0_), channel_id=1, source_target_pairs={{0,1},{1,0},{2,3},{3,2},{4,5},{5,4},{6,7},{7,6},{8,9},{9,8},{10,11... | collective-permute-start | bytes 2359304 | tf_op jit(solution)/shard_map/ppermute | solution.py:166
  93.0 7.7 %collective-permute-start.8 = (f32[32,1536]{1,0:T(8,128)S(1)}, f32[32,1536]{1,0:T(8,128)S(1)}, u32[]{:S(2)}, u32[]{:S(2)}) collective-permute-start(f32[32,1536]{1,0:T(8,128)S(1)} %collective-permute-done.7), channel_id=1, source_target_pairs={{0,8},{1,9},{2,10},{3,11},{4,12},{5,13},{6,14},{7,15},{8,16},{9,17... | collective-permute-start | bytes 589832 | tf_op jit(solution)/shard_map/ppermute | solution.py:166
  94.3 10.7 %collective-permute-start.9 = (f32[32,1536]{1,0:T(8,128)S(1)}, f32[32,1536]{1,0:T(8,128)S(1)}, u32[]{:S(2)}, u32[]{:S(2)}) collective-permute-start(f32[32,1536]{1,0:T(8,128)S(1)} %collective-permute-done.7), channel_id=1, source_target_pairs={{0,16},{1,17},{2,18},{3,19},{4,20},{5,21},{6,22},{7,23},{8,24},{9,... | collective-permute-start | bytes 589832 | tf_op jit(solution)/shard_map/ppermute | solution.py:166
  95.8 10.4 %collective-permute-start.10 = (f32[32,1536]{1,0:T(8,128)S(1)}, f32[32,1536]{1,0:T(8,128)S(1)}, u32[]{:S(2)}, u32[]{:S(2)}) collective-permute-start(f32[32,1536]{1,0:T(8,128)S(1)} %collective-permute-done.7), channel_id=1, source_target_pairs={{0,24},{1,25},{2,26},{3,27},{4,28},{5,29},{6,30},{7,31},{8,0},{9,1... | collective-permute-start | bytes 589832 | tf_op jit(solution)/shard_map/ppermute | solution.py:166
  100.7 9.9 %collective-permute-start.29 = (f32[4,32,512]{2,1,0:T(8,128)S(1)}, f32[4,32,512]{2,1,0:T(8,128)S(1)}, u32[]{:S(2)}, u32[]{:S(2)}) collective-permute-start(f32[4,32,512]{2,1,0:T(8,128)S(1)} %get-tuple-element.25), channel_id=1, source_target_pairs={{0,2},{1,9},{2,4},{3,11},{4,6},{5,13},{6,0},{7,15},{8,10},{9,17},{... | collective-permute-start | bytes 786440 | tf_op jit(solution)/shard_map/ppermute | solution.py:166
  105.0 7.0 %collective-permute-start.30 = (f32[4,32,512]{2,1,0:T(8,128)S(1)}, f32[4,32,512]{2,1,0:T(8,128)S(1)}, u32[]{:S(2)}, u32[]{:S(2)}) collective-permute-start(f32[4,32,512]{2,1,0:T(8,128)S(1)} %get-tuple-element.23), channel_id=1, source_target_pairs={{0,4},{1,17},{2,6},{3,19},{4,0},{5,21},{6,2},{7,23},{8,12},{9,25},... | collective-permute-start | bytes 786440 | tf_op jit(solution)/shard_map/ppermute | solution.py:166
  106.1 7.1 %collective-permute-start.31 = (f32[4,32,512]{2,1,0:T(8,128)S(1)}, f32[4,32,512]{2,1,0:T(8,128)S(1)}, u32[]{:S(2)}, u32[]{:S(2)}) collective-permute-start(f32[4,32,512]{2,1,0:T(8,128)S(1)} %get-tuple-element.24), channel_id=1, source_target_pairs={{0,6},{1,25},{2,0},{3,27},{4,2},{5,29},{6,4},{7,31},{8,14},{9,1},{... | collective-permute-start | bytes 786440 | tf_op jit(solution)/shard_map/ppermute | solution.py:166
  106.8 24.6 %collective-permute-start.11 = (f32[4,32,1536]{2,1,0:T(8,128)S(1)}, f32[4,32,1536]{2,1,0:T(8,128)S(1)}, u32[]{:S(2)}, u32[]{:S(2)}) collective-permute-start(f32[4,32,1536]{2,1,0:T(8,128)S(1)} %pad_maximum_fusion.1.refs_2_), channel_id=1, source_target_pairs={{0,1},{1,0},{2,3},{3,2},{4,5},{5,4},{6,7},{7,6},{8,9},{9,8},{10,11... | collective-permute-start | bytes 2359304 | tf_op jit(solution)/shard_map/ppermute | solution.py:166
  110.6 9.3 %collective-permute-start.36 = (f32[4,32,512]{2,1,0:T(8,128)S(1)}, f32[4,32,512]{2,1,0:T(8,128)S(1)}, u32[]{:S(2)}, u32[]{:S(2)}) collective-permute-start(f32[4,32,512]{2,1,0:T(8,128)S(1)} %get-tuple-element.22), channel_id=1, source_target_pairs={{0,2},{1,9},{2,4},{3,11},{4,6},{5,13},{6,0},{7,15},{8,10},{9,17},{... | collective-permute-start | bytes 786440 | tf_op jit(solution)/shard_map/ppermute | solution.py:166
  112.0 7.9 %collective-permute-start.37 = (f32[4,32,512]{2,1,0:T(8,128)S(1)}, f32[4,32,512]{2,1,0:T(8,128)S(1)}, u32[]{:S(2)}, u32[]{:S(2)}) collective-permute-start(f32[4,32,512]{2,1,0:T(8,128)S(1)} %get-tuple-element.20), channel_id=1, source_target_pairs={{0,4},{1,17},{2,6},{3,19},{4,0},{5,21},{6,2},{7,23},{8,12},{9,25},... | collective-permute-start | bytes 786440 | tf_op jit(solution)/shard_map/ppermute | solution.py:166
  113.2 9.2 %collective-permute-start.38 = (f32[4,32,512]{2,1,0:T(8,128)S(1)}, f32[4,32,512]{2,1,0:T(8,128)S(1)}, u32[]{:S(2)}, u32[]{:S(2)}) collective-permute-start(f32[4,32,512]{2,1,0:T(8,128)S(1)} %get-tuple-element.21), channel_id=1, source_target_pairs={{0,6},{1,25},{2,0},{3,27},{4,2},{5,29},{6,4},{7,31},{8,14},{9,1},{... | collective-permute-start | bytes 786440 | tf_op jit(solution)/shard_map/ppermute | solution.py:166
  119.9 5.5 %collective-permute-start.32 = (f32[32,512]{1,0:T(8,128)S(1)}, f32[32,512]{1,0:T(8,128)S(1)}, u32[]{:S(2)}, u32[]{:S(2)}) collective-permute-start(f32[32,512]{1,0:T(8,128)S(1)} %get-tuple-element.37), channel_id=1, source_target_pairs={{0,8},{1,3},{2,10},{3,5},{4,12},{5,7},{6,14},{7,1},{8,16},{9,11},{... | collective-permute-start | bytes 196616 | tf_op jit(solution)/shard_map/ppermute | solution.py:166
  119.9 5.5 %collective-permute-start.33 = (f32[32,512]{1,0:T(8,128)S(1)}, f32[32,512]{1,0:T(8,128)S(1)}, u32[]{:S(2)}, u32[]{:S(2)}) collective-permute-start(f32[32,512]{1,0:T(8,128)S(1)} %get-tuple-element.35), channel_id=1, source_target_pairs={{0,16},{1,5},{2,18},{3,7},{4,20},{5,1},{6,22},{7,3},{8,24},{9,13},... | collective-permute-start | bytes 196616 | tf_op jit(solution)/shard_map/ppermute | solution.py:166
  122.5 4.6 %collective-permute-start.34 = (f32[32,512]{1,0:T(8,128)S(1)}, f32[32,512]{1,0:T(8,128)S(1)}, u32[]{:S(2)}, u32[]{:S(2)}) collective-permute-start(f32[32,512]{1,0:T(8,128)S(1)} %get-tuple-element.36), channel_id=1, source_target_pairs={{0,24},{1,7},{2,26},{3,1},{4,28},{5,3},{6,30},{7,5},{8,0},{9,15},{... | collective-permute-start | bytes 196616 | tf_op jit(solution)/shard_map/ppermute | solution.py:166
  125.4 5.0 %collective-permute-start.39 = (f32[32,512]{1,0:T(8,128)S(1)}, f32[32,512]{1,0:T(8,128)S(1)}, u32[]{:S(2)}, u32[]{:S(2)}) collective-permute-start(f32[32,512]{1,0:T(8,128)S(1)} %get-tuple-element.34), channel_id=1, source_target_pairs={{0,8},{1,3},{2,10},{3,5},{4,12},{5,7},{6,14},{7,1},{8,16},{9,11},{... | collective-permute-start | bytes 196616 | tf_op jit(solution)/shard_map/ppermute | solution.py:166
  125.4 5.0 %collective-permute-start.40 = (f32[32,512]{1,0:T(8,128)S(1)}, f32[32,512]{1,0:T(8,128)S(1)}, u32[]{:S(2)}, u32[]{:S(2)}) collective-permute-start(f32[32,512]{1,0:T(8,128)S(1)} %get-tuple-element.32), channel_id=1, source_target_pairs={{0,16},{1,5},{2,18},{3,7},{4,20},{5,1},{6,22},{7,3},{8,24},{9,13},... | collective-permute-start | bytes 196616 | tf_op jit(solution)/shard_map/ppermute | solution.py:166
  127.1 4.2 %collective-permute-start.41 = (f32[32,512]{1,0:T(8,128)S(1)}, f32[32,512]{1,0:T(8,128)S(1)}, u32[]{:S(2)}, u32[]{:S(2)}) collective-permute-start(f32[32,512]{1,0:T(8,128)S(1)} %get-tuple-element.33), channel_id=1, source_target_pairs={{0,24},{1,7},{2,26},{3,1},{4,28},{5,3},{6,30},{7,5},{8,0},{9,15},{... | collective-permute-start | bytes 196616 | tf_op jit(solution)/shard_map/ppermute | solution.py:166
  129.4 22.8 %copy-start.3 = (f32[1024]{0:T(1024)S(1)}, f32[1024]{0:T(1024)}, u32[]{:S(2)}) copy-start(f32[1024]{0:T(1024)} %param.8) | copy-start | bytes 12292
  134.2 50.4 %all-to-all-start = ((f32[256,6,128]{2,1,0:T(8,128)}), f32[256,6,128]{2,1,0:T(8,128)S(1)}, u32[]{:S(2)}, u32[]{:S(2)}) async-start(f32[256,6,128]{2,1,0:T(8,128)} %reshape.49), calls=%async_computation | async-start | bytes 2097152 | tf_op jit(solution)/shard_map/all_to_all | solution.py:195
  185.7 4.5 %copy-start.4 = (f32[6]{0:T(128)S(1)}, f32[6]{0:T(128)}, u32[]{:S(2)}) copy-start(f32[6]{0:T(128)} %param.9) | copy-start | bytes 76

commit v2 on v0

v2 whole, which is shorter than its diff:
```python
import math

import jax
import jax.numpy as jnp
from jax import lax
from jax.experimental import pallas as pl
from jax.experimental.pallas import tpu as pltpu
from jax.sharding import PartitionSpec as P

entropy = 2.0
NX = NY = 4
NC = 2
NH = 2
NG = 4
WIDE = NH * NY * NX * NC
MIB = 1024 * 1024
BIG = 10**11


def coords(w):
    return w // (NY * NX * NC), (w // (NX * NC)) % NY, (w // NC) % NX, w % NC


def wide_index(h, y, x, c):
    return ((h * NY + y % NY) * NX + x % NX) * NC + c


def wide_pairs(move):
    return [(w, wide_index(*move(*coords(w)))) for w in range(WIDE)]


def row_pairs(d):
    return wide_pairs(lambda h, y, x, c: (h, y, x + d, c) if c == 0 else (h, y + d, x, c))


def column_pairs(d):
    return wide_pairs(lambda h, y, x, c: (h, y + d, x, c) if c == 0 else (h, y, x + d, c))


CORE_SWAP = wide_pairs(lambda h, y, x, c: (h, y, x, 1 - c))
H_SWAP = wide_pairs(lambda h, y, x, c: (1 - h, y, x, c))
GATHER_GROUPS = [
    [
        g * WIDE + (wide_index(h, b, a, 0) if c == 0 else wide_index(h, a, b, 1))
        for g in range(NG)
        for h in range(NH)
        for b in range(4)
    ]
    for c in range(NC)
    for a in range(4)
]


def halves(v):
    hi = v.astype(jnp.bfloat16)
    return hi, (v - hi.astype(jnp.float32)).astype(jnp.bfloat16)


def dot3(a, b):
    def dot(u, v):
        return jnp.dot(u, v, preferred_element_type=jnp.float32)

    return dot(a[0], b[0]) + (dot(a[0], b[1]) + dot(a[1], b[0]))


def params():
    return pltpu.CompilerParams(vmem_limit_bytes=40 * MIB)


COST = pl.CostEstimate(flops=1000, bytes_accessed=1000, transcendentals=0)
VMEM = pl.BlockSpec(memory_space=pltpu.VMEM)
SMEM = pl.BlockSpec(memory_space=pltpu.SMEM)


def split_kernel(place, plan_ref, hi_ref, lo_ref):
    h = place[3]
    groups, nx, run, depth = plan_ref.shape
    per = groups // NH
    for xx in range(nx):
        for dh in range(NH):
            for i in range(per):
                hi, lo = halves(plan_ref[lax.rem(h + dh, NH) * per + i, xx])
                at = (dh * per + i) * run
                hi_ref[xx, at : at + run, :] = hi
                lo_ref[xx, at : at + run, :] = lo


def split(place, plan5):
    groups, nx, run, depth = plan5.shape
    out = jax.ShapeDtypeStruct((nx, groups * run, depth), jnp.bfloat16)
    return pl.pallas_call(
        split_kernel,
        in_specs=[SMEM, VMEM],
        out_specs=[VMEM, VMEM],
        out_shape=[out, out],
        compiler_params=params(),
        cost_estimate=COST,
        name="split",
    )(place, plan5)


def carry_kernel(place, hi_ref, lo_ref, *refs):
    blocks, (own_ref, send_ref, held) = refs[:-3], refs[-3:]
    c, x, y = place[0], place[1], place[2]
    nx, rows, _ = hi_ref.shape
    per = rows // (NH * NY)

    def put(cc, d1, d2, n, chunk):
        @pl.when(c == cc)
        def _():
            own_ref[d1, d2, n] = chunk

        @pl.when(c != cc)
        def _():
            send_ref[d1, d2, n] = chunk

    for n, block in enumerate(blocks):
        right = halves(block[...])
        half = block.shape[1] // NC
        part = half // 4

        def step(xx, carried):
            out = dot3((hi_ref[xx], lo_ref[xx]), right)
            low = out[:, :half].T
            for yy in range(NY):
                put(0, lax.rem(xx - x + NX, NX), lax.rem(yy - y + NY, NY), n, low[yy * part : (yy + 1) * part])
            for i in range(NH * NY):
                held[i, xx] = out[i * per : (i + 1) * per, half:]
            return carried

        lax.fori_loop(0, nx, step, 0)
        for yy in range(NY):
            piece = [held[dh * NY + yy].reshape(nx * per, half) for dh in range(NH)]
            high = jnp.concatenate(piece, axis=0).T
            for xo in range(NX):
                put(1, lax.rem(yy - y + NY, NY), lax.rem(xo - x + NX, NX), n, high[xo * part : (xo + 1) * part])


def carry(place, plan, blocks, flops):
    nx, rows, _ = plan[0].shape
    cols = blocks[0].shape[1]
    out = jax.ShapeDtypeStruct((4, 4, len(blocks), cols // (NC * 4), rows), jnp.float32)
    return pl.pallas_call(
        carry_kernel,
        in_specs=[SMEM, VMEM, VMEM] + [VMEM] * len(blocks),
        out_specs=[VMEM, VMEM],
        out_shape=[out, out],
        scratch_shapes=[pltpu.VMEM((NH * NY, nx, rows // (NH * NY), cols // NC), jnp.float32)],
        compiler_params=params(),
        cost_estimate=pl.CostEstimate(flops=flops, bytes_accessed=1000, transcendentals=0),
        name="carry",
    )(place, *plan, *blocks)


def grad_kernel(place, *refs, factor):
    pieces, (blocks, out_ref, cost, held, full) = refs[:4], refs[4:]
    c, x, y, g = place[0], place[1], place[2], place[4]
    a, b = jnp.where(c == 0, x, y), jnp.where(c == 0, y, x)
    run = pieces[0].shape[1]
    for d in range(4):
        bb = lax.rem(b - d + 4, 4)
        for dc in range(NC):
            at = (bb * NC + lax.rem(c + dc, NC)) * run
            cost[pl.ds(pl.multiple_of(at, run), run), :] = pieces[d][dc]
    part = blocks.shape[1]
    low, even = g < 2, lax.rem(g, 2) == 0
    near = jnp.where(even, g + 1, g - 1)
    order = [g, near, jnp.where(low, g + 2, g - 2), jnp.where(low, near + 2, near - 2)]
    for k, j in enumerate(order):
        held[pl.ds(pl.multiple_of(j * part, part), part), :] = blocks[k]
    left = halves(held[...])
    step = 512
    width = cost.shape[1]
    for at in range(0, width, step):
        full[at : at + step, :] = factor * dot3(left, halves(cost[:, at : at + step])).T
    full[width:, :] = jnp.zeros((full.shape[0] - width, full.shape[1]), jnp.float32)
    chips = NG * NH * NY * NX
    rows = width // chips
    pad = out_ref.shape[2]
    for cc in range(NC):

        @pl.when(c == cc)
        def _(cc=cc):
            for o in range(chips):
                gh, yy, xx = o // (NY * NX), (o // NX) % NY, o % NX
                aa, bb = (xx, yy) if cc == 0 else (yy, xx)
                out_ref[lax.rem(aa - a + 4, 4), gh * 4 + bb] = full[o * rows : o * rows + pad, :]


def grad(place, pieces, blocks, factor):
    _, run, width = pieces[0].shape
    rows = NC * 4 * run
    cols = blocks.shape[0] * blocks.shape[1]
    pad = -(-width // (NG * NH * NY * NX) // 8) * 8
    return pl.pallas_call(
        lambda place, *refs: grad_kernel(place, *refs, factor=factor),
        in_specs=[SMEM] + [VMEM] * 5,
        out_specs=VMEM,
        out_shape=jax.ShapeDtypeStruct((4, NG * NH * 4, pad, cols), jnp.float32),
        scratch_shapes=[
            pltpu.VMEM((rows, width), jnp.float32),
            pltpu.VMEM((cols, rows), jnp.float32),
            pltpu.VMEM((width + 8, cols), jnp.float32),
        ],
        compiler_params=params(),
        cost_estimate=COST,
        name="grad",
    )(place, *pieces, blocks)


def arrange_kernel(place, own, got, potential, out_ref, log_ref):
    c = place[0]
    rows = out_ref.shape[0]

    def mine(v):
        return jnp.where(c == 0, v[:, :rows, :], v[:, rows : 2 * rows, :])

    mine_own, mine_got = mine(own), mine(got)
    low = jnp.where(c == 0, mine_own, mine_got)
    high = jnp.where(c == 0, mine_got, mine_own)
    part = own.shape[2] // 4
    pieces = [v[b, :, j * part : (j + 1) * part] for j in range(4) for v in (low, high) for b in range(4)]
    gradient = jnp.concatenate(pieces, axis=1)
    out_ref[...] = gradient
    scores = (potential[...] - gradient) / entropy
    peak = jnp.max(scores, axis=1, keepdims=True)
    total = jnp.sum(jnp.exp(scores - peak), axis=1, keepdims=True)
    log_ref[...] = peak + jnp.log(total)


def arrange(place, own, got, potential, rows):
    return pl.pallas_call(
        arrange_kernel,
        in_specs=[SMEM, VMEM, VMEM, VMEM],
        out_specs=[VMEM, VMEM],
        out_shape=[
            jax.ShapeDtypeStruct((rows, potential.shape[1]), jnp.float32),
            jax.ShapeDtypeStruct((rows, 1), jnp.float32),
        ],
        compiler_params=params(),
        cost_estimate=COST,
        name="arrange",
    )(place, own, got, potential)


def meet_kernel(*refs):
    refs[-1][...] = jnp.zeros_like(refs[-1])


def meet(flops, width, *arrays):
    return pl.pallas_call(
        meet_kernel,
        in_specs=[pl.BlockSpec(memory_space=pl.ANY)] * len(arrays),
        out_specs=VMEM,
        out_shape=jax.ShapeDtypeStruct((1, width), jnp.float32),
        compiler_params=params(),
        cost_estimate=pl.CostEstimate(flops=flops, bytes_accessed=1000, transcendentals=0),
        name="meet",
    )(*arrays)


def after(value, *others):
    return lax.optimization_barrier((value, *others))[0]


def body(plan, cost_source, cost_target, potential_col, row_mass):
    num_source = plan.shape[0] * NG
    num_target = plan.shape[1] * WIDE
    factor = -2.0 / math.sqrt(num_source * num_target)
    g = lax.axis_index("grp")
    w = lax.axis_index("wide")
    h, y, x, c = coords(w)
    place = jnp.stack([c, x, y, h, g]).astype(jnp.int32)
    plan5 = plan.reshape(NH * NY, NX, NC * cost_source.shape[0], plan.shape[1])

    def wide(v, pairs):
        return lax.ppermute(v, "wide", pairs)

    both = jnp.stack([cost_source, wide(cost_source, CORE_SWAP)])
    costs = [wide(both, column_pairs(d)) for d in (1, 2, 3)]
    halved = split(place, plan5)

    def along_rows(own, got):
        parts = [own[d] + got[d] for d in range(4)]
        return parts[0] + sum(wide(parts[d], row_pairs(d)) for d in (1, 2, 3))

    def finish(total):
        total = total[0] + sum(wide(total[d], column_pairs(d)) for d in (1, 2, 3))
        rows = total.shape[-1] // NH
        return total[..., :rows] + wide(total[..., rows:], H_SWAP)

    near = lax.ppermute(cost_target, "grp", [(i, i ^ 1) for i in range(NG)])
    far = lax.ppermute(cost_target, "grp", [(i, i ^ 2) for i in range(NG)])
    own0, send0 = carry(place, halved, (cost_target,), 1000)
    got0 = wide(send0, CORE_SWAP) + meet(BIG, own0.shape[-1], own0, far, *costs)
    last = lax.ppermute(far, "grp", [(i, i ^ 1) for i in range(NG)])
    total0 = along_rows(own0, got0)
    own1, send1 = carry(place, halved, (near, far), BIG)
    total1 = along_rows(own1, wide(send1, CORE_SWAP))
    own2, send2 = carry(place, halved, (after(last, total0),), BIG)
    total2 = along_rows(own2, wide(send2, CORE_SWAP)) + meet(1000, own0.shape[-1], total1)
    blocks = finish(jnp.concatenate([total0, total1, total2], axis=1))

    partial = grad(place, [both] + costs, blocks, factor)
    partial = partial[0] + sum(wide(partial[d], row_pairs(d)) for d in (1, 2, 3))
    parts = lax.all_to_all(partial, ("grp", "wide"), 0, 0, axis_index_groups=GATHER_GROUPS, tiled=True)
    summed = parts.reshape((NG * NH, 4) + parts.shape[1:]).sum(axis=0)
    gradient, log_total = arrange(place, summed, wide(summed, CORE_SWAP), potential_col[None, :], row_mass.shape[0])
    potential_row = entropy * jnp.log(row_mass) - entropy * log_total[:, 0]
    return (gradient, potential_row)


def solution(mesh):
    placed = (P("grp", "wide"), P(("grp", "wide"), None), P("wide", "grp"), P(), P(("grp", "wide")))
    return jax.shard_map(
        body,
        mesh=mesh,
        in_specs=placed,
        out_specs=(P(("grp", "wide"), None), P(("grp", "wide"))),
        check_vma=False,
    )
```

time: 792 us -> 134 us (0.17)
  waiting for transfers between devices: 748 us -> 43.4 us
  starting transfers between devices: 0.12 us -> 42.8 us
  matrix products: 26 us -> 0 us
  blocking collectives: 0 us -> 21.1 us
  Pallas kernels: 0 us -> 20.3 us
  between operations: 13.8 us -> 0.84 us
    reduce_scatter x1 -> x0, waiting for transfers between devices: 418 us -> none  [body(): lax.psum_scatter(jnp.dot(plan, gathered, precision=highest), 'wide', scat...]
    unnamed x4 -> x0, waiting for transfers between devices: 275 us -> none
    all_gather x1 -> x0, waiting for transfers between devices: 55.7 us -> none  [body(): gathered = lax.all_gather(cost_target, 'grp', axis=1, tiled=True)]
    ppermute x0 -> x27, waiting for transfers between devices: none -> 43.4 us  [the longest x24 33.4 us: wide(): return lax.ppermute(v, 'wide', pairs)]
    ppermute x0 -> x27, starting transfers between devices: none -> 42.8 us  [the longest x24 39.9 us: wide(): return lax.ppermute(v, 'wide', pairs)]
    dot_general x2 -> x0, matrix products: 26 us -> none  [the longest x1 17.9 us: body(): jnp.dot(plan, gathered, precision=highest)]
    all_to_all x0 -> x1, blocking collectives: none -> 21.1 us  [body(): lax.all_to_all(partial, ('grp', 'wide'), 0, 0, axis_index_groups=GATHER_G...]
    pallas_call x0 -> x8, Pallas kernels: none -> 20.3 us  [the longest x3 16.6 us: carry(): pl.pallas_call(carry_kernel, in_specs=[SMEM, VMEM, VMEM] + [VMEM] * len(b...]
  transfers between devices with their start and end apart: 3 -> 27, of which waited for: 3 -> 15; matrix products, arithmetic and copies ran while one was open for 0% -> 2% of each run, Pallas kernels for 0% -> 13%
where the time goes in v2:
time: 134 us
  waiting for transfers between devices  43.4 us (32%)
  starting transfers between devices  42.8 us (32%)
  blocking collectives  21.1 us (16%)
  Pallas kernels  20.3 us (15%)
  other arithmetic  3.19 us (2%)
  local copies, waits for them, and re-layouts  2.41 us (2%)
    ppermute x24, starting transfers between devices, wide(): return lax.ppermute(v, 'wide', pairs)  39.9 us
    ppermute x24, waiting for transfers between devices, wide(): return lax.ppermute(v, 'wide', pairs)  33.4 us
    all_to_all x1, blocking collectives, body(): lax.all_to_all(partial, ('grp', 'wide'), 0, 0, axis_index_groups=GATHER_G...  21.1 us
    pallas_call x3, Pallas kernels, carry(): pl.pallas_call(carry_kernel, in_specs=[SMEM, VMEM, VMEM] + [VMEM] * len(b...  16.6 us
    ppermute x1, waiting for transfers between devices, body(): far = lax.ppermute(cost_target, 'grp', [(i, i ^ 2) for i in range(NG)])  9.99 us
  transfers between devices with their start and end apart: 27, of which 15 were waited for; matrix products, arithmetic and copies ran while one was open for 2% of the time, Pallas kernels for 13%

profile of v2, /device:TPU:1, one launch (start us, length us, event | category | flops | bytes accessed | tf_op | source)
XLA Modules:
  0.0 134.0 jit_solution(13661844117263512227)
XLA Ops:
  0.6 3.3 %collective-permute-start = (f32[32,1536]{1,0:T(8,128)}, f32[32,1536]{1,0:T(8,128)S(1)}, u32[]{:S(2)}, u32[]{:S(2)}) collective-permute-start(f32[32,1536]{1,0:T(8,128)} %param.6), channel_id=1, source_target_pairs={{0,1},{1,0},{2,3},{3,2},{4,5},{5,4},{6,7},{7,6},{8,9},{9,8},{10,11... | collective-permute-start | bytes 589832 | tf_op jit(solution)/shard_map/ppermute | solution.py:277
  4.0 1.3 collective-permute-start.5
  5.2 1.0 pad_maximum_fusion.1.refs_0_
  6.2 1.3 collective-permute-start.1
  7.5 2.5 %collective-permute-start.2 = (f32[2,32,1536]{2,1,0:T(8,128)S(1)}, f32[2,32,1536]{2,1,0:T(8,128)S(1)}, u32[]{:S(2)}, u32[]{:S(2)}) collective-permute-start(f32[2,32,1536]{2,1,0:T(8,128)S(1)} %pad_maximum_fusion.1.refs_0_), channel_id=1, source_target_pairs={{0,16},{1,5},{2,18},{3,7},{4,20},{5,1},{6,22},{7,3},{8,24},{9,13},... | collective-permute-start | bytes 1179656 | tf_op jit(solution)/shard_map/ppermute | solution.py:277
  9.9 1.2 collective-permute-start.3
  11.1 1.6 %collective-permute-start.9 = (f32[512,256]{1,0:T(8,128)}, f32[512,256]{1,0:T(8,128)S(1)}, u32[]{:S(2)}, u32[]{:S(2)}) collective-permute-start(f32[512,256]{1,0:T(8,128)} %refs_0_.1), channel_id=1, source_target_pairs={{0,64},{64,0},{128,192},{192,128},{1,65},{65,1},{129,193},{193,129... | collective-permute-start | bytes 1572872 | tf_op jit(solution)/shard_map/ppermute | solution.py:292
  12.7 0.1 stack.32.place
  12.8 2.2 %copy-done = f32[2048,512]{1,0:T(8,128)S(1)} copy-done((f32[2048,512]{1,0:T(8,128)S(1)}, f32[2048,512]{1,0:T(8,128)}, u32[]{:S(2)}) %copy-start) | copy-done | bytes 4194328
  15.0 1.0 split.1
  16.0 4.0 %carry.3 = (f32[4,4,1,32,512]{4,3,2,1,0:T(8,128)S(1)}, f32[4,4,1,32,512]{4,3,2,1,0:T(8,128)S(1)}) custom-call(s32[5]{0:T(128)S(1)} %stack.32.place, bf16[4,512,512]{2,1,0:T(8,128)(2,1)S(1)} %get-tuple-element.13.hi_ref, bf16[4,512,512]{2,1,0:T(8,128)(2,1)S(1)} %get-tuple-element.14.lo_ref, f32[512,256]{1,0:T(8,128)S(1)} %copy-done.1), custom_call_target="tpu_custom_call" | custom-call | flops 1000 | bytes 1000 | tf_op jit(solution)/shard_map/carry/pallas_call | solution.py:143
  20.1 10.0 %collective-permute-done.5.refs_1_ = f32[512,256]{1,0:T(8,128)} collective-permute-done((f32[512,256]{1,0:T(8,128)}, f32[512,256]{1,0:T(8,128)}, u32[]{:S(2)}, u32[]{:S(2)}) %collective-permute-start.5) | collective-permute-done | bytes 524320 | tf_op jit(solution)/shard_map/ppermute | solution.py:293
  30.1 0.8 collective-permute-start.4
  30.9 2.3 %collective-permute-done.4 = f32[4,4,1,32,512]{4,3,1,2,0:T(8,128)S(1)} collective-permute-done((f32[4,4,1,32,512]{4,3,1,2,0:T(8,128)S(1)}, f32[4,4,1,32,512]{4,3,1,2,0:T(8,128)S(1)}, u32[]{:S(2)}, u32[]{:S(2)}) %collective-permute-start.4) | collective-permute-done | bytes 1048608 | tf_op jit(solution)/shard_map/ppermute | solution.py:277
  33.2 0.1 broadcast_add_fusion
  33.3 0.1 fusion.14
  33.5 0.2 collective-permute-start.6
  33.7 2.6 %collective-permute-start.7 = (f32[4,1,32,512]{3,2,0,1:T(8,128)S(1)}, f32[4,1,32,512]{3,2,0,1:T(8,128)S(1)}, u32[]{:S(2)}, u32[]{:S(2)}) collective-permute-start(f32[4,1,32,512]{3,2,0,1:T(8,128)S(1)} %get-tuple-element.30), channel_id=1, source_target_pairs={{0,4},{1,17},{2,6},{3,19},{4,0},{5,21},{6,2},{7,23},{8,12},{9,25},... | collective-permute-start | bytes 786440 | tf_op jit(solution)/shard_map/ppermute | solution.py:277
  36.3 1.1 collective-permute-start.8
  37.4 8.0 %carry.4 = (f32[4,4,2,32,512]{4,3,2,1,0:T(8,128)S(1)}, f32[4,4,2,32,512]{4,3,2,1,0:T(8,128)S(1)}) custom-call(s32[5]{0:T(128)S(1)} %stack.32.place, bf16[4,512,512]{2,1,0:T(8,128)(2,1)S(1)} %get-tuple-element.13.hi_ref, bf16[4,512,512]{2,1,0:T(8,128)(2,1)S(1)} %get-tuple-element.14.lo_ref, f32[512,256]{1,0:T(8,128)S(1)} %collective-permute-done.9.refs_0_, ...), custom_call_target="tpu_custom_call" | custom-call | flops 99999997952 | bytes 1000 | tf_op jit(solution)/shard_map/carry/pallas_call | solution.py:143
  45.4 1.3 collective-permute-start.10
  46.8 0.1 fusion.17
  46.9 4.6 %carry.5 = (f32[4,4,1,32,512]{4,3,2,1,0:T(8,128)S(1)}, f32[4,4,1,32,512]{4,3,2,1,0:T(8,128)S(1)}) custom-call(s32[5]{0:T(128)S(1)} %stack.32.place, bf16[4,512,512]{2,1,0:T(8,128)(2,1)S(1)} %get-tuple-element.13.hi_ref, bf16[4,512,512]{2,1,0:T(8,128)(2,1)S(1)} %get-tuple-element.14.lo_ref, f32[512,256]{1,0:T(8,128)} %collective-permute-done.14.refs_0_), custom_call_target="tpu_custom_call" | custom-call | flops 99999997952 | bytes 1000 | tf_op jit(solution)/shard_map/carry/pallas_call | solution.py:143
  51.5 1.3 collective-permute-start.15
  52.7 0.3 fusion.1
  53.1 0.2 collective-permute-start.11
  53.3 2.6 %collective-permute-start.12 = (f32[4,2,32,512]{3,2,1,0:T(8,128)S(1)}, f32[4,2,32,512]{3,2,1,0:T(8,128)S(1)}, u32[]{:S(2)}, u32[]{:S(2)}) collective-permute-start(f32[4,2,32,512]{3,2,1,0:T(8,128)S(1)} %get-tuple-element.24), channel_id=1, source_target_pairs={{0,4},{1,17},{2,6},{3,19},{4,0},{5,21},{6,2},{7,23},{8,12},{9,25},... | collective-permute-start | bytes 1572872 | tf_op jit(solution)/shard_map/ppermute | solution.py:277
  55.9 1.1 collective-permute-start.13
  57.0 0.1 fusion.8
  57.1 0.5 collective-permute-start.16
  57.6 0.9 collective-permute-start.17
  58.5 4.2 %collective-permute-done.11 = f32[4,2,32,512]{3,2,1,0:T(8,128)S(1)} collective-permute-done((f32[4,2,32,512]{3,2,1,0:T(8,128)S(1)}, f32[4,2,32,512]{3,2,1,0:T(8,128)S(1)}, u32[]{:S(2)}, u32[]{:S(2)}) %collective-permute-start.11) | collective-permute-done | bytes 524320 | tf_op jit(solution)/shard_map/ppermute | solution.py:277
  62.7 0.4 collective-permute-start.18
  63.1 5.1 %collective-permute-done.12 = f32[4,2,32,512]{3,2,1,0:T(8,128)S(1)} collective-permute-done((f32[4,2,32,512]{3,2,1,0:T(8,128)S(1)}, f32[4,2,32,512]{3,2,1,0:T(8,128)S(1)}, u32[]{:S(2)}, u32[]{:S(2)}) %collective-permute-start.12) | collective-permute-done | bytes 524320 | tf_op jit(solution)/shard_map/ppermute | solution.py:277
  68.2 0.7 collective-permute-done.13
  68.9 0.3 fusion.4.refs_0_
  69.2 1.9 %collective-permute-done.16 = f32[4,1,32,512]{3,2,0,1:T(8,128)S(1)} collective-permute-done((f32[4,1,32,512]{3,2,0,1:T(8,128)S(1)}, f32[4,1,32,512]{3,2,0,1:T(8,128)S(1)}, u32[]{:S(2)}, u32[]{:S(2)}) %collective-permute-start.16) | collective-permute-done | bytes 262176 | tf_op jit(solution)/shard_map/ppermute | solution.py:277
  71.1 2.7 %collective-permute-done.17 = f32[4,1,32,512]{3,2,0,1:T(8,128)S(1)} collective-permute-done((f32[4,1,32,512]{3,2,0,1:T(8,128)S(1)}, f32[4,1,32,512]{3,2,0,1:T(8,128)S(1)}, u32[]{:S(2)}, u32[]{:S(2)}) %collective-permute-start.17) | collective-permute-done | bytes 262176 | tf_op jit(solution)/shard_map/ppermute | solution.py:277
  73.8 0.8 collective-permute-done.18
  74.6 0.1 fusion.12
  74.7 0.1 pad_maximum_fusion
  74.9 0.1 collective-permute-start.19
  75.0 1.9 %collective-permute-start.20 = (f32[4,32,512]{2,1,0:T(8,128)S(1)}, f32[4,32,512]{2,1,0:T(8,128)S(1)}, u32[]{:S(2)}, u32[]{:S(2)}) collective-permute-start(f32[4,32,512]{2,1,0:T(8,128)S(1)} %get-tuple-element.36), channel_id=1, source_target_pairs={{0,16},{1,5},{2,18},{3,7},{4,20},{5,1},{6,22},{7,3},{8,24},{9,13},... | collective-permute-start | bytes 786440 | tf_op jit(solution)/shard_map/ppermute | solution.py:277
  76.9 1.2 collective-permute-start.21
  78.1 6.4 %collective-permute-done.19 = f32[4,32,512]{2,1,0:T(8,128)S(1)} collective-permute-done((f32[4,32,512]{2,1,0:T(8,128)S(1)}, f32[4,32,512]{2,1,0:T(8,128)S(1)}, u32[]{:S(2)}, u32[]{:S(2)}) %collective-permute-start.19) | collective-permute-done | bytes 262176 | tf_op jit(solution)/shard_map/ppermute | solution.py:277
  84.5 0.6 collective-permute-done.21
  85.1 0.1 fusion.6
  85.2 5.6 %collective-permute-start.22 = (f32[4,32,256]{2,1,0:T(8,128)S(1)}, f32[4,32,256]{2,1,0:T(8,128)S(1)}, u32[]{:S(2)}, u32[]{:S(2)}) collective-permute-start(f32[4,32,256]{2,1,0:T(8,128)S(1)} %slice.161), channel_id=1, source_target_pairs={{0,32},{1,33},{2,34},{3,35},{4,36},{5,37},{6,38},{7,39},{8,40},{9,... | collective-permute-start | bytes 393224 | tf_op jit(solution)/shard_map/ppermute | solution.py:277
  90.8 2.4 %collective-permute-done.22 = f32[4,32,256]{2,1,0:T(8,128)S(1)} collective-permute-done((f32[4,32,256]{2,1,0:T(8,128)S(1)}, f32[4,32,256]{2,1,0:T(8,128)S(1)}, u32[]{:S(2)}, u32[]{:S(2)}) %collective-permute-start.22) | collective-permute-done | bytes 131104 | tf_op jit(solution)/shard_map/ppermute | solution.py:277
  93.2 1.3 grad.1
  94.5 0.1 slice_bitcast_fusion.1
  94.6 1.7 %collective-permute-start.23 = (f32[32,16,128]{2,1,0:T(8,128)S(1)}, f32[32,16,128]{2,1,0:T(8,128)S(1)}, u32[]{:S(2)}, u32[]{:S(2)}) collective-permute-start(f32[32,16,128]{2,1,0:T(8,128)S(1)} %get-tuple-element.35), channel_id=1, source_target_pairs={{0,2},{1,9},{2,4},{3,11},{4,6},{5,13},{6,0},{7,15},{8,10},{9,17},{... | collective-permute-start | bytes 786440 | tf_op jit(solution)/shard_map/ppermute | solution.py:277
  96.3 1.8 %collective-permute-start.24 = (f32[32,16,128]{2,1,0:T(8,128)S(1)}, f32[32,16,128]{2,1,0:T(8,128)S(1)}, u32[]{:S(2)}, u32[]{:S(2)}) collective-permute-start(f32[32,16,128]{2,1,0:T(8,128)S(1)} %get-tuple-element.33), channel_id=1, source_target_pairs={{0,4},{1,17},{2,6},{3,19},{4,0},{5,21},{6,2},{7,23},{8,12},{9,25},... | collective-permute-start | bytes 786440 | tf_op jit(solution)/shard_map/ppermute | solution.py:277
  98.1 1.2 collective-permute-start.25
  99.4 1.8 %collective-permute-done.23 = f32[32,16,128]{2,1,0:T(8,128)S(1)} collective-permute-done((f32[32,16,128]{2,1,0:T(8,128)S(1)}, f32[32,16,128]{2,1,0:T(8,128)S(1)}, u32[]{:S(2)}, u32[]{:S(2)}) %collective-permute-start.23) | collective-permute-done | bytes 262176 | tf_op jit(solution)/shard_map/ppermute | solution.py:277
  101.1 3.6 %collective-permute-done.24 = f32[32,16,128]{2,1,0:T(8,128)S(1)} collective-permute-done((f32[32,16,128]{2,1,0:T(8,128)S(1)}, f32[32,16,128]{2,1,0:T(8,128)S(1)}, u32[]{:S(2)}, u32[]{:S(2)}) %collective-permute-start.24) | collective-permute-done | bytes 262176 | tf_op jit(solution)/shard_map/ppermute | solution.py:277
  104.7 0.1 collective-permute-done.25
  104.8 0.1 fusion.5
  104.9 21.1 %all_to_all.5 = f32[32,16,128]{2,1,0:T(8,128)S(1)} all-to-all(f32[32,16,128]{2,1,0:T(8,128)S(1)} %fusion.5), channel_id=1, replica_groups={{0,8,16,24,32,40,48,56,64,72,80,88,96,104,112,120,128,136,144,152,160,1..., dimensions={0} | all-to-all | bytes 524288 | tf_op jit(solution)/shard_map/all_to_all | solution.py:306
  126.0 5.2 %collective-permute-start.26 = (f32[4,16,128]{2,1,0:T(8,128)S(1)}, f32[4,16,128]{2,1,0:T(8,128)S(1)}, u32[]{:S(2)}, u32[]{:S(2)}) collective-permute-start(f32[4,16,128]{2,1,0:T(8,128)S(1)} %reduce_sum.9.own), channel_id=1, source_target_pairs={{0,1},{1,0},{2,3},{3,2},{4,5},{5,4},{6,7},{7,6},{8,9},{9,8},{10,11... | collective-permute-start | bytes 98312 | tf_op jit(solution)/shard_map/ppermute | solution.py:277
  131.2 0.9 collective-permute-done.26.got
  132.1 1.3 arrange.1
  133.3 0.1 multiply_reduce_fusion
  133.4 0.5 multiply_subtract_fusion
  (26 shorter events, 0.2 us)
Async XLA Ops:
  0.6 4.6 %collective-permute-start = (f32[32,1536]{1,0:T(8,128)}, f32[32,1536]{1,0:T(8,128)S(1)}, u32[]{:S(2)}, u32[]{:S(2)}) collective-permute-start(f32[32,1536]{1,0:T(8,128)} %param.6), channel_id=1, source_target_pairs={{0,1},{1,0},{2,3},{3,2},{4,5},{5,4},{6,7},{7,6},{8,9},{9,8},{10,11... | collective-permute-start | bytes 589832 | tf_op jit(solution)/shard_map/ppermute | solution.py:277
  4.0 26.1 %collective-permute-start.5 = (f32[512,256]{1,0:T(8,128)}, f32[512,256]{1,0:T(8,128)}, u32[]{:S(2)}, u32[]{:S(2)}) collective-permute-start(f32[512,256]{1,0:T(8,128)} %refs_0_.1), channel_id=1, source_target_pairs={{0,128},{64,192},{128,0},{192,64},{1,129},{65,193},{129,1},{193,65... | collective-permute-start | bytes 1572872 | tf_op jit(solution)/shard_map/ppermute | solution.py:293
  6.2 24.7 %collective-permute-start.1 = (f32[2,32,1536]{2,1,0:T(8,128)S(1)}, f32[2,32,1536]{2,1,0:T(8,128)S(1)}, u32[]{:S(2)}, u32[]{:S(2)}) collective-permute-start(f32[2,32,1536]{2,1,0:T(8,128)S(1)} %pad_maximum_fusion.1.refs_0_), channel_id=1, source_target_pairs={{0,8},{1,3},{2,10},{3,5},{4,12},{5,7},{6,14},{7,1},{8,16},{9,11},{... | collective-permute-start | bytes 1179656 | tf_op jit(solution)/shard_map/ppermute | solution.py:277
  7.5 23.4 %collective-permute-start.2 = (f32[2,32,1536]{2,1,0:T(8,128)S(1)}, f32[2,32,1536]{2,1,0:T(8,128)S(1)}, u32[]{:S(2)}, u32[]{:S(2)}) collective-permute-start(f32[2,32,1536]{2,1,0:T(8,128)S(1)} %pad_maximum_fusion.1.refs_0_), channel_id=1, source_target_pairs={{0,16},{1,5},{2,18},{3,7},{4,20},{5,1},{6,22},{7,3},{8,24},{9,13},... | collective-permute-start | bytes 1179656 | tf_op jit(solution)/shard_map/ppermute | solution.py:277
  9.9 21.0 %collective-permute-start.3 = (f32[2,32,1536]{2,1,0:T(8,128)S(1)}, f32[2,32,1536]{2,1,0:T(8,128)S(1)}, u32[]{:S(2)}, u32[]{:S(2)}) collective-permute-start(f32[2,32,1536]{2,1,0:T(8,128)S(1)} %pad_maximum_fusion.1.refs_0_), channel_id=1, source_target_pairs={{0,24},{1,7},{2,26},{3,1},{4,28},{5,3},{6,30},{7,5},{8,0},{9,15},{... | collective-permute-start | bytes 1179656 | tf_op jit(solution)/shard_map/ppermute | solution.py:277
  11.1 26.3 %collective-permute-start.9 = (f32[512,256]{1,0:T(8,128)}, f32[512,256]{1,0:T(8,128)S(1)}, u32[]{:S(2)}, u32[]{:S(2)}) collective-permute-start(f32[512,256]{1,0:T(8,128)} %refs_0_.1), channel_id=1, source_target_pairs={{0,64},{64,0},{128,192},{192,128},{1,65},{65,1},{129,193},{193,129... | collective-permute-start | bytes 1572872 | tf_op jit(solution)/shard_map/ppermute | solution.py:292
  12.8 2.2 %copy-start = (f32[2048,512]{1,0:T(8,128)S(1)}, f32[2048,512]{1,0:T(8,128)}, u32[]{:S(2)}) copy-start(f32[2048,512]{1,0:T(8,128)} %param.5) | copy-start | bytes 12582916
  15.0 1.0 copy-start.1
  30.1 3.1 %collective-permute-start.4 = (f32[4,4,1,32,512]{4,3,1,2,0:T(8,128)S(1)}, f32[4,4,1,32,512]{4,3,1,2,0:T(8,128)S(1)}, u32[]{:S(2)}, u32[]{:S(2)}) collective-permute-start(f32[4,4,1,32,512]{4,3,1,2,0:T(8,128)S(1)} %bitcast.89), channel_id=1, source_target_pairs={{0,1},{1,0},{2,3},{3,2},{4,5},{5,4},{6,7},{7,6},{8,9},{9,8},{10,11... | collective-permute-start | bytes 3145736 | tf_op jit(solution)/shard_map/ppermute | solution.py:277
  30.9 16.0 %collective-permute-start.14 = (f32[512,256]{1,0:T(8,128)}, f32[512,256]{1,0:T(8,128)}, u32[]{:S(2)}, u32[]{:S(2)}) collective-permute-start(f32[512,256]{1,0:T(8,128)} %collective-permute-done.5.refs_1_), channel_id=1, source_target_pairs={{0,64},{64,0},{128,192},{192,128},{1,65},{65,1},{129,193},{193,129... | collective-permute-start | bytes 1572872 | tf_op jit(solution)/shard_map/ppermute | solution.py:296
  33.5 13.3 %collective-permute-start.6 = (f32[4,1,32,512]{3,2,0,1:T(8,128)S(1)}, f32[4,1,32,512]{3,2,0,1:T(8,128)S(1)}, u32[]{:S(2)}, u32[]{:S(2)}) collective-permute-start(f32[4,1,32,512]{3,2,0,1:T(8,128)S(1)} %get-tuple-element.32), channel_id=1, source_target_pairs={{0,2},{1,9},{2,4},{3,11},{4,6},{5,13},{6,0},{7,15},{8,10},{9,17},{... | collective-permute-start | bytes 786440 | tf_op jit(solution)/shard_map/ppermute | solution.py:277
  33.7 13.0 %collective-permute-start.7 = (f32[4,1,32,512]{3,2,0,1:T(8,128)S(1)}, f32[4,1,32,512]{3,2,0,1:T(8,128)S(1)}, u32[]{:S(2)}, u32[]{:S(2)}) collective-permute-start(f32[4,1,32,512]{3,2,0,1:T(8,128)S(1)} %get-tuple-element.30), channel_id=1, source_target_pairs={{0,4},{1,17},{2,6},{3,19},{4,0},{5,21},{6,2},{7,23},{8,12},{9,25},... | collective-permute-start | bytes 786440 | tf_op jit(solution)/shard_map/ppermute | solution.py:277
  36.3 10.4 %collective-permute-start.8 = (f32[4,1,32,512]{3,2,1,0:T(8,128)S(1)}, f32[4,1,32,512]{3,2,1,0:T(8,128)S(1)}, u32[]{:S(2)}, u32[]{:S(2)}) collective-permute-start(f32[4,1,32,512]{3,2,1,0:T(8,128)S(1)} %get-tuple-element.31), channel_id=1, source_target_pairs={{0,6},{1,25},{2,0},{3,27},{4,2},{5,29},{6,4},{7,31},{8,14},{9,1},{... | collective-permute-start | bytes 786440 | tf_op jit(solution)/shard_map/ppermute | solution.py:277
  45.4 7.3 %collective-permute-start.10 = (f32[4,4,2,32,512]{4,3,2,1,0:T(8,128)S(1)}, f32[4,4,2,32,512]{4,3,2,1,0:T(8,128)S(1)}, u32[]{:S(2)}, u32[]{:S(2)}) collective-permute-start(f32[4,4,2,32,512]{4,3,2,1,0:T(8,128)S(1)} %get-tuple-element.18), channel_id=1, source_target_pairs={{0,1},{1,0},{2,3},{3,2},{4,5},{5,4},{6,7},{7,6},{8,9},{9,8},{10,11... | collective-permute-start | bytes 6291464 | tf_op jit(solution)/shard_map/ppermute | solution.py:277
  51.5 5.5 %collective-permute-start.15 = (f32[4,4,1,32,512]{4,3,1,2,0:T(8,128)S(1)}, f32[4,4,1,32,512]{4,3,1,2,0:T(8,128)S(1)}, u32[]{:S(2)}, u32[]{:S(2)}) collective-permute-start(f32[4,4,1,32,512]{4,3,1,2,0:T(8,128)S(1)} %bitcast.88), channel_id=1, source_target_pairs={{0,1},{1,0},{2,3},{3,2},{4,5},{5,4},{6,7},{7,6},{8,9},{9,8},{10,11... | collective-permute-start | bytes 3145736 | tf_op jit(solution)/shard_map/ppermute | solution.py:277
  53.1 9.6 %collective-permute-start.11 = (f32[4,2,32,512]{3,2,1,0:T(8,128)S(1)}, f32[4,2,32,512]{3,2,1,0:T(8,128)S(1)}, u32[]{:S(2)}, u32[]{:S(2)}) collective-permute-start(f32[4,2,32,512]{3,2,1,0:T(8,128)S(1)} %get-tuple-element.26), channel_id=1, source_target_pairs={{0,2},{1,9},{2,4},{3,11},{4,6},{5,13},{6,0},{7,15},{8,10},{9,17},{... | collective-permute-start | bytes 1572872 | tf_op jit(solution)/shard_map/ppermute | solution.py:277
  53.3 14.9 %collective-permute-start.12 = (f32[4,2,32,512]{3,2,1,0:T(8,128)S(1)}, f32[4,2,32,512]{3,2,1,0:T(8,128)S(1)}, u32[]{:S(2)}, u32[]{:S(2)}) collective-permute-start(f32[4,2,32,512]{3,2,1,0:T(8,128)S(1)} %get-tuple-element.24), channel_id=1, source_target_pairs={{0,4},{1,17},{2,6},{3,19},{4,0},{5,21},{6,2},{7,23},{8,12},{9,25},... | collective-permute-start | bytes 1572872 | tf_op jit(solution)/shard_map/ppermute | solution.py:277
  55.9 13.0 %collective-permute-start.13 = (f32[4,2,32,512]{3,2,1,0:T(8,128)S(1)}, f32[4,2,32,512]{3,2,1,0:T(8,128)S(1)}, u32[]{:S(2)}, u32[]{:S(2)}) collective-permute-start(f32[4,2,32,512]{3,2,1,0:T(8,128)S(1)} %get-tuple-element.25), channel_id=1, source_target_pairs={{0,6},{1,25},{2,0},{3,27},{4,2},{5,29},{6,4},{7,31},{8,14},{9,1},{... | collective-permute-start | bytes 1572872 | tf_op jit(solution)/shard_map/ppermute | solution.py:277
  57.1 14.0 %collective-permute-start.16 = (f32[4,1,32,512]{3,2,0,1:T(8,128)S(1)}, f32[4,1,32,512]{3,2,0,1:T(8,128)S(1)}, u32[]{:S(2)}, u32[]{:S(2)}) collective-permute-start(f32[4,1,32,512]{3,2,0,1:T(8,128)S(1)} %get-tuple-element.29), channel_id=1, source_target_pairs={{0,2},{1,9},{2,4},{3,11},{4,6},{5,13},{6,0},{7,15},{8,10},{9,17},{... | collective-permute-start | bytes 786440 | tf_op jit(solution)/shard_map/ppermute | solution.py:277
  57.6 16.2 %collective-permute-start.17 = (f32[4,1,32,512]{3,2,0,1:T(8,128)S(1)}, f32[4,1,32,512]{3,2,0,1:T(8,128)S(1)}, u32[]{:S(2)}, u32[]{:S(2)}) collective-permute-start(f32[4,1,32,512]{3,2,0,1:T(8,128)S(1)} %get-tuple-element.27), channel_id=1, source_target_pairs={{0,4},{1,17},{2,6},{3,19},{4,0},{5,21},{6,2},{7,23},{8,12},{9,25},... | collective-permute-start | bytes 786440 | tf_op jit(solution)/shard_map/ppermute | solution.py:277
  62.7 11.9 %collective-permute-start.18 = (f32[4,1,32,512]{3,2,1,0:T(8,128)S(1)}, f32[4,1,32,512]{3,2,1,0:T(8,128)S(1)}, u32[]{:S(2)}, u32[]{:S(2)}) collective-permute-start(f32[4,1,32,512]{3,2,1,0:T(8,128)S(1)} %get-tuple-element.28), channel_id=1, source_target_pairs={{0,6},{1,25},{2,0},{3,27},{4,2},{5,29},{6,4},{7,31},{8,14},{9,1},{... | collective-permute-start | bytes 786440 | tf_op jit(solution)/shard_map/ppermute | solution.py:277
  74.9 9.6 %collective-permute-start.19 = (f32[4,32,512]{2,1,0:T(8,128)S(1)}, f32[4,32,512]{2,1,0:T(8,128)S(1)}, u32[]{:S(2)}, u32[]{:S(2)}) collective-permute-start(f32[4,32,512]{2,1,0:T(8,128)S(1)} %get-tuple-element.38), channel_id=1, source_target_pairs={{0,8},{1,3},{2,10},{3,5},{4,12},{5,7},{6,14},{7,1},{8,16},{9,11},{... | collective-permute-start | bytes 786440 | tf_op jit(solution)/shard_map/ppermute | solution.py:277
  75.0 9.5 %collective-permute-start.20 = (f32[4,32,512]{2,1,0:T(8,128)S(1)}, f32[4,32,512]{2,1,0:T(8,128)S(1)}, u32[]{:S(2)}, u32[]{:S(2)}) collective-permute-start(f32[4,32,512]{2,1,0:T(8,128)S(1)} %get-tuple-element.36), channel_id=1, source_target_pairs={{0,16},{1,5},{2,18},{3,7},{4,20},{5,1},{6,22},{7,3},{8,24},{9,13},... | collective-permute-start | bytes 786440 | tf_op jit(solution)/shard_map/ppermute | solution.py:277
  76.9 8.2 %collective-permute-start.21 = (f32[4,32,512]{2,1,0:T(8,128)S(1)}, f32[4,32,512]{2,1,0:T(8,128)S(1)}, u32[]{:S(2)}, u32[]{:S(2)}) collective-permute-start(f32[4,32,512]{2,1,0:T(8,128)S(1)} %get-tuple-element.37), channel_id=1, source_target_pairs={{0,24},{1,7},{2,26},{3,1},{4,28},{5,3},{6,30},{7,5},{8,0},{9,15},{... | collective-permute-start | bytes 786440 | tf_op jit(solution)/shard_map/ppermute | solution.py:277
  85.2 7.9 %collective-permute-start.22 = (f32[4,32,256]{2,1,0:T(8,128)S(1)}, f32[4,32,256]{2,1,0:T(8,128)S(1)}, u32[]{:S(2)}, u32[]{:S(2)}) collective-permute-start(f32[4,32,256]{2,1,0:T(8,128)S(1)} %slice.161), channel_id=1, source_target_pairs={{0,32},{1,33},{2,34},{3,35},{4,36},{5,37},{6,38},{7,39},{8,40},{9,... | collective-permute-start | bytes 393224 | tf_op jit(solution)/shard_map/ppermute | solution.py:277
  94.5 37.5 %copy-start.2 = (f32[1024]{0:T(1024)S(1)}, f32[1024]{0:T(1024)}, u32[]{:S(2)}) copy-start(f32[1024]{0:T(1024)} %param.8) | copy-start | bytes 12292
  94.5 38.9 %copy-start.3 = (f32[6]{0:T(128)S(1)}, f32[6]{0:T(128)}, u32[]{:S(2)}) copy-start(f32[6]{0:T(128)} %param.9) | copy-start | bytes 76
  94.6 6.5 %collective-permute-start.23 = (f32[32,16,128]{2,1,0:T(8,128)S(1)}, f32[32,16,128]{2,1,0:T(8,128)S(1)}, u32[]{:S(2)}, u32[]{:S(2)}) collective-permute-start(f32[32,16,128]{2,1,0:T(8,128)S(1)} %get-tuple-element.35), channel_id=1, source_target_pairs={{0,2},{1,9},{2,4},{3,11},{4,6},{5,13},{6,0},{7,15},{8,10},{9,17},{... | collective-permute-start | bytes 786440 | tf_op jit(solution)/shard_map/ppermute | solution.py:277
  96.3 8.3 %collective-permute-start.24 = (f32[32,16,128]{2,1,0:T(8,128)S(1)}, f32[32,16,128]{2,1,0:T(8,128)S(1)}, u32[]{:S(2)}, u32[]{:S(2)}) collective-permute-start(f32[32,16,128]{2,1,0:T(8,128)S(1)} %get-tuple-element.33), channel_id=1, source_target_pairs={{0,4},{1,17},{2,6},{3,19},{4,0},{5,21},{6,2},{7,23},{8,12},{9,25},... | collective-permute-start | bytes 786440 | tf_op jit(solution)/shard_map/ppermute | solution.py:277
  98.1 6.7 %collective-permute-start.25 = (f32[32,16,128]{2,1,0:T(8,128)S(1)}, f32[32,16,128]{2,1,0:T(8,128)S(1)}, u32[]{:S(2)}, u32[]{:S(2)}) collective-permute-start(f32[32,16,128]{2,1,0:T(8,128)S(1)} %get-tuple-element.34), channel_id=1, source_target_pairs={{0,6},{1,25},{2,0},{3,27},{4,2},{5,29},{6,4},{7,31},{8,14},{9,1},{... | collective-permute-start | bytes 786440 | tf_op jit(solution)/shard_map/ppermute | solution.py:277
  126.0 6.1 %collective-permute-start.26 = (f32[4,16,128]{2,1,0:T(8,128)S(1)}, f32[4,16,128]{2,1,0:T(8,128)S(1)}, u32[]{:S(2)}, u32[]{:S(2)}) collective-permute-start(f32[4,16,128]{2,1,0:T(8,128)S(1)} %reduce_sum.9.own), channel_id=1, source_target_pairs={{0,1},{1,0},{2,3},{3,2},{4,5},{5,4},{6,7},{7,6},{8,9},{9,8},{10,11... | collective-permute-start | bytes 98312 | tf_op jit(solution)/shard_map/ppermute | solution.py:277

commit v3 on v2

--- a/solution.py
+++ b/solution.py
@@ -104,38 +104,26 @@
     c, x, y = place[0], place[1], place[2]
     nx, rows, _ = hi_ref.shape
     per = rows // (NH * NY)
-
-    def put(cc, d1, d2, n, chunk):
-        @pl.when(c == cc)
-        def _():
-            own_ref[d1, d2, n] = chunk
-
-        @pl.when(c != cc)
-        def _():
-            send_ref[d1, d2, n] = chunk
-
     for n, block in enumerate(blocks):
         right = halves(block[...])
         half = block.shape[1] // NC
         part = half // 4
-
-        def step(xx, carried):
+        for xx in range(nx):
             out = dot3((hi_ref[xx], lo_ref[xx]), right)
-            low = out[:, :half].T
-            for yy in range(NY):
-                put(0, lax.rem(xx - x + NX, NX), lax.rem(yy - y + NY, NY), n, low[yy * part : (yy + 1) * part])
             for i in range(NH * NY):
-                held[i, xx] = out[i * per : (i + 1) * per, half:]
-            return carried
-
-        lax.fori_loop(0, nx, step, 0)
-        for yy in range(NY):
-            piece = [held[dh * NY + yy].reshape(nx * per, half) for dh in range(NH)]
-            high = jnp.concatenate(piece, axis=0).T
-            for xo in range(NX):
-                put(1, lax.rem(yy - y + NY, NY), lax.rem(xo - x + NX, NX), n, high[xo * part : (xo + 1) * part])
-
-
+                held[n, i, xx] = out[i * per : (i + 1) * per]
+        for ref, core in ((own_ref, c), (send_ref, 1 - c)):
+            a, b = jnp.where(core == 0, x, y), jnp.where(core == 0, y, x)
+            lanes = pl.ds(pl.multiple_of(core * half, half), half)
+            for i in range(4):
+                tiles = []
+                for dh in range(NH):
+                    for j in range(4):
+                        yy, xx = jnp.where(core == 0, j, i), jnp.where(core == 0, i, j)
+                        tiles.append(held[n, dh * NY + yy, xx, :, lanes])
+                turned = jnp.concatenate(tiles, axis=0).T
+                for j in range(4):
+                    ref[lax.rem(i - a + 4, 4), lax.rem(j - b + 4, 4), n] = turned[j * part : (j + 1) * part]
 def carry(place, plan, blocks, flops):
     nx, rows, _ = plan[0].shape
     cols = blocks[0].shape[1]
@@ -145,7 +133,7 @@
         in_specs=[SMEM, VMEM, VMEM] + [VMEM] * len(blocks),
         out_specs=[VMEM, VMEM],
         out_shape=[out, out],
-        scratch_shapes=[pltpu.VMEM((NH * NY, nx, rows // (NH * NY), cols // NC), jnp.float32)],
+        scratch_shapes=[pltpu.VMEM((len(blocks), NH * NY, nx, rows // (NH * NY), cols), jnp.float32)],
         compiler_params=params(),
         cost_estimate=pl.CostEstimate(flops=flops, bytes_accessed=1000, transcendentals=0),
         name="carry",

time: 134 us -> 132 us (0.985)
  waiting for transfers between devices: 43.4 us -> 49.4 us
  Pallas kernels: 20.3 us -> 15.2 us
  blocking collectives: 21.1 us -> 19 us
    pallas_call x3, Pallas kernels: 16.6 us -> 11.5 us  [carry(): pl.pallas_call(carry_kernel, in_specs=[SMEM, VMEM, VMEM] + [VMEM] * len(b...]
    ppermute x24, waiting for transfers between devices: 33.4 us -> 36.3 us  [wide(): return lax.ppermute(v, 'wide', pairs)]
    all_to_all x1, blocking collectives: 21.1 us -> 19 us  [body(): lax.all_to_all(partial, ('grp', 'wide'), 0, 0, axis_index_groups=GATHER_G...]
    ppermute x1, waiting for transfers between devices: 0.01 us -> 1.95 us  [body(): last = lax.ppermute(far, 'grp', [(i, i ^ 1) for i in range(NG)])]
  transfers between devices with their start and end apart: 27 -> 27, of which waited for: 15 -> 14; matrix products, arithmetic and copies ran while one was open for 2% -> 2% of each run, Pallas kernels for 13% -> 10%
where the time goes in v3:
time: 132 us
  waiting for transfers between devices  49.4 us (37%)
  starting transfers between devices  41.8 us (32%)
  blocking collectives  19 us (14%)
  Pallas kernels  15.2 us (12%)
  other arithmetic  3.19 us (2%)
  local copies, waits for them, and re-layouts  2.41 us (2%)
    ppermute x24, starting transfers between devices, wide(): return lax.ppermute(v, 'wide', pairs)  38.9 us
    ppermute x24, waiting for transfers between devices, wide(): return lax.ppermute(v, 'wide', pairs)  36.3 us
    all_to_all x1, blocking collectives, body(): lax.all_to_all(partial, ('grp', 'wide'), 0, 0, axis_index_groups=GATHER_G...  19 us
    pallas_call x3, Pallas kernels, carry(): pl.pallas_call(carry_kernel, in_specs=[SMEM, VMEM, VMEM] + [VMEM] * len(b...  11.5 us
    ppermute x1, waiting for transfers between devices, body(): far = lax.ppermute(cost_target, 'grp', [(i, i ^ 2) for i in range(NG)])  11.1 us
  transfers between devices with their start and end apart: 27, of which 14 were waited for; matrix products, arithmetic and copies ran while one was open for 2% of the time, Pallas kernels for 10%

profile of v3, /device:TPU:1, one launch (start us, length us, event | category | flops | bytes accessed | tf_op | source)
XLA Modules:
  0.0 131.8 jit_solution(8737780778430773987)
XLA Ops:
  0.6 3.3 %collective-permute-start = (f32[32,1536]{1,0:T(8,128)}, f32[32,1536]{1,0:T(8,128)S(1)}, u32[]{:S(2)}, u32[]{:S(2)}) collective-permute-start(f32[32,1536]{1,0:T(8,128)} %param.6), channel_id=1, source_target_pairs={{0,1},{1,0},{2,3},{3,2},{4,5},{5,4},{6,7},{7,6},{8,9},{9,8},{10,11... | collective-permute-start | bytes 589832 | tf_op jit(solution)/shard_map/ppermute | solution.py:265
  4.0 1.3 collective-permute-start.5
  5.2 0.0 collective-permute-done
  5.2 1.0 pad_maximum_fusion.1.refs_0_
  6.2 1.3 collective-permute-start.1
  7.5 2.5 %collective-permute-start.2 = (f32[2,32,1536]{2,1,0:T(8,128)S(1)}, f32[2,32,1536]{2,1,0:T(8,128)S(1)}, u32[]{:S(2)}, u32[]{:S(2)}) collective-permute-start(f32[2,32,1536]{2,1,0:T(8,128)S(1)} %pad_maximum_fusion.1.refs_0_), channel_id=1, source_target_pairs={{0,16},{1,5},{2,18},{3,7},{4,20},{5,1},{6,22},{7,3},{8,24},{9,13},... | collective-permute-start | bytes 1179656 | tf_op jit(solution)/shard_map/ppermute | solution.py:265
  9.9 1.2 collective-permute-start.3
  11.1 1.6 %collective-permute-start.9 = (f32[512,256]{1,0:T(8,128)}, f32[512,256]{1,0:T(8,128)S(1)}, u32[]{:S(2)}, u32[]{:S(2)}) collective-permute-start(f32[512,256]{1,0:T(8,128)} %refs_0_.1), channel_id=1, source_target_pairs={{0,64},{64,0},{128,192},{192,128},{1,65},{65,1},{129,193},{193,129... | collective-permute-start | bytes 1572872 | tf_op jit(solution)/shard_map/ppermute | solution.py:280
  12.7 0.1 stack.32.place
  12.8 2.2 %copy-done = f32[2048,512]{1,0:T(8,128)S(1)} copy-done((f32[2048,512]{1,0:T(8,128)S(1)}, f32[2048,512]{1,0:T(8,128)}, u32[]{:S(2)}) %copy-start) | copy-done | bytes 4194328
  15.0 1.0 split.1
  16.0 0.0 copy-done.1
  16.0 2.9 %carry.3 = (f32[4,4,1,32,512]{4,3,2,1,0:T(8,128)S(1)}, f32[4,4,1,32,512]{4,3,2,1,0:T(8,128)S(1)}) custom-call(s32[5]{0:T(128)S(1)} %stack.32.place, bf16[4,512,512]{2,1,0:T(8,128)(2,1)S(1)} %get-tuple-element.13.hi_ref, bf16[4,512,512]{2,1,0:T(8,128)(2,1)S(1)} %get-tuple-element.14.lo_ref, f32[512,256]{1,0:T(8,128)S(1)} %copy-done.1), custom_call_target="tpu_custom_call" | custom-call | flops 1000 | bytes 1000 | tf_op jit(solution)/shard_map/carry/pallas_call | solution.py:131
  19.0 11.1 %collective-permute-done.5.refs_1_ = f32[512,256]{1,0:T(8,128)} collective-permute-done((f32[512,256]{1,0:T(8,128)}, f32[512,256]{1,0:T(8,128)}, u32[]{:S(2)}, u32[]{:S(2)}) %collective-permute-start.5) | collective-permute-done | bytes 524320 | tf_op jit(solution)/shard_map/ppermute | solution.py:281
  30.1 0.8 collective-permute-start.4
  30.9 2.3 %collective-permute-done.4 = f32[4,4,1,32,512]{4,3,1,2,0:T(8,128)S(1)} collective-permute-done((f32[4,4,1,32,512]{4,3,1,2,0:T(8,128)S(1)}, f32[4,4,1,32,512]{4,3,1,2,0:T(8,128)S(1)}, u32[]{:S(2)}, u32[]{:S(2)}) %collective-permute-start.4) | collective-permute-done | bytes 1048608 | tf_op jit(solution)/shard_map/ppermute | solution.py:265
  33.2 0.1 broadcast_add_fusion
  33.3 0.1 fusion.14
  33.5 0.2 collective-permute-start.6
  33.7 2.6 %collective-permute-start.7 = (f32[4,1,32,512]{3,2,0,1:T(8,128)S(1)}, f32[4,1,32,512]{3,2,0,1:T(8,128)S(1)}, u32[]{:S(2)}, u32[]{:S(2)}) collective-permute-start(f32[4,1,32,512]{3,2,0,1:T(8,128)S(1)} %get-tuple-element.30), channel_id=1, source_target_pairs={{0,4},{1,17},{2,6},{3,19},{4,0},{5,21},{6,2},{7,23},{8,12},{9,25},... | collective-permute-start | bytes 786440 | tf_op jit(solution)/shard_map/ppermute | solution.py:265
  36.3 1.1 collective-permute-start.8
  37.4 5.1 %carry.4 = (f32[4,4,2,32,512]{4,3,2,1,0:T(8,128)S(1)}, f32[4,4,2,32,512]{4,3,2,1,0:T(8,128)S(1)}) custom-call(s32[5]{0:T(128)S(1)} %stack.32.place, bf16[4,512,512]{2,1,0:T(8,128)(2,1)S(1)} %get-tuple-element.13.hi_ref, bf16[4,512,512]{2,1,0:T(8,128)(2,1)S(1)} %get-tuple-element.14.lo_ref, f32[512,256]{1,0:T(8,128)S(1)} %collective-permute-done.9.refs_0_, ...), custom_call_target="tpu_custom_call" | custom-call | flops 99999997952 | bytes 1000 | tf_op jit(solution)/shard_map/carry/pallas_call | solution.py:131
  42.5 1.3 collective-permute-start.10
  43.9 0.1 fusion.17
  44.0 2.0 %collective-permute-done.14.refs_0_ = f32[512,256]{1,0:T(8,128)} collective-permute-done((f32[512,256]{1,0:T(8,128)}, f32[512,256]{1,0:T(8,128)}, u32[]{:S(2)}, u32[]{:S(2)}) %collective-permute-start.14) | collective-permute-done | bytes 524320 | tf_op jit(solution)/shard_map/ppermute | solution.py:284
  45.9 3.5 %carry.5 = (f32[4,4,1,32,512]{4,3,2,1,0:T(8,128)S(1)}, f32[4,4,1,32,512]{4,3,2,1,0:T(8,128)S(1)}) custom-call(s32[5]{0:T(128)S(1)} %stack.32.place, bf16[4,512,512]{2,1,0:T(8,128)(2,1)S(1)} %get-tuple-element.13.hi_ref, bf16[4,512,512]{2,1,0:T(8,128)(2,1)S(1)} %get-tuple-element.14.lo_ref, f32[512,256]{1,0:T(8,128)} %collective-permute-done.14.refs_0_), custom_call_target="tpu_custom_call" | custom-call | flops 99999997952 | bytes 1000 | tf_op jit(solution)/shard_map/carry/pallas_call | solution.py:131
  49.4 2.2 %collective-permute-start.15 = (f32[4,4,1,32,512]{4,3,1,2,0:T(8,128)S(1)}, f32[4,4,1,32,512]{4,3,1,2,0:T(8,128)S(1)}, u32[]{:S(2)}, u32[]{:S(2)}) collective-permute-start(f32[4,4,1,32,512]{4,3,1,2,0:T(8,128)S(1)} %bitcast.88), channel_id=1, source_target_pairs={{0,1},{1,0},{2,3},{3,2},{4,5},{5,4},{6,7},{7,6},{8,9},{9,8},{10,11... | collective-permute-start | bytes 3145736 | tf_op jit(solution)/shard_map/ppermute | solution.py:265
  51.6 0.3 fusion.1
  52.0 0.2 collective-permute-start.11
  52.2 0.6 collective-permute-start.12
  52.8 1.9 %collective-permute-start.13 = (f32[4,2,32,512]{3,2,1,0:T(8,128)S(1)}, f32[4,2,32,512]{3,2,1,0:T(8,128)S(1)}, u32[]{:S(2)}, u32[]{:S(2)}) collective-permute-start(f32[4,2,32,512]{3,2,1,0:T(8,128)S(1)} %get-tuple-element.25), channel_id=1, source_target_pairs={{0,6},{1,25},{2,0},{3,27},{4,2},{5,29},{6,4},{7,31},{8,14},{9,1},{... | collective-permute-start | bytes 1572872 | tf_op jit(solution)/shard_map/ppermute | solution.py:265
  54.7 0.1 fusion.8
  54.9 0.7 collective-permute-start.16
  55.5 1.9 %collective-permute-start.17 = (f32[4,1,32,512]{3,2,0,1:T(8,128)S(1)}, f32[4,1,32,512]{3,2,0,1:T(8,128)S(1)}, u32[]{:S(2)}, u32[]{:S(2)}) collective-permute-start(f32[4,1,32,512]{3,2,0,1:T(8,128)S(1)} %get-tuple-element.27), channel_id=1, source_target_pairs={{0,4},{1,17},{2,6},{3,19},{4,0},{5,21},{6,2},{7,23},{8,12},{9,25},... | collective-permute-start | bytes 786440 | tf_op jit(solution)/shard_map/ppermute | solution.py:265
  57.4 9.8 %collective-permute-done.11 = f32[4,2,32,512]{3,2,1,0:T(8,128)S(1)} collective-permute-done((f32[4,2,32,512]{3,2,1,0:T(8,128)S(1)}, f32[4,2,32,512]{3,2,1,0:T(8,128)S(1)}, u32[]{:S(2)}, u32[]{:S(2)}) %collective-permute-start.11) | collective-permute-done | bytes 524320 | tf_op jit(solution)/shard_map/ppermute | solution.py:265
  67.2 0.6 collective-permute-done.13
  67.8 0.3 fusion.4.refs_0_
  68.1 4.7 %collective-permute-done.16 = f32[4,1,32,512]{3,2,0,1:T(8,128)S(1)} collective-permute-done((f32[4,1,32,512]{3,2,0,1:T(8,128)S(1)}, f32[4,1,32,512]{3,2,0,1:T(8,128)S(1)}, u32[]{:S(2)}, u32[]{:S(2)}) %collective-permute-start.16) | collective-permute-done | bytes 262176 | tf_op jit(solution)/shard_map/ppermute | solution.py:265
  72.8 0.7 collective-permute-done.18
  73.5 0.1 fusion.12
  73.6 0.1 pad_maximum_fusion
  73.7 0.1 slice_bitcast_fusion.5
  73.8 0.1 collective-permute-start.19
  73.9 0.8 collective-permute-start.20
  74.7 1.9 %collective-permute-start.21 = (f32[4,32,512]{2,1,0:T(8,128)S(1)}, f32[4,32,512]{2,1,0:T(8,128)S(1)}, u32[]{:S(2)}, u32[]{:S(2)}) collective-permute-start(f32[4,32,512]{2,1,0:T(8,128)S(1)} %get-tuple-element.37), channel_id=1, source_target_pairs={{0,24},{1,7},{2,26},{3,1},{4,28},{5,3},{6,30},{7,5},{8,0},{9,15},{... | collective-permute-start | bytes 786440 | tf_op jit(solution)/shard_map/ppermute | solution.py:265
  76.5 6.9 %collective-permute-done.19 = f32[4,32,512]{2,1,0:T(8,128)S(1)} collective-permute-done((f32[4,32,512]{2,1,0:T(8,128)S(1)}, f32[4,32,512]{2,1,0:T(8,128)S(1)}, u32[]{:S(2)}, u32[]{:S(2)}) %collective-permute-start.19) | collective-permute-done | bytes 262176 | tf_op jit(solution)/shard_map/ppermute | solution.py:265
  83.4 0.6 collective-permute-done.21
  84.0 0.1 fusion.6
  84.1 4.9 %collective-permute-start.22 = (f32[4,32,256]{2,1,0:T(8,128)S(1)}, f32[4,32,256]{2,1,0:T(8,128)S(1)}, u32[]{:S(2)}, u32[]{:S(2)}) collective-permute-start(f32[4,32,256]{2,1,0:T(8,128)S(1)} %slice.161), channel_id=1, source_target_pairs={{0,32},{1,33},{2,34},{3,35},{4,36},{5,37},{6,38},{7,39},{8,40},{9,... | collective-permute-start | bytes 393224 | tf_op jit(solution)/shard_map/ppermute | solution.py:265
  89.0 3.0 %collective-permute-done.22 = f32[4,32,256]{2,1,0:T(8,128)S(1)} collective-permute-done((f32[4,32,256]{2,1,0:T(8,128)S(1)}, f32[4,32,256]{2,1,0:T(8,128)S(1)}, u32[]{:S(2)}, u32[]{:S(2)}) %collective-permute-start.22) | collective-permute-done | bytes 131104 | tf_op jit(solution)/shard_map/ppermute | solution.py:265
  92.0 1.3 %grad.1 = f32[4,32,16,128]{3,2,1,0:T(8,128)S(1)} custom-call(s32[5]{0:T(128)S(1)} %stack.32.place, f32[2,32,1536]{2,1,0:T(8,128)S(1)} %pad_maximum_fusion.1.refs_0_, f32[2,32,1536]{2,1,0:T(8,128)S(1)} %collective-permute-done.1.refs_2_.refs_1_, f32[2,32,1536]{2,1,0:T(8,128)S(1)} %collective-permute-done.2.refs_3_.refs_2_, ...), custom_call_target="tpu_custom_call" | custom-call | flops 1000 | bytes 1000 | tf_op jit(solution)/shard_map/grad/pallas_call | solution.py:183
  93.4 0.1 slice_bitcast_fusion.1
  93.5 0.5 collective-permute-start.23
  94.0 2.8 %collective-permute-start.24 = (f32[32,16,128]{2,1,0:T(8,128)S(1)}, f32[32,16,128]{2,1,0:T(8,128)S(1)}, u32[]{:S(2)}, u32[]{:S(2)}) collective-permute-start(f32[32,16,128]{2,1,0:T(8,128)S(1)} %get-tuple-element.33), channel_id=1, source_target_pairs={{0,4},{1,17},{2,6},{3,19},{4,0},{5,21},{6,2},{7,23},{8,12},{9,25},... | collective-permute-start | bytes 786440 | tf_op jit(solution)/shard_map/ppermute | solution.py:265
  96.8 3.2 %collective-permute-done.23 = f32[32,16,128]{2,1,0:T(8,128)S(1)} collective-permute-done((f32[32,16,128]{2,1,0:T(8,128)S(1)}, f32[32,16,128]{2,1,0:T(8,128)S(1)}, u32[]{:S(2)}, u32[]{:S(2)}) %collective-permute-start.23) | collective-permute-done | bytes 262176 | tf_op jit(solution)/shard_map/ppermute | solution.py:265
  100.0 3.4 %collective-permute-done.24 = f32[32,16,128]{2,1,0:T(8,128)S(1)} collective-permute-done((f32[32,16,128]{2,1,0:T(8,128)S(1)}, f32[32,16,128]{2,1,0:T(8,128)S(1)}, u32[]{:S(2)}, u32[]{:S(2)}) %collective-permute-start.24) | collective-permute-done | bytes 262176 | tf_op jit(solution)/shard_map/ppermute | solution.py:265
  103.3 0.4 collective-permute-done.25
  103.7 0.1 fusion.5
  103.8 19.0 %all_to_all.5 = f32[32,16,128]{2,1,0:T(8,128)S(1)} all-to-all(f32[32,16,128]{2,1,0:T(8,128)S(1)} %fusion.5), channel_id=1, replica_groups={{0,8,16,24,32,40,48,56,64,72,80,88,96,104,112,120,128,136,144,152,160,1..., dimensions={0} | all-to-all | bytes 524288 | tf_op jit(solution)/shard_map/all_to_all | solution.py:294
  122.8 6.2 %collective-permute-start.26 = (f32[4,16,128]{2,1,0:T(8,128)S(1)}, f32[4,16,128]{2,1,0:T(8,128)S(1)}, u32[]{:S(2)}, u32[]{:S(2)}) collective-permute-start(f32[4,16,128]{2,1,0:T(8,128)S(1)} %reduce_sum.9.own), channel_id=1, source_target_pairs={{0,1},{1,0},{2,3},{3,2},{4,5},{5,4},{6,7},{7,6},{8,9},{9,8},{10,11... | collective-permute-start | bytes 98312 | tf_op jit(solution)/shard_map/ppermute | solution.py:265
  129.1 0.9 collective-permute-done.26.got
  129.9 1.3 arrange.1
  131.2 0.1 multiply_reduce_fusion
  131.3 0.5 multiply_subtract_fusion
  (26 shorter events, 0.1 us)
Async XLA Ops:
  0.6 4.6 %collective-permute-start = (f32[32,1536]{1,0:T(8,128)}, f32[32,1536]{1,0:T(8,128)S(1)}, u32[]{:S(2)}, u32[]{:S(2)}) collective-permute-start(f32[32,1536]{1,0:T(8,128)} %param.6), channel_id=1, source_target_pairs={{0,1},{1,0},{2,3},{3,2},{4,5},{5,4},{6,7},{7,6},{8,9},{9,8},{10,11... | collective-permute-start | bytes 589832 | tf_op jit(solution)/shard_map/ppermute | solution.py:265
  4.0 26.1 %collective-permute-start.5 = (f32[512,256]{1,0:T(8,128)}, f32[512,256]{1,0:T(8,128)}, u32[]{:S(2)}, u32[]{:S(2)}) collective-permute-start(f32[512,256]{1,0:T(8,128)} %refs_0_.1), channel_id=1, source_target_pairs={{0,128},{64,192},{128,0},{192,64},{1,129},{65,193},{129,1},{193,65... | collective-permute-start | bytes 1572872 | tf_op jit(solution)/shard_map/ppermute | solution.py:281
  6.2 24.7 %collective-permute-start.1 = (f32[2,32,1536]{2,1,0:T(8,128)S(1)}, f32[2,32,1536]{2,1,0:T(8,128)S(1)}, u32[]{:S(2)}, u32[]{:S(2)}) collective-permute-start(f32[2,32,1536]{2,1,0:T(8,128)S(1)} %pad_maximum_fusion.1.refs_0_), channel_id=1, source_target_pairs={{0,8},{1,3},{2,10},{3,5},{4,12},{5,7},{6,14},{7,1},{8,16},{9,11},{... | collective-permute-start | bytes 1179656 | tf_op jit(solution)/shard_map/ppermute | solution.py:265
  7.5 23.4 %collective-permute-start.2 = (f32[2,32,1536]{2,1,0:T(8,128)S(1)}, f32[2,32,1536]{2,1,0:T(8,128)S(1)}, u32[]{:S(2)}, u32[]{:S(2)}) collective-permute-start(f32[2,32,1536]{2,1,0:T(8,128)S(1)} %pad_maximum_fusion.1.refs_0_), channel_id=1, source_target_pairs={{0,16},{1,5},{2,18},{3,7},{4,20},{5,1},{6,22},{7,3},{8,24},{9,13},... | collective-permute-start | bytes 1179656 | tf_op jit(solution)/shard_map/ppermute | solution.py:265
  9.9 21.0 %collective-permute-start.3 = (f32[2,32,1536]{2,1,0:T(8,128)S(1)}, f32[2,32,1536]{2,1,0:T(8,128)S(1)}, u32[]{:S(2)}, u32[]{:S(2)}) collective-permute-start(f32[2,32,1536]{2,1,0:T(8,128)S(1)} %pad_maximum_fusion.1.refs_0_), channel_id=1, source_target_pairs={{0,24},{1,7},{2,26},{3,1},{4,28},{5,3},{6,30},{7,5},{8,0},{9,15},{... | collective-permute-start | bytes 1179656 | tf_op jit(solution)/shard_map/ppermute | solution.py:265
  11.1 26.3 %collective-permute-start.9 = (f32[512,256]{1,0:T(8,128)}, f32[512,256]{1,0:T(8,128)S(1)}, u32[]{:S(2)}, u32[]{:S(2)}) collective-permute-start(f32[512,256]{1,0:T(8,128)} %refs_0_.1), channel_id=1, source_target_pairs={{0,64},{64,0},{128,192},{192,128},{1,65},{65,1},{129,193},{193,129... | collective-permute-start | bytes 1572872 | tf_op jit(solution)/shard_map/ppermute | solution.py:280
  12.8 2.2 %copy-start = (f32[2048,512]{1,0:T(8,128)S(1)}, f32[2048,512]{1,0:T(8,128)}, u32[]{:S(2)}) copy-start(f32[2048,512]{1,0:T(8,128)} %param.5) | copy-start | bytes 12582916
  15.0 1.0 copy-start.1
  30.1 3.1 %collective-permute-start.4 = (f32[4,4,1,32,512]{4,3,1,2,0:T(8,128)S(1)}, f32[4,4,1,32,512]{4,3,1,2,0:T(8,128)S(1)}, u32[]{:S(2)}, u32[]{:S(2)}) collective-permute-start(f32[4,4,1,32,512]{4,3,1,2,0:T(8,128)S(1)} %bitcast.89), channel_id=1, source_target_pairs={{0,1},{1,0},{2,3},{3,2},{4,5},{5,4},{6,7},{7,6},{8,9},{9,8},{10,11... | collective-permute-start | bytes 3145736 | tf_op jit(solution)/shard_map/ppermute | solution.py:265
  30.9 15.1 %collective-permute-start.14 = (f32[512,256]{1,0:T(8,128)}, f32[512,256]{1,0:T(8,128)}, u32[]{:S(2)}, u32[]{:S(2)}) collective-permute-start(f32[512,256]{1,0:T(8,128)} %collective-permute-done.5.refs_1_), channel_id=1, source_target_pairs={{0,64},{64,0},{128,192},{192,128},{1,65},{65,1},{129,193},{193,129... | collective-permute-start | bytes 1572872 | tf_op jit(solution)/shard_map/ppermute | solution.py:284
  33.5 10.4 %collective-permute-start.6 = (f32[4,1,32,512]{3,2,0,1:T(8,128)S(1)}, f32[4,1,32,512]{3,2,0,1:T(8,128)S(1)}, u32[]{:S(2)}, u32[]{:S(2)}) collective-permute-start(f32[4,1,32,512]{3,2,0,1:T(8,128)S(1)} %get-tuple-element.32), channel_id=1, source_target_pairs={{0,2},{1,9},{2,4},{3,11},{4,6},{5,13},{6,0},{7,15},{8,10},{9,17},{... | collective-permute-start | bytes 786440 | tf_op jit(solution)/shard_map/ppermute | solution.py:265
  33.7 10.1 %collective-permute-start.7 = (f32[4,1,32,512]{3,2,0,1:T(8,128)S(1)}, f32[4,1,32,512]{3,2,0,1:T(8,128)S(1)}, u32[]{:S(2)}, u32[]{:S(2)}) collective-permute-start(f32[4,1,32,512]{3,2,0,1:T(8,128)S(1)} %get-tuple-element.30), channel_id=1, source_target_pairs={{0,4},{1,17},{2,6},{3,19},{4,0},{5,21},{6,2},{7,23},{8,12},{9,25},... | collective-permute-start | bytes 786440 | tf_op jit(solution)/shard_map/ppermute | solution.py:265
  36.3 7.5 %collective-permute-start.8 = (f32[4,1,32,512]{3,2,1,0:T(8,128)S(1)}, f32[4,1,32,512]{3,2,1,0:T(8,128)S(1)}, u32[]{:S(2)}, u32[]{:S(2)}) collective-permute-start(f32[4,1,32,512]{3,2,1,0:T(8,128)S(1)} %get-tuple-element.31), channel_id=1, source_target_pairs={{0,6},{1,25},{2,0},{3,27},{4,2},{5,29},{6,4},{7,31},{8,14},{9,1},{... | collective-permute-start | bytes 786440 | tf_op jit(solution)/shard_map/ppermute | solution.py:265
  42.5 9.1 %collective-permute-start.10 = (f32[4,4,2,32,512]{4,3,2,1,0:T(8,128)S(1)}, f32[4,4,2,32,512]{4,3,2,1,0:T(8,128)S(1)}, u32[]{:S(2)}, u32[]{:S(2)}) collective-permute-start(f32[4,4,2,32,512]{4,3,2,1,0:T(8,128)S(1)} %get-tuple-element.18), channel_id=1, source_target_pairs={{0,1},{1,0},{2,3},{3,2},{4,5},{5,4},{6,7},{7,6},{8,9},{9,8},{10,11... | collective-permute-start | bytes 6291464 | tf_op jit(solution)/shard_map/ppermute | solution.py:265
  49.4 5.3 %collective-permute-start.15 = (f32[4,4,1,32,512]{4,3,1,2,0:T(8,128)S(1)}, f32[4,4,1,32,512]{4,3,1,2,0:T(8,128)S(1)}, u32[]{:S(2)}, u32[]{:S(2)}) collective-permute-start(f32[4,4,1,32,512]{4,3,1,2,0:T(8,128)S(1)} %bitcast.88), channel_id=1, source_target_pairs={{0,1},{1,0},{2,3},{3,2},{4,5},{5,4},{6,7},{7,6},{8,9},{9,8},{10,11... | collective-permute-start | bytes 3145736 | tf_op jit(solution)/shard_map/ppermute | solution.py:265
  52.0 15.2 %collective-permute-start.11 = (f32[4,2,32,512]{3,2,1,0:T(8,128)S(1)}, f32[4,2,32,512]{3,2,1,0:T(8,128)S(1)}, u32[]{:S(2)}, u32[]{:S(2)}) collective-permute-start(f32[4,2,32,512]{3,2,1,0:T(8,128)S(1)} %get-tuple-element.26), channel_id=1, source_target_pairs={{0,2},{1,9},{2,4},{3,11},{4,6},{5,13},{6,0},{7,15},{8,10},{9,17},{... | collective-permute-start | bytes 1572872 | tf_op jit(solution)/shard_map/ppermute | solution.py:265
  52.2 15.0 %collective-permute-start.12 = (f32[4,2,32,512]{3,2,1,0:T(8,128)S(1)}, f32[4,2,32,512]{3,2,1,0:T(8,128)S(1)}, u32[]{:S(2)}, u32[]{:S(2)}) collective-permute-start(f32[4,2,32,512]{3,2,1,0:T(8,128)S(1)} %get-tuple-element.24), channel_id=1, source_target_pairs={{0,4},{1,17},{2,6},{3,19},{4,0},{5,21},{6,2},{7,23},{8,12},{9,25},... | collective-permute-start | bytes 1572872 | tf_op jit(solution)/shard_map/ppermute | solution.py:265
  52.8 15.0 %collective-permute-start.13 = (f32[4,2,32,512]{3,2,1,0:T(8,128)S(1)}, f32[4,2,32,512]{3,2,1,0:T(8,128)S(1)}, u32[]{:S(2)}, u32[]{:S(2)}) collective-permute-start(f32[4,2,32,512]{3,2,1,0:T(8,128)S(1)} %get-tuple-element.25), channel_id=1, source_target_pairs={{0,6},{1,25},{2,0},{3,27},{4,2},{5,29},{6,4},{7,31},{8,14},{9,1},{... | collective-permute-start | bytes 1572872 | tf_op jit(solution)/shard_map/ppermute | solution.py:265
  54.9 17.9 %collective-permute-start.16 = (f32[4,1,32,512]{3,2,0,1:T(8,128)S(1)}, f32[4,1,32,512]{3,2,0,1:T(8,128)S(1)}, u32[]{:S(2)}, u32[]{:S(2)}) collective-permute-start(f32[4,1,32,512]{3,2,0,1:T(8,128)S(1)} %get-tuple-element.29), channel_id=1, source_target_pairs={{0,2},{1,9},{2,4},{3,11},{4,6},{5,13},{6,0},{7,15},{8,10},{9,17},{... | collective-permute-start | bytes 786440 | tf_op jit(solution)/shard_map/ppermute | solution.py:265
  55.5 17.3 %collective-permute-start.17 = (f32[4,1,32,512]{3,2,0,1:T(8,128)S(1)}, f32[4,1,32,512]{3,2,0,1:T(8,128)S(1)}, u32[]{:S(2)}, u32[]{:S(2)}) collective-permute-start(f32[4,1,32,512]{3,2,0,1:T(8,128)S(1)} %get-tuple-element.27), channel_id=1, source_target_pairs={{0,4},{1,17},{2,6},{3,19},{4,0},{5,21},{6,2},{7,23},{8,12},{9,25},... | collective-permute-start | bytes 786440 | tf_op jit(solution)/shard_map/ppermute | solution.py:265
  67.2 6.3 %collective-permute-start.18 = (f32[4,1,32,512]{3,2,1,0:T(8,128)S(1)}, f32[4,1,32,512]{3,2,1,0:T(8,128)S(1)}, u32[]{:S(2)}, u32[]{:S(2)}) collective-permute-start(f32[4,1,32,512]{3,2,1,0:T(8,128)S(1)} %get-tuple-element.28), channel_id=1, source_target_pairs={{0,6},{1,25},{2,0},{3,27},{4,2},{5,29},{6,4},{7,31},{8,14},{9,1},{... | collective-permute-start | bytes 786440 | tf_op jit(solution)/shard_map/ppermute | solution.py:265
  73.8 9.6 %collective-permute-start.19 = (f32[4,32,512]{2,1,0:T(8,128)S(1)}, f32[4,32,512]{2,1,0:T(8,128)S(1)}, u32[]{:S(2)}, u32[]{:S(2)}) collective-permute-start(f32[4,32,512]{2,1,0:T(8,128)S(1)} %get-tuple-element.38), channel_id=1, source_target_pairs={{0,8},{1,3},{2,10},{3,5},{4,12},{5,7},{6,14},{7,1},{8,16},{9,11},{... | collective-permute-start | bytes 786440 | tf_op jit(solution)/shard_map/ppermute | solution.py:265
  73.9 9.5 %collective-permute-start.20 = (f32[4,32,512]{2,1,0:T(8,128)S(1)}, f32[4,32,512]{2,1,0:T(8,128)S(1)}, u32[]{:S(2)}, u32[]{:S(2)}) collective-permute-start(f32[4,32,512]{2,1,0:T(8,128)S(1)} %get-tuple-element.36), channel_id=1, source_target_pairs={{0,16},{1,5},{2,18},{3,7},{4,20},{5,1},{6,22},{7,3},{8,24},{9,13},... | collective-permute-start | bytes 786440 | tf_op jit(solution)/shard_map/ppermute | solution.py:265
  74.7 9.4 %collective-permute-start.21 = (f32[4,32,512]{2,1,0:T(8,128)S(1)}, f32[4,32,512]{2,1,0:T(8,128)S(1)}, u32[]{:S(2)}, u32[]{:S(2)}) collective-permute-start(f32[4,32,512]{2,1,0:T(8,128)S(1)} %get-tuple-element.37), channel_id=1, source_target_pairs={{0,24},{1,7},{2,26},{3,1},{4,28},{5,3},{6,30},{7,5},{8,0},{9,15},{... | collective-permute-start | bytes 786440 | tf_op jit(solution)/shard_map/ppermute | solution.py:265
  84.1 7.9 %collective-permute-start.22 = (f32[4,32,256]{2,1,0:T(8,128)S(1)}, f32[4,32,256]{2,1,0:T(8,128)S(1)}, u32[]{:S(2)}, u32[]{:S(2)}) collective-permute-start(f32[4,32,256]{2,1,0:T(8,128)S(1)} %slice.161), channel_id=1, source_target_pairs={{0,32},{1,33},{2,34},{3,35},{4,36},{5,37},{6,38},{7,39},{8,40},{9,... | collective-permute-start | bytes 393224 | tf_op jit(solution)/shard_map/ppermute | solution.py:265
  93.4 36.6 %copy-start.2 = (f32[1024]{0:T(1024)S(1)}, f32[1024]{0:T(1024)}, u32[]{:S(2)}) copy-start(f32[1024]{0:T(1024)} %param.8) | copy-start | bytes 12292
  93.4 37.9 %copy-start.3 = (f32[6]{0:T(128)S(1)}, f32[6]{0:T(128)}, u32[]{:S(2)}) copy-start(f32[6]{0:T(128)} %param.9) | copy-start | bytes 76
  93.5 6.5 %collective-permute-start.23 = (f32[32,16,128]{2,1,0:T(8,128)S(1)}, f32[32,16,128]{2,1,0:T(8,128)S(1)}, u32[]{:S(2)}, u32[]{:S(2)}) collective-permute-start(f32[32,16,128]{2,1,0:T(8,128)S(1)} %get-tuple-element.35), channel_id=1, source_target_pairs={{0,2},{1,9},{2,4},{3,11},{4,6},{5,13},{6,0},{7,15},{8,10},{9,17},{... | collective-permute-start | bytes 786440 | tf_op jit(solution)/shard_map/ppermute | solution.py:265
  94.0 9.3 %collective-permute-start.24 = (f32[32,16,128]{2,1,0:T(8,128)S(1)}, f32[32,16,128]{2,1,0:T(8,128)S(1)}, u32[]{:S(2)}, u32[]{:S(2)}) collective-permute-start(f32[32,16,128]{2,1,0:T(8,128)S(1)} %get-tuple-element.33), channel_id=1, source_target_pairs={{0,4},{1,17},{2,6},{3,19},{4,0},{5,21},{6,2},{7,23},{8,12},{9,25},... | collective-permute-start | bytes 786440 | tf_op jit(solution)/shard_map/ppermute | solution.py:265
  96.8 6.9 %collective-permute-start.25 = (f32[32,16,128]{2,1,0:T(8,128)S(1)}, f32[32,16,128]{2,1,0:T(8,128)S(1)}, u32[]{:S(2)}, u32[]{:S(2)}) collective-permute-start(f32[32,16,128]{2,1,0:T(8,128)S(1)} %get-tuple-element.34), channel_id=1, source_target_pairs={{0,6},{1,25},{2,0},{3,27},{4,2},{5,29},{6,4},{7,31},{8,14},{9,1},{... | collective-permute-start | bytes 786440 | tf_op jit(solution)/shard_map/ppermute | solution.py:265
  122.8 7.1 %collective-permute-start.26 = (f32[4,16,128]{2,1,0:T(8,128)S(1)}, f32[4,16,128]{2,1,0:T(8,128)S(1)}, u32[]{:S(2)}, u32[]{:S(2)}) collective-permute-start(f32[4,16,128]{2,1,0:T(8,128)S(1)} %reduce_sum.9.own), channel_id=1, source_target_pairs={{0,1},{1,0},{2,3},{3,2},{4,5},{5,4},{6,7},{7,6},{8,9},{9,8},{10,11... | collective-permute-start | bytes 98312 | tf_op jit(solution)/shard_map/ppermute | solution.py:265

commit v4 on v3

--- a/solution.py
+++ b/solution.py
@@ -280,7 +280,7 @@
     near = lax.ppermute(cost_target, "grp", [(i, i ^ 1) for i in range(NG)])
     far = lax.ppermute(cost_target, "grp", [(i, i ^ 2) for i in range(NG)])
     own0, send0 = carry(place, halved, (cost_target,), 1000)
-    got0 = wide(send0, CORE_SWAP) + meet(BIG, own0.shape[-1], own0, far, *costs)
+    got0 = wide(send0, CORE_SWAP) + meet(BIG, own0.shape[-1], own0, far, near, *costs)
     last = lax.ppermute(far, "grp", [(i, i ^ 1) for i in range(NG)])
     total0 = along_rows(own0, got0)
     own1, send1 = carry(place, halved, (near, far), BIG)

time: 132 us -> 131 us (level)
  waiting for transfers between devices: 49.4 us -> 44.7 us
  starting transfers between devices: 41.8 us -> 43.6 us
  blocking collectives: 19 us -> 20.6 us
    ppermute x24, waiting for transfers between devices: 36.3 us -> 32.9 us  [wide(): return lax.ppermute(v, 'wide', pairs)]
    ppermute x24, starting transfers between devices: 38.9 us -> 40.7 us  [wide(): return lax.ppermute(v, 'wide', pairs)]
    all_to_all x1, blocking collectives: 19 us -> 20.6 us  [body(): lax.all_to_all(partial, ('grp', 'wide'), 0, 0, axis_index_groups=GATHER_G...]
  transfers between devices with their start and end apart: 27 -> 27, of which waited for: 14 -> 16; matrix products, arithmetic and copies ran while one was open for 2% -> 2% of each run, Pallas kernels for 10% -> 10%
where the time goes in v4:
time: 131 us
  waiting for transfers between devices  44.7 us (34%)
  starting transfers between devices  43.6 us (33%)
  blocking collectives  20.6 us (16%)
  Pallas kernels  15.2 us (12%)
  other arithmetic  3.19 us (2%)
  local copies, waits for them, and re-layouts  2.41 us (2%)
    ppermute x24, starting transfers between devices, wide(): return lax.ppermute(v, 'wide', pairs)  40.7 us
    ppermute x24, waiting for transfers between devices, wide(): return lax.ppermute(v, 'wide', pairs)  32.9 us
    all_to_all x1, blocking collectives, body(): lax.all_to_all(partial, ('grp', 'wide'), 0, 0, axis_index_groups=GATHER_G...  20.6 us
    pallas_call x3, Pallas kernels, carry(): pl.pallas_call(carry_kernel, in_specs=[SMEM, VMEM, VMEM] + [VMEM] * len(b...  11.5 us
    ppermute x1, waiting for transfers between devices, body(): far = lax.ppermute(cost_target, 'grp', [(i, i ^ 2) for i in range(NG)])  11.1 us
  transfers between devices with their start and end apart: 27, of which 16 were waited for; matrix products, arithmetic and copies ran while one was open for 2% of the time, Pallas kernels for 10%

profile of v4, /device:TPU:1, one launch (start us, length us, event | category | flops | bytes accessed | tf_op | source)
XLA Modules:
  0.0 130.6 jit_solution(12341562264427670538)
XLA Ops:
  0.6 3.3 %collective-permute-start = (f32[32,1536]{1,0:T(8,128)}, f32[32,1536]{1,0:T(8,128)S(1)}, u32[]{:S(2)}, u32[]{:S(2)}) collective-permute-start(f32[32,1536]{1,0:T(8,128)} %param.6), channel_id=1, source_target_pairs={{0,1},{1,0},{2,3},{3,2},{4,5},{5,4},{6,7},{7,6},{8,9},{9,8},{10,11... | collective-permute-start | bytes 589832 | tf_op jit(solution)/shard_map/ppermute | solution.py:265
  4.0 1.3 collective-permute-start.5
  5.2 1.6 %collective-permute-start.6 = (f32[512,256]{1,0:T(8,128)}, f32[512,256]{1,0:T(8,128)S(1)}, u32[]{:S(2)}, u32[]{:S(2)}) collective-permute-start(f32[512,256]{1,0:T(8,128)} %refs_0_.1), channel_id=1, source_target_pairs={{0,64},{64,0},{128,192},{192,128},{1,65},{65,1},{129,193},{193,129... | collective-permute-start | bytes 1572872 | tf_op jit(solution)/shard_map/ppermute | solution.py:280
  6.9 1.0 pad_maximum_fusion.1.refs_0_
  7.8 1.3 collective-permute-start.1
  9.1 2.5 %collective-permute-start.2 = (f32[2,32,1536]{2,1,0:T(8,128)S(1)}, f32[2,32,1536]{2,1,0:T(8,128)S(1)}, u32[]{:S(2)}, u32[]{:S(2)}) collective-permute-start(f32[2,32,1536]{2,1,0:T(8,128)S(1)} %pad_maximum_fusion.1.refs_0_), channel_id=1, source_target_pairs={{0,16},{1,5},{2,18},{3,7},{4,20},{5,1},{6,22},{7,3},{8,24},{9,13},... | collective-permute-start | bytes 1179656 | tf_op jit(solution)/shard_map/ppermute | solution.py:265
  11.6 1.2 collective-permute-start.3
  12.7 0.1 stack.32.place
  12.8 2.2 %copy-done = f32[2048,512]{1,0:T(8,128)S(1)} copy-done((f32[2048,512]{1,0:T(8,128)S(1)}, f32[2048,512]{1,0:T(8,128)}, u32[]{:S(2)}) %copy-start) | copy-done | bytes 4194328
  15.0 1.0 split.1
  16.0 2.9 %carry.3 = (f32[4,4,1,32,512]{4,3,2,1,0:T(8,128)S(1)}, f32[4,4,1,32,512]{4,3,2,1,0:T(8,128)S(1)}) custom-call(s32[5]{0:T(128)S(1)} %stack.32.place, bf16[4,512,512]{2,1,0:T(8,128)(2,1)S(1)} %get-tuple-element.13.hi_ref, bf16[4,512,512]{2,1,0:T(8,128)(2,1)S(1)} %get-tuple-element.14.lo_ref, f32[512,256]{1,0:T(8,128)S(1)} %copy-done.1), custom_call_target="tpu_custom_call" | custom-call | flops 1000 | bytes 1000 | tf_op jit(solution)/shard_map/carry/pallas_call | solution.py:131
  19.0 11.1 %collective-permute-done.5.refs_1_ = f32[512,256]{1,0:T(8,128)} collective-permute-done((f32[512,256]{1,0:T(8,128)}, f32[512,256]{1,0:T(8,128)}, u32[]{:S(2)}, u32[]{:S(2)}) %collective-permute-start.5) | collective-permute-done | bytes 524320 | tf_op jit(solution)/shard_map/ppermute | solution.py:281
  30.1 0.8 collective-permute-start.4
  30.9 2.2 %collective-permute-done.4 = f32[4,4,1,32,512]{4,3,1,2,0:T(8,128)S(1)} collective-permute-done((f32[4,4,1,32,512]{4,3,1,2,0:T(8,128)S(1)}, f32[4,4,1,32,512]{4,3,1,2,0:T(8,128)S(1)}, u32[]{:S(2)}, u32[]{:S(2)}) %collective-permute-start.4) | collective-permute-done | bytes 1048608 | tf_op jit(solution)/shard_map/ppermute | solution.py:265
  33.2 0.1 broadcast_add_fusion
  33.3 0.1 fusion.14
  33.5 0.2 collective-permute-start.7
  33.7 2.6 %collective-permute-start.8 = (f32[4,1,32,512]{3,2,0,1:T(8,128)S(1)}, f32[4,1,32,512]{3,2,0,1:T(8,128)S(1)}, u32[]{:S(2)}, u32[]{:S(2)}) collective-permute-start(f32[4,1,32,512]{3,2,0,1:T(8,128)S(1)} %get-tuple-element.30), channel_id=1, source_target_pairs={{0,4},{1,17},{2,6},{3,19},{4,0},{5,21},{6,2},{7,23},{8,12},{9,25},... | collective-permute-start | bytes 786440 | tf_op jit(solution)/shard_map/ppermute | solution.py:265
  36.3 1.1 collective-permute-start.9
  37.4 5.1 %carry.4 = (f32[4,4,2,32,512]{4,3,2,1,0:T(8,128)S(1)}, f32[4,4,2,32,512]{4,3,2,1,0:T(8,128)S(1)}) custom-call(s32[5]{0:T(128)S(1)} %stack.32.place, bf16[4,512,512]{2,1,0:T(8,128)(2,1)S(1)} %get-tuple-element.13.hi_ref, bf16[4,512,512]{2,1,0:T(8,128)(2,1)S(1)} %get-tuple-element.14.lo_ref, f32[512,256]{1,0:T(8,128)S(1)} %collective-permute-done.6.refs_2_.refs_0_, ...), custom_call_target="tpu_custom_call" | custom-call | flops 99999997952 | bytes 1000 | tf_op jit(solution)/shard_map/carry/pallas_call | solution.py:131
  42.5 1.3 collective-permute-start.10
  43.8 0.1 fusion.17
  44.0 0.8 collective-permute-done.14.refs_0_
  44.7 3.5 %carry.5 = (f32[4,4,1,32,512]{4,3,2,1,0:T(8,128)S(1)}, f32[4,4,1,32,512]{4,3,2,1,0:T(8,128)S(1)}) custom-call(s32[5]{0:T(128)S(1)} %stack.32.place, bf16[4,512,512]{2,1,0:T(8,128)(2,1)S(1)} %get-tuple-element.13.hi_ref, bf16[4,512,512]{2,1,0:T(8,128)(2,1)S(1)} %get-tuple-element.14.lo_ref, f32[512,256]{1,0:T(8,128)} %collective-permute-done.14.refs_0_), custom_call_target="tpu_custom_call" | custom-call | flops 99999997952 | bytes 1000 | tf_op jit(solution)/shard_map/carry/pallas_call | solution.py:131
  48.2 0.9 collective-permute-start.15
  49.1 0.3 fusion.1
  49.4 0.2 collective-permute-start.11
  49.7 2.6 %collective-permute-start.12 = (f32[4,2,32,512]{3,2,1,0:T(8,128)S(1)}, f32[4,2,32,512]{3,2,1,0:T(8,128)S(1)}, u32[]{:S(2)}, u32[]{:S(2)}) collective-permute-start(f32[4,2,32,512]{3,2,1,0:T(8,128)S(1)} %get-tuple-element.24), channel_id=1, source_target_pairs={{0,4},{1,17},{2,6},{3,19},{4,0},{5,21},{6,2},{7,23},{8,12},{9,25},... | collective-permute-start | bytes 1572872 | tf_op jit(solution)/shard_map/ppermute | solution.py:265
  52.3 1.1 collective-permute-start.13
  53.4 0.1 fusion.8
  53.5 0.5 collective-permute-start.16
  54.0 0.9 collective-permute-start.17
  54.9 4.2 %collective-permute-done.11 = f32[4,2,32,512]{3,2,1,0:T(8,128)S(1)} collective-permute-done((f32[4,2,32,512]{3,2,1,0:T(8,128)S(1)}, f32[4,2,32,512]{3,2,1,0:T(8,128)S(1)}, u32[]{:S(2)}, u32[]{:S(2)}) %collective-permute-start.11) | collective-permute-done | bytes 524320 | tf_op jit(solution)/shard_map/ppermute | solution.py:265
  59.0 0.4 collective-permute-start.18
  59.4 5.4 %collective-permute-done.12 = f32[4,2,32,512]{3,2,1,0:T(8,128)S(1)} collective-permute-done((f32[4,2,32,512]{3,2,1,0:T(8,128)S(1)}, f32[4,2,32,512]{3,2,1,0:T(8,128)S(1)}, u32[]{:S(2)}, u32[]{:S(2)}) %collective-permute-start.12) | collective-permute-done | bytes 524320 | tf_op jit(solution)/shard_map/ppermute | solution.py:265
  64.8 0.5 collective-permute-done.13
  65.3 0.3 fusion.4.refs_0_
  65.6 1.9 %collective-permute-done.16 = f32[4,1,32,512]{3,2,0,1:T(8,128)S(1)} collective-permute-done((f32[4,1,32,512]{3,2,0,1:T(8,128)S(1)}, f32[4,1,32,512]{3,2,0,1:T(8,128)S(1)}, u32[]{:S(2)}, u32[]{:S(2)}) %collective-permute-start.16) | collective-permute-done | bytes 262176 | tf_op jit(solution)/shard_map/ppermute | solution.py:265
  67.5 3.0 %collective-permute-done.17 = f32[4,1,32,512]{3,2,0,1:T(8,128)S(1)} collective-permute-done((f32[4,1,32,512]{3,2,0,1:T(8,128)S(1)}, f32[4,1,32,512]{3,2,0,1:T(8,128)S(1)}, u32[]{:S(2)}, u32[]{:S(2)}) %collective-permute-start.17) | collective-permute-done | bytes 262176 | tf_op jit(solution)/shard_map/ppermute | solution.py:265
  70.4 0.5 collective-permute-done.18
  70.9 0.1 fusion.12
  71.1 0.1 pad_maximum_fusion
  71.2 0.9 collective-permute-start.19
  72.1 2.6 %collective-permute-start.20 = (f32[4,32,512]{2,1,0:T(8,128)S(1)}, f32[4,32,512]{2,1,0:T(8,128)S(1)}, u32[]{:S(2)}, u32[]{:S(2)}) collective-permute-start(f32[4,32,512]{2,1,0:T(8,128)S(1)} %get-tuple-element.36), channel_id=1, source_target_pairs={{0,16},{1,5},{2,18},{3,7},{4,20},{5,1},{6,22},{7,3},{8,24},{9,13},... | collective-permute-start | bytes 786440 | tf_op jit(solution)/shard_map/ppermute | solution.py:265
  74.7 0.7 collective-permute-start.21
  75.3 2.7 %collective-permute-done.19 = f32[4,32,512]{2,1,0:T(8,128)S(1)} collective-permute-done((f32[4,32,512]{2,1,0:T(8,128)S(1)}, f32[4,32,512]{2,1,0:T(8,128)S(1)}, u32[]{:S(2)}, u32[]{:S(2)}) %collective-permute-start.19) | collective-permute-done | bytes 262176 | tf_op jit(solution)/shard_map/ppermute | solution.py:265
  78.1 3.5 %collective-permute-done.20 = f32[4,32,512]{2,1,0:T(8,128)S(1)} collective-permute-done((f32[4,32,512]{2,1,0:T(8,128)S(1)}, f32[4,32,512]{2,1,0:T(8,128)S(1)}, u32[]{:S(2)}, u32[]{:S(2)}) %collective-permute-start.20) | collective-permute-done | bytes 262176 | tf_op jit(solution)/shard_map/ppermute | solution.py:265
  81.5 0.1 fusion.6
  81.6 5.8 %collective-permute-start.22 = (f32[4,32,256]{2,1,0:T(8,128)S(1)}, f32[4,32,256]{2,1,0:T(8,128)S(1)}, u32[]{:S(2)}, u32[]{:S(2)}) collective-permute-start(f32[4,32,256]{2,1,0:T(8,128)S(1)} %slice.161), channel_id=1, source_target_pairs={{0,32},{1,33},{2,34},{3,35},{4,36},{5,37},{6,38},{7,39},{8,40},{9,... | collective-permute-start | bytes 393224 | tf_op jit(solution)/shard_map/ppermute | solution.py:265
  87.4 2.5 %collective-permute-done.22 = f32[4,32,256]{2,1,0:T(8,128)S(1)} collective-permute-done((f32[4,32,256]{2,1,0:T(8,128)S(1)}, f32[4,32,256]{2,1,0:T(8,128)S(1)}, u32[]{:S(2)}, u32[]{:S(2)}) %collective-permute-start.22) | collective-permute-done | bytes 131104 | tf_op jit(solution)/shard_map/ppermute | solution.py:265
  89.9 1.3 %grad.1 = f32[4,32,16,128]{3,2,1,0:T(8,128)S(1)} custom-call(s32[5]{0:T(128)S(1)} %stack.32.place, f32[2,32,1536]{2,1,0:T(8,128)S(1)} %pad_maximum_fusion.1.refs_0_, f32[2,32,1536]{2,1,0:T(8,128)S(1)} %collective-permute-done.1.refs_3_.refs_1_, f32[2,32,1536]{2,1,0:T(8,128)S(1)} %collective-permute-done.2.refs_4_.refs_2_, ...), custom_call_target="tpu_custom_call" | custom-call | flops 1000 | bytes 1000 | tf_op jit(solution)/shard_map/grad/pallas_call | solution.py:183
  91.4 1.4 %collective-permute-start.23 = (f32[32,16,128]{2,1,0:T(8,128)S(1)}, f32[32,16,128]{2,1,0:T(8,128)S(1)}, u32[]{:S(2)}, u32[]{:S(2)}) collective-permute-start(f32[32,16,128]{2,1,0:T(8,128)S(1)} %get-tuple-element.35), channel_id=1, source_target_pairs={{0,2},{1,9},{2,4},{3,11},{4,6},{5,13},{6,0},{7,15},{8,10},{9,17},{... | collective-permute-start | bytes 786440 | tf_op jit(solution)/shard_map/ppermute | solution.py:265
  92.8 1.8 %collective-permute-start.24 = (f32[32,16,128]{2,1,0:T(8,128)S(1)}, f32[32,16,128]{2,1,0:T(8,128)S(1)}, u32[]{:S(2)}, u32[]{:S(2)}) collective-permute-start(f32[32,16,128]{2,1,0:T(8,128)S(1)} %get-tuple-element.33), channel_id=1, source_target_pairs={{0,4},{1,17},{2,6},{3,19},{4,0},{5,21},{6,2},{7,23},{8,12},{9,25},... | collective-permute-start | bytes 786440 | tf_op jit(solution)/shard_map/ppermute | solution.py:265
  94.5 1.3 collective-permute-start.25
  95.8 2.1 %collective-permute-done.23 = f32[32,16,128]{2,1,0:T(8,128)S(1)} collective-permute-done((f32[32,16,128]{2,1,0:T(8,128)S(1)}, f32[32,16,128]{2,1,0:T(8,128)S(1)}, u32[]{:S(2)}, u32[]{:S(2)}) %collective-permute-start.23) | collective-permute-done | bytes 262176 | tf_op jit(solution)/shard_map/ppermute | solution.py:265
  97.9 3.2 %collective-permute-done.24 = f32[32,16,128]{2,1,0:T(8,128)S(1)} collective-permute-done((f32[32,16,128]{2,1,0:T(8,128)S(1)}, f32[32,16,128]{2,1,0:T(8,128)S(1)}, u32[]{:S(2)}, u32[]{:S(2)}) %collective-permute-start.24) | collective-permute-done | bytes 262176 | tf_op jit(solution)/shard_map/ppermute | solution.py:265
  101.1 0.5 collective-permute-done.25
  101.6 0.1 fusion.5
  101.6 20.6 %all_to_all.5 = f32[32,16,128]{2,1,0:T(8,128)S(1)} all-to-all(f32[32,16,128]{2,1,0:T(8,128)S(1)} %fusion.5), channel_id=1, replica_groups={{0,8,16,24,32,40,48,56,64,72,80,88,96,104,112,120,128,136,144,152,160,1..., dimensions={0} | all-to-all | bytes 524288 | tf_op jit(solution)/shard_map/all_to_all | solution.py:294
  122.3 5.5 %collective-permute-start.26 = (f32[4,16,128]{2,1,0:T(8,128)S(1)}, f32[4,16,128]{2,1,0:T(8,128)S(1)}, u32[]{:S(2)}, u32[]{:S(2)}) collective-permute-start(f32[4,16,128]{2,1,0:T(8,128)S(1)} %reduce_sum.9.own), channel_id=1, source_target_pairs={{0,1},{1,0},{2,3},{3,2},{4,5},{5,4},{6,7},{7,6},{8,9},{9,8},{10,11... | collective-permute-start | bytes 98312 | tf_op jit(solution)/shard_map/ppermute | solution.py:265
  127.8 0.9 collective-permute-done.26.got
  128.7 1.3 arrange.1
  129.9 0.1 multiply_reduce_fusion
  130.0 0.5 multiply_subtract_fusion
  (26 shorter events, 0.2 us)
Async XLA Ops:
  0.6 6.2 %collective-permute-start = (f32[32,1536]{1,0:T(8,128)}, f32[32,1536]{1,0:T(8,128)S(1)}, u32[]{:S(2)}, u32[]{:S(2)}) collective-permute-start(f32[32,1536]{1,0:T(8,128)} %param.6), channel_id=1, source_target_pairs={{0,1},{1,0},{2,3},{3,2},{4,5},{5,4},{6,7},{7,6},{8,9},{9,8},{10,11... | collective-permute-start | bytes 589832 | tf_op jit(solution)/shard_map/ppermute | solution.py:265
  4.0 26.1 %collective-permute-start.5 = (f32[512,256]{1,0:T(8,128)}, f32[512,256]{1,0:T(8,128)}, u32[]{:S(2)}, u32[]{:S(2)}) collective-permute-start(f32[512,256]{1,0:T(8,128)} %refs_0_.1), channel_id=1, source_target_pairs={{0,128},{64,192},{128,0},{192,64},{1,129},{65,193},{129,1},{193,65... | collective-permute-start | bytes 1572872 | tf_op jit(solution)/shard_map/ppermute | solution.py:281
  5.2 25.6 %collective-permute-start.6 = (f32[512,256]{1,0:T(8,128)}, f32[512,256]{1,0:T(8,128)S(1)}, u32[]{:S(2)}, u32[]{:S(2)}) collective-permute-start(f32[512,256]{1,0:T(8,128)} %refs_0_.1), channel_id=1, source_target_pairs={{0,64},{64,0},{128,192},{192,128},{1,65},{65,1},{129,193},{193,129... | collective-permute-start | bytes 1572872 | tf_op jit(solution)/shard_map/ppermute | solution.py:280
  7.8 23.1 %collective-permute-start.1 = (f32[2,32,1536]{2,1,0:T(8,128)S(1)}, f32[2,32,1536]{2,1,0:T(8,128)S(1)}, u32[]{:S(2)}, u32[]{:S(2)}) collective-permute-start(f32[2,32,1536]{2,1,0:T(8,128)S(1)} %pad_maximum_fusion.1.refs_0_), channel_id=1, source_target_pairs={{0,8},{1,3},{2,10},{3,5},{4,12},{5,7},{6,14},{7,1},{8,16},{9,11},{... | collective-permute-start | bytes 1179656 | tf_op jit(solution)/shard_map/ppermute | solution.py:265
  9.1 21.8 %collective-permute-start.2 = (f32[2,32,1536]{2,1,0:T(8,128)S(1)}, f32[2,32,1536]{2,1,0:T(8,128)S(1)}, u32[]{:S(2)}, u32[]{:S(2)}) collective-permute-start(f32[2,32,1536]{2,1,0:T(8,128)S(1)} %pad_maximum_fusion.1.refs_0_), channel_id=1, source_target_pairs={{0,16},{1,5},{2,18},{3,7},{4,20},{5,1},{6,22},{7,3},{8,24},{9,13},... | collective-permute-start | bytes 1179656 | tf_op jit(solution)/shard_map/ppermute | solution.py:265
  11.6 19.3 %collective-permute-start.3 = (f32[2,32,1536]{2,1,0:T(8,128)S(1)}, f32[2,32,1536]{2,1,0:T(8,128)S(1)}, u32[]{:S(2)}, u32[]{:S(2)}) collective-permute-start(f32[2,32,1536]{2,1,0:T(8,128)S(1)} %pad_maximum_fusion.1.refs_0_), channel_id=1, source_target_pairs={{0,24},{1,7},{2,26},{3,1},{4,28},{5,3},{6,30},{7,5},{8,0},{9,15},{... | collective-permute-start | bytes 1179656 | tf_op jit(solution)/shard_map/ppermute | solution.py:265
  12.8 2.2 %copy-start = (f32[2048,512]{1,0:T(8,128)S(1)}, f32[2048,512]{1,0:T(8,128)}, u32[]{:S(2)}) copy-start(f32[2048,512]{1,0:T(8,128)} %param.5) | copy-start | bytes 12582916
  15.0 1.0 copy-start.1
  30.1 3.1 %collective-permute-start.4 = (f32[4,4,1,32,512]{4,3,1,2,0:T(8,128)S(1)}, f32[4,4,1,32,512]{4,3,1,2,0:T(8,128)S(1)}, u32[]{:S(2)}, u32[]{:S(2)}) collective-permute-start(f32[4,4,1,32,512]{4,3,1,2,0:T(8,128)S(1)} %bitcast.89), channel_id=1, source_target_pairs={{0,1},{1,0},{2,3},{3,2},{4,5},{5,4},{6,7},{7,6},{8,9},{9,8},{10,11... | collective-permute-start | bytes 3145736 | tf_op jit(solution)/shard_map/ppermute | solution.py:265
  30.9 13.9 %collective-permute-start.14 = (f32[512,256]{1,0:T(8,128)}, f32[512,256]{1,0:T(8,128)}, u32[]{:S(2)}, u32[]{:S(2)}) collective-permute-start(f32[512,256]{1,0:T(8,128)} %collective-permute-done.5.refs_1_), channel_id=1, source_target_pairs={{0,64},{64,0},{128,192},{192,128},{1,65},{65,1},{129,193},{193,129... | collective-permute-start | bytes 1572872 | tf_op jit(solution)/shard_map/ppermute | solution.py:284
  33.5 10.4 %collective-permute-start.7 = (f32[4,1,32,512]{3,2,0,1:T(8,128)S(1)}, f32[4,1,32,512]{3,2,0,1:T(8,128)S(1)}, u32[]{:S(2)}, u32[]{:S(2)}) collective-permute-start(f32[4,1,32,512]{3,2,0,1:T(8,128)S(1)} %get-tuple-element.32), channel_id=1, source_target_pairs={{0,2},{1,9},{2,4},{3,11},{4,6},{5,13},{6,0},{7,15},{8,10},{9,17},{... | collective-permute-start | bytes 786440 | tf_op jit(solution)/shard_map/ppermute | solution.py:265
  33.7 10.1 %collective-permute-start.8 = (f32[4,1,32,512]{3,2,0,1:T(8,128)S(1)}, f32[4,1,32,512]{3,2,0,1:T(8,128)S(1)}, u32[]{:S(2)}, u32[]{:S(2)}) collective-permute-start(f32[4,1,32,512]{3,2,0,1:T(8,128)S(1)} %get-tuple-element.30), channel_id=1, source_target_pairs={{0,4},{1,17},{2,6},{3,19},{4,0},{5,21},{6,2},{7,23},{8,12},{9,25},... | collective-permute-start | bytes 786440 | tf_op jit(solution)/shard_map/ppermute | solution.py:265
  36.3 7.5 %collective-permute-start.9 = (f32[4,1,32,512]{3,2,1,0:T(8,128)S(1)}, f32[4,1,32,512]{3,2,1,0:T(8,128)S(1)}, u32[]{:S(2)}, u32[]{:S(2)}) collective-permute-start(f32[4,1,32,512]{3,2,1,0:T(8,128)S(1)} %get-tuple-element.31), channel_id=1, source_target_pairs={{0,6},{1,25},{2,0},{3,27},{4,2},{5,29},{6,4},{7,31},{8,14},{9,1},{... | collective-permute-start | bytes 786440 | tf_op jit(solution)/shard_map/ppermute | solution.py:265
  42.5 6.6 %collective-permute-start.10 = (f32[4,4,2,32,512]{4,3,2,1,0:T(8,128)S(1)}, f32[4,4,2,32,512]{4,3,2,1,0:T(8,128)S(1)}, u32[]{:S(2)}, u32[]{:S(2)}) collective-permute-start(f32[4,4,2,32,512]{4,3,2,1,0:T(8,128)S(1)} %get-tuple-element.18), channel_id=1, source_target_pairs={{0,1},{1,0},{2,3},{3,2},{4,5},{5,4},{6,7},{7,6},{8,9},{9,8},{10,11... | collective-permute-start | bytes 6291464 | tf_op jit(solution)/shard_map/ppermute | solution.py:265
  48.2 5.2 %collective-permute-start.15 = (f32[4,4,1,32,512]{4,3,1,2,0:T(8,128)S(1)}, f32[4,4,1,32,512]{4,3,1,2,0:T(8,128)S(1)}, u32[]{:S(2)}, u32[]{:S(2)}) collective-permute-start(f32[4,4,1,32,512]{4,3,1,2,0:T(8,128)S(1)} %bitcast.88), channel_id=1, source_target_pairs={{0,1},{1,0},{2,3},{3,2},{4,5},{5,4},{6,7},{7,6},{8,9},{9,8},{10,11... | collective-permute-start | bytes 3145736 | tf_op jit(solution)/shard_map/ppermute | solution.py:265
  49.4 9.6 %collective-permute-start.11 = (f32[4,2,32,512]{3,2,1,0:T(8,128)S(1)}, f32[4,2,32,512]{3,2,1,0:T(8,128)S(1)}, u32[]{:S(2)}, u32[]{:S(2)}) collective-permute-start(f32[4,2,32,512]{3,2,1,0:T(8,128)S(1)} %get-tuple-element.26), channel_id=1, source_target_pairs={{0,2},{1,9},{2,4},{3,11},{4,6},{5,13},{6,0},{7,15},{8,10},{9,17},{... | collective-permute-start | bytes 1572872 | tf_op jit(solution)/shard_map/ppermute | solution.py:265
  49.7 15.1 %collective-permute-start.12 = (f32[4,2,32,512]{3,2,1,0:T(8,128)S(1)}, f32[4,2,32,512]{3,2,1,0:T(8,128)S(1)}, u32[]{:S(2)}, u32[]{:S(2)}) collective-permute-start(f32[4,2,32,512]{3,2,1,0:T(8,128)S(1)} %get-tuple-element.24), channel_id=1, source_target_pairs={{0,4},{1,17},{2,6},{3,19},{4,0},{5,21},{6,2},{7,23},{8,12},{9,25},... | collective-permute-start | bytes 1572872 | tf_op jit(solution)/shard_map/ppermute | solution.py:265
  52.3 13.0 %collective-permute-start.13 = (f32[4,2,32,512]{3,2,1,0:T(8,128)S(1)}, f32[4,2,32,512]{3,2,1,0:T(8,128)S(1)}, u32[]{:S(2)}, u32[]{:S(2)}) collective-permute-start(f32[4,2,32,512]{3,2,1,0:T(8,128)S(1)} %get-tuple-element.25), channel_id=1, source_target_pairs={{0,6},{1,25},{2,0},{3,27},{4,2},{5,29},{6,4},{7,31},{8,14},{9,1},{... | collective-permute-start | bytes 1572872 | tf_op jit(solution)/shard_map/ppermute | solution.py:265
  53.5 14.0 %collective-permute-start.16 = (f32[4,1,32,512]{3,2,0,1:T(8,128)S(1)}, f32[4,1,32,512]{3,2,0,1:T(8,128)S(1)}, u32[]{:S(2)}, u32[]{:S(2)}) collective-permute-start(f32[4,1,32,512]{3,2,0,1:T(8,128)S(1)} %get-tuple-element.29), channel_id=1, source_target_pairs={{0,2},{1,9},{2,4},{3,11},{4,6},{5,13},{6,0},{7,15},{8,10},{9,17},{... | collective-permute-start | bytes 786440 | tf_op jit(solution)/shard_map/ppermute | solution.py:265
  54.0 16.5 %collective-permute-start.17 = (f32[4,1,32,512]{3,2,0,1:T(8,128)S(1)}, f32[4,1,32,512]{3,2,0,1:T(8,128)S(1)}, u32[]{:S(2)}, u32[]{:S(2)}) collective-permute-start(f32[4,1,32,512]{3,2,0,1:T(8,128)S(1)} %get-tuple-element.27), channel_id=1, source_target_pairs={{0,4},{1,17},{2,6},{3,19},{4,0},{5,21},{6,2},{7,23},{8,12},{9,25},... | collective-permute-start | bytes 786440 | tf_op jit(solution)/shard_map/ppermute | solution.py:265
  59.0 11.9 %collective-permute-start.18 = (f32[4,1,32,512]{3,2,1,0:T(8,128)S(1)}, f32[4,1,32,512]{3,2,1,0:T(8,128)S(1)}, u32[]{:S(2)}, u32[]{:S(2)}) collective-permute-start(f32[4,1,32,512]{3,2,1,0:T(8,128)S(1)} %get-tuple-element.28), channel_id=1, source_target_pairs={{0,6},{1,25},{2,0},{3,27},{4,2},{5,29},{6,4},{7,31},{8,14},{9,1},{... | collective-permute-start | bytes 786440 | tf_op jit(solution)/shard_map/ppermute | solution.py:265
  71.2 6.8 %collective-permute-start.19 = (f32[4,32,512]{2,1,0:T(8,128)S(1)}, f32[4,32,512]{2,1,0:T(8,128)S(1)}, u32[]{:S(2)}, u32[]{:S(2)}) collective-permute-start(f32[4,32,512]{2,1,0:T(8,128)S(1)} %get-tuple-element.38), channel_id=1, source_target_pairs={{0,8},{1,3},{2,10},{3,5},{4,12},{5,7},{6,14},{7,1},{8,16},{9,11},{... | collective-permute-start | bytes 786440 | tf_op jit(solution)/shard_map/ppermute | solution.py:265
  72.1 9.4 %collective-permute-start.20 = (f32[4,32,512]{2,1,0:T(8,128)S(1)}, f32[4,32,512]{2,1,0:T(8,128)S(1)}, u32[]{:S(2)}, u32[]{:S(2)}) collective-permute-start(f32[4,32,512]{2,1,0:T(8,128)S(1)} %get-tuple-element.36), channel_id=1, source_target_pairs={{0,16},{1,5},{2,18},{3,7},{4,20},{5,1},{6,22},{7,3},{8,24},{9,13},... | collective-permute-start | bytes 786440 | tf_op jit(solution)/shard_map/ppermute | solution.py:265
  74.7 6.9 %collective-permute-start.21 = (f32[4,32,512]{2,1,0:T(8,128)S(1)}, f32[4,32,512]{2,1,0:T(8,128)S(1)}, u32[]{:S(2)}, u32[]{:S(2)}) collective-permute-start(f32[4,32,512]{2,1,0:T(8,128)S(1)} %get-tuple-element.37), channel_id=1, source_target_pairs={{0,24},{1,7},{2,26},{3,1},{4,28},{5,3},{6,30},{7,5},{8,0},{9,15},{... | collective-permute-start | bytes 786440 | tf_op jit(solution)/shard_map/ppermute | solution.py:265
  81.6 8.3 %collective-permute-start.22 = (f32[4,32,256]{2,1,0:T(8,128)S(1)}, f32[4,32,256]{2,1,0:T(8,128)S(1)}, u32[]{:S(2)}, u32[]{:S(2)}) collective-permute-start(f32[4,32,256]{2,1,0:T(8,128)S(1)} %slice.161), channel_id=1, source_target_pairs={{0,32},{1,33},{2,34},{3,35},{4,36},{5,37},{6,38},{7,39},{8,40},{9,... | collective-permute-start | bytes 393224 | tf_op jit(solution)/shard_map/ppermute | solution.py:265
  91.3 37.4 %copy-start.2 = (f32[1024]{0:T(1024)S(1)}, f32[1024]{0:T(1024)}, u32[]{:S(2)}) copy-start(f32[1024]{0:T(1024)} %param.8) | copy-start | bytes 12292
  91.3 38.8 %copy-start.3 = (f32[6]{0:T(128)S(1)}, f32[6]{0:T(128)}, u32[]{:S(2)}) copy-start(f32[6]{0:T(128)} %param.9) | copy-start | bytes 76
  91.4 6.5 %collective-permute-start.23 = (f32[32,16,128]{2,1,0:T(8,128)S(1)}, f32[32,16,128]{2,1,0:T(8,128)S(1)}, u32[]{:S(2)}, u32[]{:S(2)}) collective-permute-start(f32[32,16,128]{2,1,0:T(8,128)S(1)} %get-tuple-element.35), channel_id=1, source_target_pairs={{0,2},{1,9},{2,4},{3,11},{4,6},{5,13},{6,0},{7,15},{8,10},{9,17},{... | collective-permute-start | bytes 786440 | tf_op jit(solution)/shard_map/ppermute | solution.py:265
  92.8 8.3 %collective-permute-start.24 = (f32[32,16,128]{2,1,0:T(8,128)S(1)}, f32[32,16,128]{2,1,0:T(8,128)S(1)}, u32[]{:S(2)}, u32[]{:S(2)}) collective-permute-start(f32[32,16,128]{2,1,0:T(8,128)S(1)} %get-tuple-element.33), channel_id=1, source_target_pairs={{0,4},{1,17},{2,6},{3,19},{4,0},{5,21},{6,2},{7,23},{8,12},{9,25},... | collective-permute-start | bytes 786440 | tf_op jit(solution)/shard_map/ppermute | solution.py:265
  94.5 7.0 %collective-permute-start.25 = (f32[32,16,128]{2,1,0:T(8,128)S(1)}, f32[32,16,128]{2,1,0:T(8,128)S(1)}, u32[]{:S(2)}, u32[]{:S(2)}) collective-permute-start(f32[32,16,128]{2,1,0:T(8,128)S(1)} %get-tuple-element.34), channel_id=1, source_target_pairs={{0,6},{1,25},{2,0},{3,27},{4,2},{5,29},{6,4},{7,31},{8,14},{9,1},{... | collective-permute-start | bytes 786440 | tf_op jit(solution)/shard_map/ppermute | solution.py:265
  122.3 6.4 %collective-permute-start.26 = (f32[4,16,128]{2,1,0:T(8,128)S(1)}, f32[4,16,128]{2,1,0:T(8,128)S(1)}, u32[]{:S(2)}, u32[]{:S(2)}) collective-permute-start(f32[4,16,128]{2,1,0:T(8,128)S(1)} %reduce_sum.9.own), channel_id=1, source_target_pairs={{0,1},{1,0},{2,3},{3,2},{4,5},{5,4},{6,7},{7,6},{8,9},{9,8},{10,11... | collective-permute-start | bytes 98312 | tf_op jit(solution)/shard_map/ppermute | solution.py:265

commit v5 on v4

--- a/solution.py
+++ b/solution.py
@@ -161,10 +161,8 @@
     width = cost.shape[1]
     for at in range(0, width, step):
         full[at : at + step, :] = factor * dot3(left, halves(cost[:, at : at + step])).T
-    full[width:, :] = jnp.zeros((full.shape[0] - width, full.shape[1]), jnp.float32)
     chips = NG * NH * NY * NX
     rows = width // chips
-    pad = out_ref.shape[2]
     for cc in range(NC):
 
         @pl.when(c == cc)
@@ -172,23 +170,23 @@
             for o in range(chips):
                 gh, yy, xx = o // (NY * NX), (o // NX) % NY, o % NX
                 aa, bb = (xx, yy) if cc == 0 else (yy, xx)
-                out_ref[lax.rem(aa - a + 4, 4), gh * 4 + bb] = full[o * rows : o * rows + pad, :]
+                at = (gh * 4 + bb) * rows
+                out_ref[lax.rem(aa - a + 4, 4), at : at + rows, :] = full[o * rows : (o + 1) * rows, :]
 
 
 def grad(place, pieces, blocks, factor):
     _, run, width = pieces[0].shape
     rows = NC * 4 * run
     cols = blocks.shape[0] * blocks.shape[1]
-    pad = -(-width // (NG * NH * NY * NX) // 8) * 8
     return pl.pallas_call(
         lambda place, *refs: grad_kernel(place, *refs, factor=factor),
         in_specs=[SMEM] + [VMEM] * 5,
         out_specs=VMEM,
-        out_shape=jax.ShapeDtypeStruct((4, NG * NH * 4, pad, cols), jnp.float32),
+        out_shape=jax.ShapeDtypeStruct((4, width // 4, cols), jnp.float32),
         scratch_shapes=[
             pltpu.VMEM((rows, width), jnp.float32),
             pltpu.VMEM((cols, rows), jnp.float32),
-            pltpu.VMEM((width + 8, cols), jnp.float32),
+            pltpu.VMEM((width, cols), jnp.float32),
         ],
         compiler_params=params(),
         cost_estimate=COST,
@@ -291,6 +289,7 @@
 
     partial = grad(place, [both] + costs, blocks, factor)
     partial = partial[0] + sum(wide(partial[d], row_pairs(d)) for d in (1, 2, 3))
+    partial = partial.reshape(NG * NH * 4, -1, partial.shape[-1])
     parts = lax.all_to_all(partial, ("grp", "wide"), 0, 0, axis_index_groups=GATHER_GROUPS, tiled=True)
     summed = parts.reshape((NG * NH, 4) + parts.shape[1:]).sum(axis=0)
     gradient, log_total = arrange(place, summed, wide(summed, CORE_SWAP), potential_col[None, :], row_mass.shape[0])

time: 131 us -> 129 us (0.985)
  waiting for transfers between devices: 44.7 us -> 43 us
    ppermute x24, waiting for transfers between devices: 32.9 us -> 31.2 us  [wide(): return lax.ppermute(v, 'wide', pairs)]
where the time goes in v5:
time: 129 us
  starting transfers between devices  43.9 us (34%)
  waiting for transfers between devices  43 us (33%)
  blocking collectives  20.7 us (16%)
  Pallas kernels  15.2 us (12%)
  other arithmetic  3.17 us (2%)
  local copies, waits for them, and re-layouts  2.41 us (2%)
    ppermute x24, starting transfers between devices, wide(): return lax.ppermute(v, 'wide', pairs)  41 us
    ppermute x24, waiting for transfers between devices, wide(): return lax.ppermute(v, 'wide', pairs)  31.2 us
    all_to_all x1, blocking collectives, body(): lax.all_to_all(partial, ('grp', 'wide'), 0, 0, axis_index_groups=GATHER_G...  20.7 us
    pallas_call x3, Pallas kernels, carry(): pl.pallas_call(carry_kernel, in_specs=[SMEM, VMEM, VMEM] + [VMEM] * len(b...  11.5 us
    ppermute x1, waiting for transfers between devices, body(): far = lax.ppermute(cost_target, 'grp', [(i, i ^ 2) for i in range(NG)])  11.1 us
  transfers between devices with their start and end apart: 27, of which 16 were waited for; matrix products, arithmetic and copies ran while one was open for 2% of the time, Pallas kernels for 10%

profile of v5, /device:TPU:1, one launch (start us, length us, event | category | flops | bytes accessed | tf_op | source)
XLA Modules:
  0.0 129.2 jit_solution(12151880305223000310)
XLA Ops:
  0.6 3.3 %collective-permute-start = (f32[32,1536]{1,0:T(8,128)}, f32[32,1536]{1,0:T(8,128)S(1)}, u32[]{:S(2)}, u32[]{:S(2)}) collective-permute-start(f32[32,1536]{1,0:T(8,128)} %param.6), channel_id=1, source_target_pairs={{0,1},{1,0},{2,3},{3,2},{4,5},{5,4},{6,7},{7,6},{8,9},{9,8},{10,11... | collective-permute-start | bytes 589832 | tf_op jit(solution)/shard_map/ppermute | solution.py:263
  4.0 1.3 collective-permute-start.5
  5.2 1.6 %collective-permute-start.6 = (f32[512,256]{1,0:T(8,128)}, f32[512,256]{1,0:T(8,128)S(1)}, u32[]{:S(2)}, u32[]{:S(2)}) collective-permute-start(f32[512,256]{1,0:T(8,128)} %refs_0_.1), channel_id=1, source_target_pairs={{0,64},{64,0},{128,192},{192,128},{1,65},{65,1},{129,193},{193,129... | collective-permute-start | bytes 1572872 | tf_op jit(solution)/shard_map/ppermute | solution.py:278
  6.9 1.0 pad_maximum_fusion.1.refs_0_
  7.8 1.3 collective-permute-start.1
  9.1 2.5 %collective-permute-start.2 = (f32[2,32,1536]{2,1,0:T(8,128)S(1)}, f32[2,32,1536]{2,1,0:T(8,128)S(1)}, u32[]{:S(2)}, u32[]{:S(2)}) collective-permute-start(f32[2,32,1536]{2,1,0:T(8,128)S(1)} %pad_maximum_fusion.1.refs_0_), channel_id=1, source_target_pairs={{0,16},{1,5},{2,18},{3,7},{4,20},{5,1},{6,22},{7,3},{8,24},{9,13},... | collective-permute-start | bytes 1179656 | tf_op jit(solution)/shard_map/ppermute | solution.py:263
  11.6 1.2 collective-permute-start.3
  12.7 0.1 stack.32.place
  12.8 2.2 %copy-done = f32[2048,512]{1,0:T(8,128)S(1)} copy-done((f32[2048,512]{1,0:T(8,128)S(1)}, f32[2048,512]{1,0:T(8,128)}, u32[]{:S(2)}) %copy-start) | copy-done | bytes 4194328
  15.0 1.0 split.1
  16.0 2.9 %carry.3 = (f32[4,4,1,32,512]{4,3,2,1,0:T(8,128)S(1)}, f32[4,4,1,32,512]{4,3,2,1,0:T(8,128)S(1)}) custom-call(s32[5]{0:T(128)S(1)} %stack.32.place, bf16[4,512,512]{2,1,0:T(8,128)(2,1)S(1)} %get-tuple-element.13.hi_ref, bf16[4,512,512]{2,1,0:T(8,128)(2,1)S(1)} %get-tuple-element.14.lo_ref, f32[512,256]{1,0:T(8,128)S(1)} %copy-done.1), custom_call_target="tpu_custom_call" | custom-call | flops 1000 | bytes 1000 | tf_op jit(solution)/shard_map/carry/pallas_call | solution.py:131
  19.0 11.1 %collective-permute-done.5.refs_1_ = f32[512,256]{1,0:T(8,128)} collective-permute-done((f32[512,256]{1,0:T(8,128)}, f32[512,256]{1,0:T(8,128)}, u32[]{:S(2)}, u32[]{:S(2)}) %collective-permute-start.5) | collective-permute-done | bytes 524320 | tf_op jit(solution)/shard_map/ppermute | solution.py:279
  30.1 0.8 collective-permute-start.4
  30.9 2.2 %collective-permute-done.4 = f32[4,4,1,32,512]{4,3,1,2,0:T(8,128)S(1)} collective-permute-done((f32[4,4,1,32,512]{4,3,1,2,0:T(8,128)S(1)}, f32[4,4,1,32,512]{4,3,1,2,0:T(8,128)S(1)}, u32[]{:S(2)}, u32[]{:S(2)}) %collective-permute-start.4) | collective-permute-done | bytes 1048608 | tf_op jit(solution)/shard_map/ppermute | solution.py:263
  33.2 0.1 broadcast_add_fusion
  33.3 0.1 fusion.13
  33.5 0.2 collective-permute-start.7
  33.7 2.6 %collective-permute-start.8 = (f32[4,1,32,512]{3,2,0,1:T(8,128)S(1)}, f32[4,1,32,512]{3,2,0,1:T(8,128)S(1)}, u32[]{:S(2)}, u32[]{:S(2)}) collective-permute-start(f32[4,1,32,512]{3,2,0,1:T(8,128)S(1)} %get-tuple-element.30), channel_id=1, source_target_pairs={{0,4},{1,17},{2,6},{3,19},{4,0},{5,21},{6,2},{7,23},{8,12},{9,25},... | collective-permute-start | bytes 786440 | tf_op jit(solution)/shard_map/ppermute | solution.py:263
  36.3 1.1 collective-permute-start.9
  37.4 5.1 %carry.4 = (f32[4,4,2,32,512]{4,3,2,1,0:T(8,128)S(1)}, f32[4,4,2,32,512]{4,3,2,1,0:T(8,128)S(1)}) custom-call(s32[5]{0:T(128)S(1)} %stack.32.place, bf16[4,512,512]{2,1,0:T(8,128)(2,1)S(1)} %get-tuple-element.13.hi_ref, bf16[4,512,512]{2,1,0:T(8,128)(2,1)S(1)} %get-tuple-element.14.lo_ref, f32[512,256]{1,0:T(8,128)S(1)} %collective-permute-done.6.refs_2_.refs_0_, ...), custom_call_target="tpu_custom_call" | custom-call | flops 99999997952 | bytes 1000 | tf_op jit(solution)/shard_map/carry/pallas_call | solution.py:131
  42.5 1.3 %collective-permute-start.10 = (f32[4,4,2,32,512]{4,3,2,1,0:T(8,128)S(1)}, f32[4,4,2,32,512]{4,3,2,1,0:T(8,128)S(1)}, u32[]{:S(2)}, u32[]{:S(2)}) collective-permute-start(f32[4,4,2,32,512]{4,3,2,1,0:T(8,128)S(1)} %get-tuple-element.18), channel_id=1, source_target_pairs={{0,1},{1,0},{2,3},{3,2},{4,5},{5,4},{6,7},{7,6},{8,9},{9,8},{10,11... | collective-permute-start | bytes 6291464 | tf_op jit(solution)/shard_map/ppermute | solution.py:263
  43.8 0.1 fusion.16
  44.0 0.8 collective-permute-done.14.refs_0_
  44.7 3.5 %carry.5 = (f32[4,4,1,32,512]{4,3,2,1,0:T(8,128)S(1)}, f32[4,4,1,32,512]{4,3,2,1,0:T(8,128)S(1)}) custom-call(s32[5]{0:T(128)S(1)} %stack.32.place, bf16[4,512,512]{2,1,0:T(8,128)(2,1)S(1)} %get-tuple-element.13.hi_ref, bf16[4,512,512]{2,1,0:T(8,128)(2,1)S(1)} %get-tuple-element.14.lo_ref, f32[512,256]{1,0:T(8,128)} %collective-permute-done.14.refs_0_), custom_call_target="tpu_custom_call" | custom-call | flops 99999997952 | bytes 1000 | tf_op jit(solution)/shard_map/carry/pallas_call | solution.py:131
  48.2 0.9 collective-permute-start.15
  49.1 0.3 fusion.1
  49.4 0.2 collective-permute-start.11
  49.7 2.6 %collective-permute-start.12 = (f32[4,2,32,512]{3,2,1,0:T(8,128)S(1)}, f32[4,2,32,512]{3,2,1,0:T(8,128)S(1)}, u32[]{:S(2)}, u32[]{:S(2)}) collective-permute-start(f32[4,2,32,512]{3,2,1,0:T(8,128)S(1)} %get-tuple-element.24), channel_id=1, source_target_pairs={{0,4},{1,17},{2,6},{3,19},{4,0},{5,21},{6,2},{7,23},{8,12},{9,25},... | collective-permute-start | bytes 1572872 | tf_op jit(solution)/shard_map/ppermute | solution.py:263
  52.3 1.1 collective-permute-start.13
  53.4 0.1 fusion.7
  53.5 0.5 collective-permute-start.16
  54.0 0.9 collective-permute-start.17
  54.9 4.2 %collective-permute-done.11 = f32[4,2,32,512]{3,2,1,0:T(8,128)S(1)} collective-permute-done((f32[4,2,32,512]{3,2,1,0:T(8,128)S(1)}, f32[4,2,32,512]{3,2,1,0:T(8,128)S(1)}, u32[]{:S(2)}, u32[]{:S(2)}) %collective-permute-start.11) | collective-permute-done | bytes 524320 | tf_op jit(solution)/shard_map/ppermute | solution.py:263
  59.0 0.4 collective-permute-start.18
  59.4 5.4 %collective-permute-done.12 = f32[4,2,32,512]{3,2,1,0:T(8,128)S(1)} collective-permute-done((f32[4,2,32,512]{3,2,1,0:T(8,128)S(1)}, f32[4,2,32,512]{3,2,1,0:T(8,128)S(1)}, u32[]{:S(2)}, u32[]{:S(2)}) %collective-permute-start.12) | collective-permute-done | bytes 524320 | tf_op jit(solution)/shard_map/ppermute | solution.py:263
  64.8 0.5 collective-permute-done.13
  65.3 0.3 fusion.4.refs_0_
  65.6 1.9 %collective-permute-done.16 = f32[4,1,32,512]{3,2,0,1:T(8,128)S(1)} collective-permute-done((f32[4,1,32,512]{3,2,0,1:T(8,128)S(1)}, f32[4,1,32,512]{3,2,0,1:T(8,128)S(1)}, u32[]{:S(2)}, u32[]{:S(2)}) %collective-permute-start.16) | collective-permute-done | bytes 262176 | tf_op jit(solution)/shard_map/ppermute | solution.py:263
  67.5 3.0 %collective-permute-done.17 = f32[4,1,32,512]{3,2,0,1:T(8,128)S(1)} collective-permute-done((f32[4,1,32,512]{3,2,0,1:T(8,128)S(1)}, f32[4,1,32,512]{3,2,0,1:T(8,128)S(1)}, u32[]{:S(2)}, u32[]{:S(2)}) %collective-permute-start.17) | collective-permute-done | bytes 262176 | tf_op jit(solution)/shard_map/ppermute | solution.py:263
  70.4 0.5 collective-permute-done.18
  70.9 0.1 fusion.11
  71.1 0.1 pad_maximum_fusion
  71.2 0.1 slice_bitcast_fusion.1
  71.2 0.9 collective-permute-start.19
  72.1 2.6 %collective-permute-start.20 = (f32[4,32,512]{2,1,0:T(8,128)S(1)}, f32[4,32,512]{2,1,0:T(8,128)S(1)}, u32[]{:S(2)}, u32[]{:S(2)}) collective-permute-start(f32[4,32,512]{2,1,0:T(8,128)S(1)} %get-tuple-element.33), channel_id=1, source_target_pairs={{0,16},{1,5},{2,18},{3,7},{4,20},{5,1},{6,22},{7,3},{8,24},{9,13},... | collective-permute-start | bytes 786440 | tf_op jit(solution)/shard_map/ppermute | solution.py:263
  74.7 0.7 collective-permute-start.21
  75.3 2.7 %collective-permute-done.19 = f32[4,32,512]{2,1,0:T(8,128)S(1)} collective-permute-done((f32[4,32,512]{2,1,0:T(8,128)S(1)}, f32[4,32,512]{2,1,0:T(8,128)S(1)}, u32[]{:S(2)}, u32[]{:S(2)}) %collective-permute-start.19) | collective-permute-done | bytes 262176 | tf_op jit(solution)/shard_map/ppermute | solution.py:263
  78.1 3.5 %collective-permute-done.20 = f32[4,32,512]{2,1,0:T(8,128)S(1)} collective-permute-done((f32[4,32,512]{2,1,0:T(8,128)S(1)}, f32[4,32,512]{2,1,0:T(8,128)S(1)}, u32[]{:S(2)}, u32[]{:S(2)}) %collective-permute-start.20) | collective-permute-done | bytes 262176 | tf_op jit(solution)/shard_map/ppermute | solution.py:263
  81.5 0.1 fusion.5
  81.6 5.8 %collective-permute-start.22 = (f32[4,32,256]{2,1,0:T(8,128)S(1)}, f32[4,32,256]{2,1,0:T(8,128)S(1)}, u32[]{:S(2)}, u32[]{:S(2)}) collective-permute-start(f32[4,32,256]{2,1,0:T(8,128)S(1)} %slice.161), channel_id=1, source_target_pairs={{0,32},{1,33},{2,34},{3,35},{4,36},{5,37},{6,38},{7,39},{8,40},{9,... | collective-permute-start | bytes 393224 | tf_op jit(solution)/shard_map/ppermute | solution.py:263
  87.4 2.5 %collective-permute-done.22 = f32[4,32,256]{2,1,0:T(8,128)S(1)} collective-permute-done((f32[4,32,256]{2,1,0:T(8,128)S(1)}, f32[4,32,256]{2,1,0:T(8,128)S(1)}, u32[]{:S(2)}, u32[]{:S(2)}) %collective-permute-start.22) | collective-permute-done | bytes 131104 | tf_op jit(solution)/shard_map/ppermute | solution.py:263
  89.9 1.3 %grad.1 = f32[4,384,128]{2,1,0:T(8,128)S(1)} custom-call(s32[5]{0:T(128)S(1)} %stack.32.place, f32[2,32,1536]{2,1,0:T(8,128)S(1)} %pad_maximum_fusion.1.refs_0_, f32[2,32,1536]{2,1,0:T(8,128)S(1)} %collective-permute-done.1.refs_3_.refs_1_, f32[2,32,1536]{2,1,0:T(8,128)S(1)} %collective-permute-done.2.refs_4_.refs_2_, ...), custom_call_target="tpu_custom_call" | custom-call | flops 1000 | bytes 1000 | tf_op jit(solution)/shard_map/grad/pallas_call | solution.py:181
  91.3 1.4 %collective-permute-start.23 = (f32[384,128]{1,0:T(8,128)S(1)}, f32[384,128]{1,0:T(8,128)S(1)}, u32[]{:S(2)}, u32[]{:S(2)}) collective-permute-start(f32[384,128]{1,0:T(8,128)S(1)} %get-tuple-element.38), channel_id=1, source_target_pairs={{0,2},{1,9},{2,4},{3,11},{4,6},{5,13},{6,0},{7,15},{8,10},{9,17},{... | collective-permute-start | bytes 589832 | tf_op jit(solution)/shard_map/ppermute | solution.py:263
  92.8 1.8 %collective-permute-start.24 = (f32[384,128]{1,0:T(8,128)S(1)}, f32[384,128]{1,0:T(8,128)S(1)}, u32[]{:S(2)}, u32[]{:S(2)}) collective-permute-start(f32[384,128]{1,0:T(8,128)S(1)} %get-tuple-element.36), channel_id=1, source_target_pairs={{0,4},{1,17},{2,6},{3,19},{4,0},{5,21},{6,2},{7,23},{8,12},{9,25},... | collective-permute-start | bytes 589832 | tf_op jit(solution)/shard_map/ppermute | solution.py:263
  94.5 1.3 collective-permute-start.25
  95.8 1.4 %collective-permute-done.23 = f32[384,128]{1,0:T(8,128)S(1)} collective-permute-done((f32[384,128]{1,0:T(8,128)S(1)}, f32[384,128]{1,0:T(8,128)S(1)}, u32[]{:S(2)}, u32[]{:S(2)}) %collective-permute-start.23) | collective-permute-done | bytes 196640 | tf_op jit(solution)/shard_map/ppermute | solution.py:263
  97.2 2.5 %collective-permute-done.24 = f32[384,128]{1,0:T(8,128)S(1)} collective-permute-done((f32[384,128]{1,0:T(8,128)S(1)}, f32[384,128]{1,0:T(8,128)S(1)}, u32[]{:S(2)}, u32[]{:S(2)}) %collective-permute-start.24) | collective-permute-done | bytes 196640 | tf_op jit(solution)/shard_map/ppermute | solution.py:263
  99.7 0.2 collective-permute-done.25
  99.9 20.7 %all_to_all.5 = f32[32,12,128]{2,1,0:T(8,128)S(1)} all-to-all(f32[32,12,128]{2,1,0:T(8,128)S(1)} %reshape.194), channel_id=1, replica_groups={{0,8,16,24,32,40,48,56,64,72,80,88,96,104,112,120,128,136,144,152,160,1..., dimensions={0} | all-to-all | bytes 393216 | tf_op jit(solution)/shard_map/all_to_all | solution.py:293
  120.6 5.8 %collective-permute-start.26 = (f32[4,12,128]{2,1,0:T(8,128)S(1)}, f32[4,12,128]{2,1,0:T(8,128)S(1)}, u32[]{:S(2)}, u32[]{:S(2)}) collective-permute-start(f32[4,12,128]{2,1,0:T(8,128)S(1)} %reduce_sum.9.own), channel_id=1, source_target_pairs={{0,1},{1,0},{2,3},{3,2},{4,5},{5,4},{6,7},{7,6},{8,9},{9,8},{10,11... | collective-permute-start | bytes 73736 | tf_op jit(solution)/shard_map/ppermute | solution.py:263
  126.4 0.9 collective-permute-done.26.got
  127.3 1.3 arrange.1
  128.5 0.1 multiply_reduce_fusion
  128.6 0.5 multiply_subtract_fusion
  (27 shorter events, 0.2 us)
Async XLA Ops:
  0.6 6.2 %collective-permute-start = (f32[32,1536]{1,0:T(8,128)}, f32[32,1536]{1,0:T(8,128)S(1)}, u32[]{:S(2)}, u32[]{:S(2)}) collective-permute-start(f32[32,1536]{1,0:T(8,128)} %param.6), channel_id=1, source_target_pairs={{0,1},{1,0},{2,3},{3,2},{4,5},{5,4},{6,7},{7,6},{8,9},{9,8},{10,11... | collective-permute-start | bytes 589832 | tf_op jit(solution)/shard_map/ppermute | solution.py:263
  4.0 26.1 %collective-permute-start.5 = (f32[512,256]{1,0:T(8,128)}, f32[512,256]{1,0:T(8,128)}, u32[]{:S(2)}, u32[]{:S(2)}) collective-permute-start(f32[512,256]{1,0:T(8,128)} %refs_0_.1), channel_id=1, source_target_pairs={{0,128},{64,192},{128,0},{192,64},{1,129},{65,193},{129,1},{193,65... | collective-permute-start | bytes 1572872 | tf_op jit(solution)/shard_map/ppermute | solution.py:279
  5.2 25.6 %collective-permute-start.6 = (f32[512,256]{1,0:T(8,128)}, f32[512,256]{1,0:T(8,128)S(1)}, u32[]{:S(2)}, u32[]{:S(2)}) collective-permute-start(f32[512,256]{1,0:T(8,128)} %refs_0_.1), channel_id=1, source_target_pairs={{0,64},{64,0},{128,192},{192,128},{1,65},{65,1},{129,193},{193,129... | collective-permute-start | bytes 1572872 | tf_op jit(solution)/shard_map/ppermute | solution.py:278
  7.8 23.1 %collective-permute-start.1 = (f32[2,32,1536]{2,1,0:T(8,128)S(1)}, f32[2,32,1536]{2,1,0:T(8,128)S(1)}, u32[]{:S(2)}, u32[]{:S(2)}) collective-permute-start(f32[2,32,1536]{2,1,0:T(8,128)S(1)} %pad_maximum_fusion.1.refs_0_), channel_id=1, source_target_pairs={{0,8},{1,3},{2,10},{3,5},{4,12},{5,7},{6,14},{7,1},{8,16},{9,11},{... | collective-permute-start | bytes 1179656 | tf_op jit(solution)/shard_map/ppermute | solution.py:263
  9.1 21.8 %collective-permute-start.2 = (f32[2,32,1536]{2,1,0:T(8,128)S(1)}, f32[2,32,1536]{2,1,0:T(8,128)S(1)}, u32[]{:S(2)}, u32[]{:S(2)}) collective-permute-start(f32[2,32,1536]{2,1,0:T(8,128)S(1)} %pad_maximum_fusion.1.refs_0_), channel_id=1, source_target_pairs={{0,16},{1,5},{2,18},{3,7},{4,20},{5,1},{6,22},{7,3},{8,24},{9,13},... | collective-permute-start | bytes 1179656 | tf_op jit(solution)/shard_map/ppermute | solution.py:263
  11.6 19.3 %collective-permute-start.3 = (f32[2,32,1536]{2,1,0:T(8,128)S(1)}, f32[2,32,1536]{2,1,0:T(8,128)S(1)}, u32[]{:S(2)}, u32[]{:S(2)}) collective-permute-start(f32[2,32,1536]{2,1,0:T(8,128)S(1)} %pad_maximum_fusion.1.refs_0_), channel_id=1, source_target_pairs={{0,24},{1,7},{2,26},{3,1},{4,28},{5,3},{6,30},{7,5},{8,0},{9,15},{... | collective-permute-start | bytes 1179656 | tf_op jit(solution)/shard_map/ppermute | solution.py:263
  12.8 2.2 %copy-start = (f32[2048,512]{1,0:T(8,128)S(1)}, f32[2048,512]{1,0:T(8,128)}, u32[]{:S(2)}) copy-start(f32[2048,512]{1,0:T(8,128)} %param.5) | copy-start | bytes 12582916
  15.0 1.0 copy-start.1
  30.1 3.1 %collective-permute-start.4 = (f32[4,4,1,32,512]{4,3,1,2,0:T(8,128)S(1)}, f32[4,4,1,32,512]{4,3,1,2,0:T(8,128)S(1)}, u32[]{:S(2)}, u32[]{:S(2)}) collective-permute-start(f32[4,4,1,32,512]{4,3,1,2,0:T(8,128)S(1)} %bitcast.89), channel_id=1, source_target_pairs={{0,1},{1,0},{2,3},{3,2},{4,5},{5,4},{6,7},{7,6},{8,9},{9,8},{10,11... | collective-permute-start | bytes 3145736 | tf_op jit(solution)/shard_map/ppermute | solution.py:263
  30.9 13.9 %collective-permute-start.14 = (f32[512,256]{1,0:T(8,128)}, f32[512,256]{1,0:T(8,128)}, u32[]{:S(2)}, u32[]{:S(2)}) collective-permute-start(f32[512,256]{1,0:T(8,128)} %collective-permute-done.5.refs_1_), channel_id=1, source_target_pairs={{0,64},{64,0},{128,192},{192,128},{1,65},{65,1},{129,193},{193,129... | collective-permute-start | bytes 1572872 | tf_op jit(solution)/shard_map/ppermute | solution.py:282
  33.5 10.4 %collective-permute-start.7 = (f32[4,1,32,512]{3,2,0,1:T(8,128)S(1)}, f32[4,1,32,512]{3,2,0,1:T(8,128)S(1)}, u32[]{:S(2)}, u32[]{:S(2)}) collective-permute-start(f32[4,1,32,512]{3,2,0,1:T(8,128)S(1)} %get-tuple-element.32), channel_id=1, source_target_pairs={{0,2},{1,9},{2,4},{3,11},{4,6},{5,13},{6,0},{7,15},{8,10},{9,17},{... | collective-permute-start | bytes 786440 | tf_op jit(solution)/shard_map/ppermute | solution.py:263
  33.7 10.1 %collective-permute-start.8 = (f32[4,1,32,512]{3,2,0,1:T(8,128)S(1)}, f32[4,1,32,512]{3,2,0,1:T(8,128)S(1)}, u32[]{:S(2)}, u32[]{:S(2)}) collective-permute-start(f32[4,1,32,512]{3,2,0,1:T(8,128)S(1)} %get-tuple-element.30), channel_id=1, source_target_pairs={{0,4},{1,17},{2,6},{3,19},{4,0},{5,21},{6,2},{7,23},{8,12},{9,25},... | collective-permute-start | bytes 786440 | tf_op jit(solution)/shard_map/ppermute | solution.py:263
  36.3 7.5 %collective-permute-start.9 = (f32[4,1,32,512]{3,2,1,0:T(8,128)S(1)}, f32[4,1,32,512]{3,2,1,0:T(8,128)S(1)}, u32[]{:S(2)}, u32[]{:S(2)}) collective-permute-start(f32[4,1,32,512]{3,2,1,0:T(8,128)S(1)} %get-tuple-element.31), channel_id=1, source_target_pairs={{0,6},{1,25},{2,0},{3,27},{4,2},{5,29},{6,4},{7,31},{8,14},{9,1},{... | collective-permute-start | bytes 786440 | tf_op jit(solution)/shard_map/ppermute | solution.py:263
  42.5 6.6 %collective-permute-start.10 = (f32[4,4,2,32,512]{4,3,2,1,0:T(8,128)S(1)}, f32[4,4,2,32,512]{4,3,2,1,0:T(8,128)S(1)}, u32[]{:S(2)}, u32[]{:S(2)}) collective-permute-start(f32[4,4,2,32,512]{4,3,2,1,0:T(8,128)S(1)} %get-tuple-element.18), channel_id=1, source_target_pairs={{0,1},{1,0},{2,3},{3,2},{4,5},{5,4},{6,7},{7,6},{8,9},{9,8},{10,11... | collective-permute-start | bytes 6291464 | tf_op jit(solution)/shard_map/ppermute | solution.py:263
  48.2 5.2 %collective-permute-start.15 = (f32[4,4,1,32,512]{4,3,1,2,0:T(8,128)S(1)}, f32[4,4,1,32,512]{4,3,1,2,0:T(8,128)S(1)}, u32[]{:S(2)}, u32[]{:S(2)}) collective-permute-start(f32[4,4,1,32,512]{4,3,1,2,0:T(8,128)S(1)} %bitcast.88), channel_id=1, source_target_pairs={{0,1},{1,0},{2,3},{3,2},{4,5},{5,4},{6,7},{7,6},{8,9},{9,8},{10,11... | collective-permute-start | bytes 3145736 | tf_op jit(solution)/shard_map/ppermute | solution.py:263
  49.4 9.6 %collective-permute-start.11 = (f32[4,2,32,512]{3,2,1,0:T(8,128)S(1)}, f32[4,2,32,512]{3,2,1,0:T(8,128)S(1)}, u32[]{:S(2)}, u32[]{:S(2)}) collective-permute-start(f32[4,2,32,512]{3,2,1,0:T(8,128)S(1)} %get-tuple-element.26), channel_id=1, source_target_pairs={{0,2},{1,9},{2,4},{3,11},{4,6},{5,13},{6,0},{7,15},{8,10},{9,17},{... | collective-permute-start | bytes 1572872 | tf_op jit(solution)/shard_map/ppermute | solution.py:263
  49.7 15.1 %collective-permute-start.12 = (f32[4,2,32,512]{3,2,1,0:T(8,128)S(1)}, f32[4,2,32,512]{3,2,1,0:T(8,128)S(1)}, u32[]{:S(2)}, u32[]{:S(2)}) collective-permute-start(f32[4,2,32,512]{3,2,1,0:T(8,128)S(1)} %get-tuple-element.24), channel_id=1, source_target_pairs={{0,4},{1,17},{2,6},{3,19},{4,0},{5,21},{6,2},{7,23},{8,12},{9,25},... | collective-permute-start | bytes 1572872 | tf_op jit(solution)/shard_map/ppermute | solution.py:263
  52.3 13.0 %collective-permute-start.13 = (f32[4,2,32,512]{3,2,1,0:T(8,128)S(1)}, f32[4,2,32,512]{3,2,1,0:T(8,128)S(1)}, u32[]{:S(2)}, u32[]{:S(2)}) collective-permute-start(f32[4,2,32,512]{3,2,1,0:T(8,128)S(1)} %get-tuple-element.25), channel_id=1, source_target_pairs={{0,6},{1,25},{2,0},{3,27},{4,2},{5,29},{6,4},{7,31},{8,14},{9,1},{... | collective-permute-start | bytes 1572872 | tf_op jit(solution)/shard_map/ppermute | solution.py:263
  53.5 14.0 %collective-permute-start.16 = (f32[4,1,32,512]{3,2,0,1:T(8,128)S(1)}, f32[4,1,32,512]{3,2,0,1:T(8,128)S(1)}, u32[]{:S(2)}, u32[]{:S(2)}) collective-permute-start(f32[4,1,32,512]{3,2,0,1:T(8,128)S(1)} %get-tuple-element.29), channel_id=1, source_target_pairs={{0,2},{1,9},{2,4},{3,11},{4,6},{5,13},{6,0},{7,15},{8,10},{9,17},{... | collective-permute-start | bytes 786440 | tf_op jit(solution)/shard_map/ppermute | solution.py:263
  54.0 16.5 %collective-permute-start.17 = (f32[4,1,32,512]{3,2,0,1:T(8,128)S(1)}, f32[4,1,32,512]{3,2,0,1:T(8,128)S(1)}, u32[]{:S(2)}, u32[]{:S(2)}) collective-permute-start(f32[4,1,32,512]{3,2,0,1:T(8,128)S(1)} %get-tuple-element.27), channel_id=1, source_target_pairs={{0,4},{1,17},{2,6},{3,19},{4,0},{5,21},{6,2},{7,23},{8,12},{9,25},... | collective-permute-start | bytes 786440 | tf_op jit(solution)/shard_map/ppermute | solution.py:263
  59.0 11.9 %collective-permute-start.18 = (f32[4,1,32,512]{3,2,1,0:T(8,128)S(1)}, f32[4,1,32,512]{3,2,1,0:T(8,128)S(1)}, u32[]{:S(2)}, u32[]{:S(2)}) collective-permute-start(f32[4,1,32,512]{3,2,1,0:T(8,128)S(1)} %get-tuple-element.28), channel_id=1, source_target_pairs={{0,6},{1,25},{2,0},{3,27},{4,2},{5,29},{6,4},{7,31},{8,14},{9,1},{... | collective-permute-start | bytes 786440 | tf_op jit(solution)/shard_map/ppermute | solution.py:263
  71.2 6.8 %collective-permute-start.19 = (f32[4,32,512]{2,1,0:T(8,128)S(1)}, f32[4,32,512]{2,1,0:T(8,128)S(1)}, u32[]{:S(2)}, u32[]{:S(2)}) collective-permute-start(f32[4,32,512]{2,1,0:T(8,128)S(1)} %get-tuple-element.35), channel_id=1, source_target_pairs={{0,8},{1,3},{2,10},{3,5},{4,12},{5,7},{6,14},{7,1},{8,16},{9,11},{... | collective-permute-start | bytes 786440 | tf_op jit(solution)/shard_map/ppermute | solution.py:263
  72.1 9.4 %collective-permute-start.20 = (f32[4,32,512]{2,1,0:T(8,128)S(1)}, f32[4,32,512]{2,1,0:T(8,128)S(1)}, u32[]{:S(2)}, u32[]{:S(2)}) collective-permute-start(f32[4,32,512]{2,1,0:T(8,128)S(1)} %get-tuple-element.33), channel_id=1, source_target_pairs={{0,16},{1,5},{2,18},{3,7},{4,20},{5,1},{6,22},{7,3},{8,24},{9,13},... | collective-permute-start | bytes 786440 | tf_op jit(solution)/shard_map/ppermute | solution.py:263
  74.7 6.9 %collective-permute-start.21 = (f32[4,32,512]{2,1,0:T(8,128)S(1)}, f32[4,32,512]{2,1,0:T(8,128)S(1)}, u32[]{:S(2)}, u32[]{:S(2)}) collective-permute-start(f32[4,32,512]{2,1,0:T(8,128)S(1)} %get-tuple-element.34), channel_id=1, source_target_pairs={{0,24},{1,7},{2,26},{3,1},{4,28},{5,3},{6,30},{7,5},{8,0},{9,15},{... | collective-permute-start | bytes 786440 | tf_op jit(solution)/shard_map/ppermute | solution.py:263
  81.6 8.3 %collective-permute-start.22 = (f32[4,32,256]{2,1,0:T(8,128)S(1)}, f32[4,32,256]{2,1,0:T(8,128)S(1)}, u32[]{:S(2)}, u32[]{:S(2)}) collective-permute-start(f32[4,32,256]{2,1,0:T(8,128)S(1)} %slice.161), channel_id=1, source_target_pairs={{0,32},{1,33},{2,34},{3,35},{4,36},{5,37},{6,38},{7,39},{8,40},{9,... | collective-permute-start | bytes 393224 | tf_op jit(solution)/shard_map/ppermute | solution.py:263
  91.3 36.0 %copy-start.2 = (f32[1024]{0:T(1024)S(1)}, f32[1024]{0:T(1024)}, u32[]{:S(2)}) copy-start(f32[1024]{0:T(1024)} %param.8) | copy-start | bytes 12292
  91.3 37.3 %copy-start.3 = (f32[6]{0:T(128)S(1)}, f32[6]{0:T(128)}, u32[]{:S(2)}) copy-start(f32[6]{0:T(128)} %param.9) | copy-start | bytes 76
  91.3 5.8 %collective-permute-start.23 = (f32[384,128]{1,0:T(8,128)S(1)}, f32[384,128]{1,0:T(8,128)S(1)}, u32[]{:S(2)}, u32[]{:S(2)}) collective-permute-start(f32[384,128]{1,0:T(8,128)S(1)} %get-tuple-element.38), channel_id=1, source_target_pairs={{0,2},{1,9},{2,4},{3,11},{4,6},{5,13},{6,0},{7,15},{8,10},{9,17},{... | collective-permute-start | bytes 589832 | tf_op jit(solution)/shard_map/ppermute | solution.py:263
  92.8 6.9 %collective-permute-start.24 = (f32[384,128]{1,0:T(8,128)S(1)}, f32[384,128]{1,0:T(8,128)S(1)}, u32[]{:S(2)}, u32[]{:S(2)}) collective-permute-start(f32[384,128]{1,0:T(8,128)S(1)} %get-tuple-element.36), channel_id=1, source_target_pairs={{0,4},{1,17},{2,6},{3,19},{4,0},{5,21},{6,2},{7,23},{8,12},{9,25},... | collective-permute-start | bytes 589832 | tf_op jit(solution)/shard_map/ppermute | solution.py:263
  94.5 5.3 %collective-permute-start.25 = (f32[384,128]{1,0:T(8,128)S(1)}, f32[384,128]{1,0:T(8,128)S(1)}, u32[]{:S(2)}, u32[]{:S(2)}) collective-permute-start(f32[384,128]{1,0:T(8,128)S(1)} %get-tuple-element.37), channel_id=1, source_target_pairs={{0,6},{1,25},{2,0},{3,27},{4,2},{5,29},{6,4},{7,31},{8,14},{9,1},{... | collective-permute-start | bytes 589832 | tf_op jit(solution)/shard_map/ppermute | solution.py:263
  120.6 6.6 %collective-permute-start.26 = (f32[4,12,128]{2,1,0:T(8,128)S(1)}, f32[4,12,128]{2,1,0:T(8,128)S(1)}, u32[]{:S(2)}, u32[]{:S(2)}) collective-permute-start(f32[4,12,128]{2,1,0:T(8,128)S(1)} %reduce_sum.9.own), channel_id=1, source_target_pairs={{0,1},{1,0},{2,3},{3,2},{4,5},{5,4},{6,7},{7,6},{8,9},{9,8},{10,11... | collective-permute-start | bytes 73736 | tf_op jit(solution)/shard_map/ppermute | solution.py:263

commit v6 on v5

--- a/solution.py
+++ b/solution.py
@@ -268,10 +268,10 @@
 
     def along_rows(own, got):
         parts = [own[d] + got[d] for d in range(4)]
-        return parts[0] + sum(wide(parts[d], row_pairs(d)) for d in (1, 2, 3))
+        return parts[0] + sum(wide(parts[d], row_pairs(d)) for d in (2, 1, 3))
 
     def finish(total):
-        total = total[0] + sum(wide(total[d], column_pairs(d)) for d in (1, 2, 3))
+        total = total[0] + sum(wide(total[d], column_pairs(d)) for d in (2, 1, 3))
         rows = total.shape[-1] // NH
         return total[..., :rows] + wide(total[..., rows:], H_SWAP)
 
@@ -288,7 +288,7 @@
     blocks = finish(jnp.concatenate([total0, total1, total2], axis=1))
 
     partial = grad(place, [both] + costs, blocks, factor)
-    partial = partial[0] + sum(wide(partial[d], row_pairs(d)) for d in (1, 2, 3))
+    partial = partial[0] + sum(wide(partial[d], row_pairs(d)) for d in (2, 1, 3))
     partial = partial.reshape(NG * NH * 4, -1, partial.shape[-1])
     parts = lax.all_to_all(partial, ("grp", "wide"), 0, 0, axis_index_groups=GATHER_GROUPS, tiled=True)
     summed = parts.reshape((NG * NH, 4) + parts.shape[1:]).sum(axis=0)

time: 129 us -> 128 us (level)
  waiting for transfers between devices: 43 us -> 39.2 us
  starting transfers between devices: 43.9 us -> 46.6 us
    ppermute x24, waiting for transfers between devices: 31.2 us -> 27.9 us  [wide(): return lax.ppermute(v, 'wide', pairs)]
    ppermute x24, starting transfers between devices: 41 us -> 43.7 us  [wide(): return lax.ppermute(v, 'wide', pairs)]
  transfers between devices with their start and end apart: 27 -> 27, of which waited for: 16 -> 13; matrix products, arithmetic and copies ran while one was open for 2% -> 2% of each run, Pallas kernels for 10% -> 10%
where the time goes in v6:
time: 128 us
  starting transfers between devices  46.6 us (36%)
  waiting for transfers between devices  39.2 us (31%)
  blocking collectives  20.4 us (16%)
  Pallas kernels  15.2 us (12%)
  other arithmetic  3.17 us (2%)
  local copies, waits for them, and re-layouts  2.41 us (2%)
    ppermute x24, starting transfers between devices, wide(): return lax.ppermute(v, 'wide', pairs)  43.7 us
    ppermute x24, waiting for transfers between devices, wide(): return lax.ppermute(v, 'wide', pairs)  27.9 us
    all_to_all x1, blocking collectives, body(): lax.all_to_all(partial, ('grp', 'wide'), 0, 0, axis_index_groups=GATHER_G...  20.4 us
    pallas_call x3, Pallas kernels, carry(): pl.pallas_call(carry_kernel, in_specs=[SMEM, VMEM, VMEM] + [VMEM] * len(b...  11.5 us
    ppermute x1, waiting for transfers between devices, body(): far = lax.ppermute(cost_target, 'grp', [(i, i ^ 2) for i in range(NG)])  11.1 us
  transfers between devices with their start and end apart: 27, of which 13 were waited for; matrix products, arithmetic and copies ran while one was open for 2% of the time, Pallas kernels for 10%

profile of v6, /device:TPU:1, one launch (start us, length us, event | category | flops | bytes accessed | tf_op | source)
XLA Modules:
  0.0 127.8 jit_solution(7316195003315589711)
XLA Ops:
  0.6 3.3 %collective-permute-start = (f32[32,1536]{1,0:T(8,128)}, f32[32,1536]{1,0:T(8,128)S(1)}, u32[]{:S(2)}, u32[]{:S(2)}) collective-permute-start(f32[32,1536]{1,0:T(8,128)} %param.6), channel_id=1, source_target_pairs={{0,1},{1,0},{2,3},{3,2},{4,5},{5,4},{6,7},{7,6},{8,9},{9,8},{10,11... | collective-permute-start | bytes 589832 | tf_op jit(solution)/shard_map/ppermute | solution.py:263
  4.0 1.3 collective-permute-start.5
  5.2 1.6 %collective-permute-start.6 = (f32[512,256]{1,0:T(8,128)}, f32[512,256]{1,0:T(8,128)S(1)}, u32[]{:S(2)}, u32[]{:S(2)}) collective-permute-start(f32[512,256]{1,0:T(8,128)} %refs_0_.1), channel_id=1, source_target_pairs={{0,64},{64,0},{128,192},{192,128},{1,65},{65,1},{129,193},{193,129... | collective-permute-start | bytes 1572872 | tf_op jit(solution)/shard_map/ppermute | solution.py:278
  6.9 1.0 pad_maximum_fusion.1.refs_0_
  7.8 1.3 %collective-permute-start.1 = (f32[2,32,1536]{2,1,0:T(8,128)S(1)}, f32[2,32,1536]{2,1,0:T(8,128)S(1)}, u32[]{:S(2)}, u32[]{:S(2)}) collective-permute-start(f32[2,32,1536]{2,1,0:T(8,128)S(1)} %pad_maximum_fusion.1.refs_0_), channel_id=1, source_target_pairs={{0,8},{1,3},{2,10},{3,5},{4,12},{5,7},{6,14},{7,1},{8,16},{9,11},{... | collective-permute-start | bytes 1179656 | tf_op jit(solution)/shard_map/ppermute | solution.py:263
  9.1 2.5 %collective-permute-start.2 = (f32[2,32,1536]{2,1,0:T(8,128)S(1)}, f32[2,32,1536]{2,1,0:T(8,128)S(1)}, u32[]{:S(2)}, u32[]{:S(2)}) collective-permute-start(f32[2,32,1536]{2,1,0:T(8,128)S(1)} %pad_maximum_fusion.1.refs_0_), channel_id=1, source_target_pairs={{0,16},{1,5},{2,18},{3,7},{4,20},{5,1},{6,22},{7,3},{8,24},{9,13},... | collective-permute-start | bytes 1179656 | tf_op jit(solution)/shard_map/ppermute | solution.py:263
  11.6 1.2 collective-permute-start.3
  12.7 0.1 stack.32.place
  12.8 2.2 %copy-done = f32[2048,512]{1,0:T(8,128)S(1)} copy-done((f32[2048,512]{1,0:T(8,128)S(1)}, f32[2048,512]{1,0:T(8,128)}, u32[]{:S(2)}) %copy-start) | copy-done | bytes 4194328
  15.0 1.0 split.1
  16.0 0.0 copy-done.1
  16.0 2.9 %carry.3 = (f32[4,4,1,32,512]{4,3,2,1,0:T(8,128)S(1)}, f32[4,4,1,32,512]{4,3,2,1,0:T(8,128)S(1)}) custom-call(s32[5]{0:T(128)S(1)} %stack.32.place, bf16[4,512,512]{2,1,0:T(8,128)(2,1)S(1)} %get-tuple-element.13.hi_ref, bf16[4,512,512]{2,1,0:T(8,128)(2,1)S(1)} %get-tuple-element.14.lo_ref, f32[512,256]{1,0:T(8,128)S(1)} %copy-done.1), custom_call_target="tpu_custom_call" | custom-call | flops 1000 | bytes 1000 | tf_op jit(solution)/shard_map/carry/pallas_call | solution.py:131
  19.0 11.1 %collective-permute-done.5.refs_1_ = f32[512,256]{1,0:T(8,128)} collective-permute-done((f32[512,256]{1,0:T(8,128)}, f32[512,256]{1,0:T(8,128)}, u32[]{:S(2)}, u32[]{:S(2)}) %collective-permute-start.5) | collective-permute-done | bytes 524320 | tf_op jit(solution)/shard_map/ppermute | solution.py:279
  30.1 0.8 collective-permute-start.4
  30.9 2.2 %collective-permute-done.4 = f32[4,4,1,32,512]{4,3,1,2,0:T(8,128)S(1)} collective-permute-done((f32[4,4,1,32,512]{4,3,1,2,0:T(8,128)S(1)}, f32[4,4,1,32,512]{4,3,1,2,0:T(8,128)S(1)}, u32[]{:S(2)}, u32[]{:S(2)}) %collective-permute-start.4) | collective-permute-done | bytes 1048608 | tf_op jit(solution)/shard_map/ppermute | solution.py:263
  33.2 0.1 broadcast_add_fusion
  33.3 0.1 fusion.13
  33.5 1.9 %collective-permute-start.7 = (f32[4,1,32,512]{3,2,0,1:T(8,128)S(1)}, f32[4,1,32,512]{3,2,0,1:T(8,128)S(1)}, u32[]{:S(2)}, u32[]{:S(2)}) collective-permute-start(f32[4,1,32,512]{3,2,0,1:T(8,128)S(1)} %get-tuple-element.32), channel_id=1, source_target_pairs={{0,4},{1,17},{2,6},{3,19},{4,0},{5,21},{6,2},{7,23},{8,12},{9,25},... | collective-permute-start | bytes 786440 | tf_op jit(solution)/shard_map/ppermute | solution.py:263
  35.3 0.4 collective-permute-start.8
  35.7 2.3 %collective-permute-start.9 = (f32[4,1,32,512]{3,2,1,0:T(8,128)S(1)}, f32[4,1,32,512]{3,2,1,0:T(8,128)S(1)}, u32[]{:S(2)}, u32[]{:S(2)}) collective-permute-start(f32[4,1,32,512]{3,2,1,0:T(8,128)S(1)} %get-tuple-element.31), channel_id=1, source_target_pairs={{0,6},{1,25},{2,0},{3,27},{4,2},{5,29},{6,4},{7,31},{8,14},{9,1},{... | collective-permute-start | bytes 786440 | tf_op jit(solution)/shard_map/ppermute | solution.py:263
  38.0 5.1 %carry.4 = (f32[4,4,2,32,512]{4,3,2,1,0:T(8,128)S(1)}, f32[4,4,2,32,512]{4,3,2,1,0:T(8,128)S(1)}) custom-call(s32[5]{0:T(128)S(1)} %stack.32.place, bf16[4,512,512]{2,1,0:T(8,128)(2,1)S(1)} %get-tuple-element.13.hi_ref, bf16[4,512,512]{2,1,0:T(8,128)(2,1)S(1)} %get-tuple-element.14.lo_ref, f32[512,256]{1,0:T(8,128)S(1)} %collective-permute-done.6.refs_2_.refs_0_, ...), custom_call_target="tpu_custom_call" | custom-call | flops 99999997952 | bytes 1000 | tf_op jit(solution)/shard_map/carry/pallas_call | solution.py:131
  43.1 1.3 %collective-permute-start.10 = (f32[4,4,2,32,512]{4,3,2,1,0:T(8,128)S(1)}, f32[4,4,2,32,512]{4,3,2,1,0:T(8,128)S(1)}, u32[]{:S(2)}, u32[]{:S(2)}) collective-permute-start(f32[4,4,2,32,512]{4,3,2,1,0:T(8,128)S(1)} %get-tuple-element.18), channel_id=1, source_target_pairs={{0,1},{1,0},{2,3},{3,2},{4,5},{5,4},{6,7},{7,6},{8,9},{9,8},{10,11... | collective-permute-start | bytes 6291464 | tf_op jit(solution)/shard_map/ppermute | solution.py:263
  44.5 0.1 fusion.16
  44.6 0.1 collective-permute-done.14.refs_0_
  44.7 3.5 %carry.5 = (f32[4,4,1,32,512]{4,3,2,1,0:T(8,128)S(1)}, f32[4,4,1,32,512]{4,3,2,1,0:T(8,128)S(1)}) custom-call(s32[5]{0:T(128)S(1)} %stack.32.place, bf16[4,512,512]{2,1,0:T(8,128)(2,1)S(1)} %get-tuple-element.13.hi_ref, bf16[4,512,512]{2,1,0:T(8,128)(2,1)S(1)} %get-tuple-element.14.lo_ref, f32[512,256]{1,0:T(8,128)} %collective-permute-done.14.refs_0_), custom_call_target="tpu_custom_call" | custom-call | flops 99999997952 | bytes 1000 | tf_op jit(solution)/shard_map/carry/pallas_call | solution.py:131
  48.2 0.9 collective-permute-start.15
  49.1 0.3 fusion.1
  49.4 2.2 %collective-permute-start.11 = (f32[4,2,32,512]{3,2,1,0:T(8,128)S(1)}, f32[4,2,32,512]{3,2,1,0:T(8,128)S(1)}, u32[]{:S(2)}, u32[]{:S(2)}) collective-permute-start(f32[4,2,32,512]{3,2,1,0:T(8,128)S(1)} %get-tuple-element.26), channel_id=1, source_target_pairs={{0,4},{1,17},{2,6},{3,19},{4,0},{5,21},{6,2},{7,23},{8,12},{9,25},... | collective-permute-start | bytes 1572872 | tf_op jit(solution)/shard_map/ppermute | solution.py:263
  51.6 0.4 collective-permute-start.12
  52.0 2.3 %collective-permute-start.13 = (f32[4,2,32,512]{3,2,1,0:T(8,128)S(1)}, f32[4,2,32,512]{3,2,1,0:T(8,128)S(1)}, u32[]{:S(2)}, u32[]{:S(2)}) collective-permute-start(f32[4,2,32,512]{3,2,1,0:T(8,128)S(1)} %get-tuple-element.25), channel_id=1, source_target_pairs={{0,6},{1,25},{2,0},{3,27},{4,2},{5,29},{6,4},{7,31},{8,14},{9,1},{... | collective-permute-start | bytes 1572872 | tf_op jit(solution)/shard_map/ppermute | solution.py:263
  54.3 0.1 fusion.7
  54.4 0.1 collective-permute-start.16
  54.5 0.6 collective-permute-start.17
  55.1 4.3 %collective-permute-done.11 = f32[4,2,32,512]{3,2,1,0:T(8,128)S(1)} collective-permute-done((f32[4,2,32,512]{3,2,1,0:T(8,128)S(1)}, f32[4,2,32,512]{3,2,1,0:T(8,128)S(1)}, u32[]{:S(2)}, u32[]{:S(2)}) %collective-permute-start.11) | collective-permute-done | bytes 524320 | tf_op jit(solution)/shard_map/ppermute | solution.py:263
  59.4 1.9 %collective-permute-start.18 = (f32[4,1,32,512]{3,2,1,0:T(8,128)S(1)}, f32[4,1,32,512]{3,2,1,0:T(8,128)S(1)}, u32[]{:S(2)}, u32[]{:S(2)}) collective-permute-start(f32[4,1,32,512]{3,2,1,0:T(8,128)S(1)} %get-tuple-element.28), channel_id=1, source_target_pairs={{0,6},{1,25},{2,0},{3,27},{4,2},{5,29},{6,4},{7,31},{8,14},{9,1},{... | collective-permute-start | bytes 786440 | tf_op jit(solution)/shard_map/ppermute | solution.py:263
  61.3 3.7 %collective-permute-done.12 = f32[4,2,32,512]{3,2,1,0:T(8,128)S(1)} collective-permute-done((f32[4,2,32,512]{3,2,1,0:T(8,128)S(1)}, f32[4,2,32,512]{3,2,1,0:T(8,128)S(1)}, u32[]{:S(2)}, u32[]{:S(2)}) %collective-permute-start.12) | collective-permute-done | bytes 524320 | tf_op jit(solution)/shard_map/ppermute | solution.py:263
  65.0 0.3 fusion.4.refs_0_
  65.3 2.6 %collective-permute-done.16 = f32[4,1,32,512]{3,2,0,1:T(8,128)S(1)} collective-permute-done((f32[4,1,32,512]{3,2,0,1:T(8,128)S(1)}, f32[4,1,32,512]{3,2,0,1:T(8,128)S(1)}, u32[]{:S(2)}, u32[]{:S(2)}) %collective-permute-start.16) | collective-permute-done | bytes 262176 | tf_op jit(solution)/shard_map/ppermute | solution.py:263
  67.9 2.7 %collective-permute-done.17 = f32[4,1,32,512]{3,2,0,1:T(8,128)S(1)} collective-permute-done((f32[4,1,32,512]{3,2,0,1:T(8,128)S(1)}, f32[4,1,32,512]{3,2,0,1:T(8,128)S(1)}, u32[]{:S(2)}, u32[]{:S(2)}) %collective-permute-start.17) | collective-permute-done | bytes 262176 | tf_op jit(solution)/shard_map/ppermute | solution.py:263
  70.6 0.1 fusion.11
  70.7 0.1 pad_maximum_fusion
  70.8 0.1 slice_bitcast_fusion.1
  70.9 2.1 %collective-permute-start.19 = (f32[4,32,512]{2,1,0:T(8,128)S(1)}, f32[4,32,512]{2,1,0:T(8,128)S(1)}, u32[]{:S(2)}, u32[]{:S(2)}) collective-permute-start(f32[4,32,512]{2,1,0:T(8,128)S(1)} %get-tuple-element.35), channel_id=1, source_target_pairs={{0,16},{1,5},{2,18},{3,7},{4,20},{5,1},{6,22},{7,3},{8,24},{9,13},... | collective-permute-start | bytes 786440 | tf_op jit(solution)/shard_map/ppermute | solution.py:263
  73.0 0.3 collective-permute-start.20
  73.3 2.4 %collective-permute-start.21 = (f32[4,32,512]{2,1,0:T(8,128)S(1)}, f32[4,32,512]{2,1,0:T(8,128)S(1)}, u32[]{:S(2)}, u32[]{:S(2)}) collective-permute-start(f32[4,32,512]{2,1,0:T(8,128)S(1)} %get-tuple-element.34), channel_id=1, source_target_pairs={{0,24},{1,7},{2,26},{3,1},{4,28},{5,3},{6,30},{7,5},{8,0},{9,15},{... | collective-permute-start | bytes 786440 | tf_op jit(solution)/shard_map/ppermute | solution.py:263
  75.7 2.3 %collective-permute-done.19 = f32[4,32,512]{2,1,0:T(8,128)S(1)} collective-permute-done((f32[4,32,512]{2,1,0:T(8,128)S(1)}, f32[4,32,512]{2,1,0:T(8,128)S(1)}, u32[]{:S(2)}, u32[]{:S(2)}) %collective-permute-start.19) | collective-permute-done | bytes 262176 | tf_op jit(solution)/shard_map/ppermute | solution.py:263
  78.0 2.8 %collective-permute-done.20 = f32[4,32,512]{2,1,0:T(8,128)S(1)} collective-permute-done((f32[4,32,512]{2,1,0:T(8,128)S(1)}, f32[4,32,512]{2,1,0:T(8,128)S(1)}, u32[]{:S(2)}, u32[]{:S(2)}) %collective-permute-start.20) | collective-permute-done | bytes 262176 | tf_op jit(solution)/shard_map/ppermute | solution.py:263
  80.8 0.1 fusion.5
  80.9 5.9 %collective-permute-start.22 = (f32[4,32,256]{2,1,0:T(8,128)S(1)}, f32[4,32,256]{2,1,0:T(8,128)S(1)}, u32[]{:S(2)}, u32[]{:S(2)}) collective-permute-start(f32[4,32,256]{2,1,0:T(8,128)S(1)} %slice.161), channel_id=1, source_target_pairs={{0,32},{1,33},{2,34},{3,35},{4,36},{5,37},{6,38},{7,39},{8,40},{9,... | collective-permute-start | bytes 393224 | tf_op jit(solution)/shard_map/ppermute | solution.py:263
  86.8 2.5 %collective-permute-done.22 = f32[4,32,256]{2,1,0:T(8,128)S(1)} collective-permute-done((f32[4,32,256]{2,1,0:T(8,128)S(1)}, f32[4,32,256]{2,1,0:T(8,128)S(1)}, u32[]{:S(2)}, u32[]{:S(2)}) %collective-permute-start.22) | collective-permute-done | bytes 131104 | tf_op jit(solution)/shard_map/ppermute | solution.py:263
  89.3 1.3 %grad.1 = f32[4,384,128]{2,1,0:T(8,128)S(1)} custom-call(s32[5]{0:T(128)S(1)} %stack.32.place, f32[2,32,1536]{2,1,0:T(8,128)S(1)} %pad_maximum_fusion.1.refs_0_, f32[2,32,1536]{2,1,0:T(8,128)S(1)} %collective-permute-done.1.refs_3_.refs_1_, f32[2,32,1536]{2,1,0:T(8,128)S(1)} %collective-permute-done.2.refs_4_.refs_2_, ...), custom_call_target="tpu_custom_call" | custom-call | flops 1000 | bytes 1000 | tf_op jit(solution)/shard_map/grad/pallas_call | solution.py:181
  90.6 0.0 copy-start.2
  90.6 0.0 copy-start.3
  90.7 1.6 %collective-permute-start.23 = (f32[384,128]{1,0:T(8,128)S(1)}, f32[384,128]{1,0:T(8,128)S(1)}, u32[]{:S(2)}, u32[]{:S(2)}) collective-permute-start(f32[384,128]{1,0:T(8,128)S(1)} %get-tuple-element.38), channel_id=1, source_target_pairs={{0,4},{1,17},{2,6},{3,19},{4,0},{5,21},{6,2},{7,23},{8,12},{9,25},... | collective-permute-start | bytes 589832 | tf_op jit(solution)/shard_map/ppermute | solution.py:263
  92.3 1.4 %collective-permute-start.24 = (f32[384,128]{1,0:T(8,128)S(1)}, f32[384,128]{1,0:T(8,128)S(1)}, u32[]{:S(2)}, u32[]{:S(2)}) collective-permute-start(f32[384,128]{1,0:T(8,128)S(1)} %get-tuple-element.36), channel_id=1, source_target_pairs={{0,2},{1,9},{2,4},{3,11},{4,6},{5,13},{6,0},{7,15},{8,10},{9,17},{... | collective-permute-start | bytes 589832 | tf_op jit(solution)/shard_map/ppermute | solution.py:263
  93.7 1.3 %collective-permute-start.25 = (f32[384,128]{1,0:T(8,128)S(1)}, f32[384,128]{1,0:T(8,128)S(1)}, u32[]{:S(2)}, u32[]{:S(2)}) collective-permute-start(f32[384,128]{1,0:T(8,128)S(1)} %get-tuple-element.37), channel_id=1, source_target_pairs={{0,6},{1,25},{2,0},{3,27},{4,2},{5,29},{6,4},{7,31},{8,14},{9,1},{... | collective-permute-start | bytes 589832 | tf_op jit(solution)/shard_map/ppermute | solution.py:263
  95.0 1.9 %collective-permute-done.23 = f32[384,128]{1,0:T(8,128)S(1)} collective-permute-done((f32[384,128]{1,0:T(8,128)S(1)}, f32[384,128]{1,0:T(8,128)S(1)}, u32[]{:S(2)}, u32[]{:S(2)}) %collective-permute-start.23) | collective-permute-done | bytes 196640 | tf_op jit(solution)/shard_map/ppermute | solution.py:263
  96.9 2.0 %collective-permute-done.24 = f32[384,128]{1,0:T(8,128)S(1)} collective-permute-done((f32[384,128]{1,0:T(8,128)S(1)}, f32[384,128]{1,0:T(8,128)S(1)}, u32[]{:S(2)}, u32[]{:S(2)}) %collective-permute-start.24) | collective-permute-done | bytes 196640 | tf_op jit(solution)/shard_map/ppermute | solution.py:263
  99.0 20.4 %all_to_all.5 = f32[32,12,128]{2,1,0:T(8,128)S(1)} all-to-all(f32[32,12,128]{2,1,0:T(8,128)S(1)} %reshape.194), channel_id=1, replica_groups={{0,8,16,24,32,40,48,56,64,72,80,88,96,104,112,120,128,136,144,152,160,1..., dimensions={0} | all-to-all | bytes 393216 | tf_op jit(solution)/shard_map/all_to_all | solution.py:293
  119.4 5.6 %collective-permute-start.26 = (f32[4,12,128]{2,1,0:T(8,128)S(1)}, f32[4,12,128]{2,1,0:T(8,128)S(1)}, u32[]{:S(2)}, u32[]{:S(2)}) collective-permute-start(f32[4,12,128]{2,1,0:T(8,128)S(1)} %reduce_sum.9.own), channel_id=1, source_target_pairs={{0,1},{1,0},{2,3},{3,2},{4,5},{5,4},{6,7},{7,6},{8,9},{9,8},{10,11... | collective-permute-start | bytes 73736 | tf_op jit(solution)/shard_map/ppermute | solution.py:263
  125.0 0.9 collective-permute-done.26.got
  125.9 1.3 arrange.1
  127.1 0.1 multiply_reduce_fusion
  127.2 0.5 multiply_subtract_fusion
  (27 shorter events, 0.2 us)
Async XLA Ops:
  0.6 6.2 %collective-permute-start = (f32[32,1536]{1,0:T(8,128)}, f32[32,1536]{1,0:T(8,128)S(1)}, u32[]{:S(2)}, u32[]{:S(2)}) collective-permute-start(f32[32,1536]{1,0:T(8,128)} %param.6), channel_id=1, source_target_pairs={{0,1},{1,0},{2,3},{3,2},{4,5},{5,4},{6,7},{7,6},{8,9},{9,8},{10,11... | collective-permute-start | bytes 589832 | tf_op jit(solution)/shard_map/ppermute | solution.py:263
  4.0 26.1 %collective-permute-start.5 = (f32[512,256]{1,0:T(8,128)}, f32[512,256]{1,0:T(8,128)}, u32[]{:S(2)}, u32[]{:S(2)}) collective-permute-start(f32[512,256]{1,0:T(8,128)} %refs_0_.1), channel_id=1, source_target_pairs={{0,128},{64,192},{128,0},{192,64},{1,129},{65,193},{129,1},{193,65... | collective-permute-start | bytes 1572872 | tf_op jit(solution)/shard_map/ppermute | solution.py:279
  5.2 25.6 %collective-permute-start.6 = (f32[512,256]{1,0:T(8,128)}, f32[512,256]{1,0:T(8,128)S(1)}, u32[]{:S(2)}, u32[]{:S(2)}) collective-permute-start(f32[512,256]{1,0:T(8,128)} %refs_0_.1), channel_id=1, source_target_pairs={{0,64},{64,0},{128,192},{192,128},{1,65},{65,1},{129,193},{193,129... | collective-permute-start | bytes 1572872 | tf_op jit(solution)/shard_map/ppermute | solution.py:278
  7.8 23.1 %collective-permute-start.1 = (f32[2,32,1536]{2,1,0:T(8,128)S(1)}, f32[2,32,1536]{2,1,0:T(8,128)S(1)}, u32[]{:S(2)}, u32[]{:S(2)}) collective-permute-start(f32[2,32,1536]{2,1,0:T(8,128)S(1)} %pad_maximum_fusion.1.refs_0_), channel_id=1, source_target_pairs={{0,8},{1,3},{2,10},{3,5},{4,12},{5,7},{6,14},{7,1},{8,16},{9,11},{... | collective-permute-start | bytes 1179656 | tf_op jit(solution)/shard_map/ppermute | solution.py:263
  9.1 21.8 %collective-permute-start.2 = (f32[2,32,1536]{2,1,0:T(8,128)S(1)}, f32[2,32,1536]{2,1,0:T(8,128)S(1)}, u32[]{:S(2)}, u32[]{:S(2)}) collective-permute-start(f32[2,32,1536]{2,1,0:T(8,128)S(1)} %pad_maximum_fusion.1.refs_0_), channel_id=1, source_target_pairs={{0,16},{1,5},{2,18},{3,7},{4,20},{5,1},{6,22},{7,3},{8,24},{9,13},... | collective-permute-start | bytes 1179656 | tf_op jit(solution)/shard_map/ppermute | solution.py:263
  11.6 19.3 %collective-permute-start.3 = (f32[2,32,1536]{2,1,0:T(8,128)S(1)}, f32[2,32,1536]{2,1,0:T(8,128)S(1)}, u32[]{:S(2)}, u32[]{:S(2)}) collective-permute-start(f32[2,32,1536]{2,1,0:T(8,128)S(1)} %pad_maximum_fusion.1.refs_0_), channel_id=1, source_target_pairs={{0,24},{1,7},{2,26},{3,1},{4,28},{5,3},{6,30},{7,5},{8,0},{9,15},{... | collective-permute-start | bytes 1179656 | tf_op jit(solution)/shard_map/ppermute | solution.py:263
  12.8 2.2 %copy-start = (f32[2048,512]{1,0:T(8,128)S(1)}, f32[2048,512]{1,0:T(8,128)}, u32[]{:S(2)}) copy-start(f32[2048,512]{1,0:T(8,128)} %param.5) | copy-start | bytes 12582916
  15.0 1.0 copy-start.1
  30.1 3.1 %collective-permute-start.4 = (f32[4,4,1,32,512]{4,3,1,2,0:T(8,128)S(1)}, f32[4,4,1,32,512]{4,3,1,2,0:T(8,128)S(1)}, u32[]{:S(2)}, u32[]{:S(2)}) collective-permute-start(f32[4,4,1,32,512]{4,3,1,2,0:T(8,128)S(1)} %bitcast.89), channel_id=1, source_target_pairs={{0,1},{1,0},{2,3},{3,2},{4,5},{5,4},{6,7},{7,6},{8,9},{9,8},{10,11... | collective-permute-start | bytes 3145736 | tf_op jit(solution)/shard_map/ppermute | solution.py:263
  30.9 13.9 %collective-permute-start.14 = (f32[512,256]{1,0:T(8,128)}, f32[512,256]{1,0:T(8,128)}, u32[]{:S(2)}, u32[]{:S(2)}) collective-permute-start(f32[512,256]{1,0:T(8,128)} %collective-permute-done.5.refs_1_), channel_id=1, source_target_pairs={{0,64},{64,0},{128,192},{192,128},{1,65},{65,1},{129,193},{193,129... | collective-permute-start | bytes 1572872 | tf_op jit(solution)/shard_map/ppermute | solution.py:282
  33.5 11.0 %collective-permute-start.7 = (f32[4,1,32,512]{3,2,0,1:T(8,128)S(1)}, f32[4,1,32,512]{3,2,0,1:T(8,128)S(1)}, u32[]{:S(2)}, u32[]{:S(2)}) collective-permute-start(f32[4,1,32,512]{3,2,0,1:T(8,128)S(1)} %get-tuple-element.32), channel_id=1, source_target_pairs={{0,4},{1,17},{2,6},{3,19},{4,0},{5,21},{6,2},{7,23},{8,12},{9,25},... | collective-permute-start | bytes 786440 | tf_op jit(solution)/shard_map/ppermute | solution.py:263
  35.3 9.1 %collective-permute-start.8 = (f32[4,1,32,512]{3,2,0,1:T(8,128)S(1)}, f32[4,1,32,512]{3,2,0,1:T(8,128)S(1)}, u32[]{:S(2)}, u32[]{:S(2)}) collective-permute-start(f32[4,1,32,512]{3,2,0,1:T(8,128)S(1)} %get-tuple-element.30), channel_id=1, source_target_pairs={{0,2},{1,9},{2,4},{3,11},{4,6},{5,13},{6,0},{7,15},{8,10},{9,17},{... | collective-permute-start | bytes 786440 | tf_op jit(solution)/shard_map/ppermute | solution.py:263
  35.7 8.7 %collective-permute-start.9 = (f32[4,1,32,512]{3,2,1,0:T(8,128)S(1)}, f32[4,1,32,512]{3,2,1,0:T(8,128)S(1)}, u32[]{:S(2)}, u32[]{:S(2)}) collective-permute-start(f32[4,1,32,512]{3,2,1,0:T(8,128)S(1)} %get-tuple-element.31), channel_id=1, source_target_pairs={{0,6},{1,25},{2,0},{3,27},{4,2},{5,29},{6,4},{7,31},{8,14},{9,1},{... | collective-permute-start | bytes 786440 | tf_op jit(solution)/shard_map/ppermute | solution.py:263
  43.1 5.9 %collective-permute-start.10 = (f32[4,4,2,32,512]{4,3,2,1,0:T(8,128)S(1)}, f32[4,4,2,32,512]{4,3,2,1,0:T(8,128)S(1)}, u32[]{:S(2)}, u32[]{:S(2)}) collective-permute-start(f32[4,4,2,32,512]{4,3,2,1,0:T(8,128)S(1)} %get-tuple-element.18), channel_id=1, source_target_pairs={{0,1},{1,0},{2,3},{3,2},{4,5},{5,4},{6,7},{7,6},{8,9},{9,8},{10,11... | collective-permute-start | bytes 6291464 | tf_op jit(solution)/shard_map/ppermute | solution.py:263
  48.2 6.1 %collective-permute-start.15 = (f32[4,4,1,32,512]{4,3,1,2,0:T(8,128)S(1)}, f32[4,4,1,32,512]{4,3,1,2,0:T(8,128)S(1)}, u32[]{:S(2)}, u32[]{:S(2)}) collective-permute-start(f32[4,4,1,32,512]{4,3,1,2,0:T(8,128)S(1)} %bitcast.88), channel_id=1, source_target_pairs={{0,1},{1,0},{2,3},{3,2},{4,5},{5,4},{6,7},{7,6},{8,9},{9,8},{10,11... | collective-permute-start | bytes 3145736 | tf_op jit(solution)/shard_map/ppermute | solution.py:263
  49.4 10.0 %collective-permute-start.11 = (f32[4,2,32,512]{3,2,1,0:T(8,128)S(1)}, f32[4,2,32,512]{3,2,1,0:T(8,128)S(1)}, u32[]{:S(2)}, u32[]{:S(2)}) collective-permute-start(f32[4,2,32,512]{3,2,1,0:T(8,128)S(1)} %get-tuple-element.26), channel_id=1, source_target_pairs={{0,4},{1,17},{2,6},{3,19},{4,0},{5,21},{6,2},{7,23},{8,12},{9,25},... | collective-permute-start | bytes 1572872 | tf_op jit(solution)/shard_map/ppermute | solution.py:263
  51.6 13.4 %collective-permute-start.12 = (f32[4,2,32,512]{3,2,1,0:T(8,128)S(1)}, f32[4,2,32,512]{3,2,1,0:T(8,128)S(1)}, u32[]{:S(2)}, u32[]{:S(2)}) collective-permute-start(f32[4,2,32,512]{3,2,1,0:T(8,128)S(1)} %get-tuple-element.24), channel_id=1, source_target_pairs={{0,2},{1,9},{2,4},{3,11},{4,6},{5,13},{6,0},{7,15},{8,10},{9,17},{... | collective-permute-start | bytes 1572872 | tf_op jit(solution)/shard_map/ppermute | solution.py:263
  52.0 13.0 %collective-permute-start.13 = (f32[4,2,32,512]{3,2,1,0:T(8,128)S(1)}, f32[4,2,32,512]{3,2,1,0:T(8,128)S(1)}, u32[]{:S(2)}, u32[]{:S(2)}) collective-permute-start(f32[4,2,32,512]{3,2,1,0:T(8,128)S(1)} %get-tuple-element.25), channel_id=1, source_target_pairs={{0,6},{1,25},{2,0},{3,27},{4,2},{5,29},{6,4},{7,31},{8,14},{9,1},{... | collective-permute-start | bytes 1572872 | tf_op jit(solution)/shard_map/ppermute | solution.py:263
  54.4 13.4 %collective-permute-start.16 = (f32[4,1,32,512]{3,2,0,1:T(8,128)S(1)}, f32[4,1,32,512]{3,2,0,1:T(8,128)S(1)}, u32[]{:S(2)}, u32[]{:S(2)}) collective-permute-start(f32[4,1,32,512]{3,2,0,1:T(8,128)S(1)} %get-tuple-element.29), channel_id=1, source_target_pairs={{0,4},{1,17},{2,6},{3,19},{4,0},{5,21},{6,2},{7,23},{8,12},{9,25},... | collective-permute-start | bytes 786440 | tf_op jit(solution)/shard_map/ppermute | solution.py:263
  54.5 16.1 %collective-permute-start.17 = (f32[4,1,32,512]{3,2,0,1:T(8,128)S(1)}, f32[4,1,32,512]{3,2,0,1:T(8,128)S(1)}, u32[]{:S(2)}, u32[]{:S(2)}) collective-permute-start(f32[4,1,32,512]{3,2,0,1:T(8,128)S(1)} %get-tuple-element.27), channel_id=1, source_target_pairs={{0,2},{1,9},{2,4},{3,11},{4,6},{5,13},{6,0},{7,15},{8,10},{9,17},{... | collective-permute-start | bytes 786440 | tf_op jit(solution)/shard_map/ppermute | solution.py:263
  59.4 11.2 %collective-permute-start.18 = (f32[4,1,32,512]{3,2,1,0:T(8,128)S(1)}, f32[4,1,32,512]{3,2,1,0:T(8,128)S(1)}, u32[]{:S(2)}, u32[]{:S(2)}) collective-permute-start(f32[4,1,32,512]{3,2,1,0:T(8,128)S(1)} %get-tuple-element.28), channel_id=1, source_target_pairs={{0,6},{1,25},{2,0},{3,27},{4,2},{5,29},{6,4},{7,31},{8,14},{9,1},{... | collective-permute-start | bytes 786440 | tf_op jit(solution)/shard_map/ppermute | solution.py:263
  70.9 7.1 %collective-permute-start.19 = (f32[4,32,512]{2,1,0:T(8,128)S(1)}, f32[4,32,512]{2,1,0:T(8,128)S(1)}, u32[]{:S(2)}, u32[]{:S(2)}) collective-permute-start(f32[4,32,512]{2,1,0:T(8,128)S(1)} %get-tuple-element.35), channel_id=1, source_target_pairs={{0,16},{1,5},{2,18},{3,7},{4,20},{5,1},{6,22},{7,3},{8,24},{9,13},... | collective-permute-start | bytes 786440 | tf_op jit(solution)/shard_map/ppermute | solution.py:263
  73.0 7.8 %collective-permute-start.20 = (f32[4,32,512]{2,1,0:T(8,128)S(1)}, f32[4,32,512]{2,1,0:T(8,128)S(1)}, u32[]{:S(2)}, u32[]{:S(2)}) collective-permute-start(f32[4,32,512]{2,1,0:T(8,128)S(1)} %get-tuple-element.33), channel_id=1, source_target_pairs={{0,8},{1,3},{2,10},{3,5},{4,12},{5,7},{6,14},{7,1},{8,16},{9,11},{... | collective-permute-start | bytes 786440 | tf_op jit(solution)/shard_map/ppermute | solution.py:263
  73.3 7.5 %collective-permute-start.21 = (f32[4,32,512]{2,1,0:T(8,128)S(1)}, f32[4,32,512]{2,1,0:T(8,128)S(1)}, u32[]{:S(2)}, u32[]{:S(2)}) collective-permute-start(f32[4,32,512]{2,1,0:T(8,128)S(1)} %get-tuple-element.34), channel_id=1, source_target_pairs={{0,24},{1,7},{2,26},{3,1},{4,28},{5,3},{6,30},{7,5},{8,0},{9,15},{... | collective-permute-start | bytes 786440 | tf_op jit(solution)/shard_map/ppermute | solution.py:263
  80.9 8.3 %collective-permute-start.22 = (f32[4,32,256]{2,1,0:T(8,128)S(1)}, f32[4,32,256]{2,1,0:T(8,128)S(1)}, u32[]{:S(2)}, u32[]{:S(2)}) collective-permute-start(f32[4,32,256]{2,1,0:T(8,128)S(1)} %slice.161), channel_id=1, source_target_pairs={{0,32},{1,33},{2,34},{3,35},{4,36},{5,37},{6,38},{7,39},{8,40},{9,... | collective-permute-start | bytes 393224 | tf_op jit(solution)/shard_map/ppermute | solution.py:263
  90.6 35.3 %copy-start.2 = (f32[1024]{0:T(1024)S(1)}, f32[1024]{0:T(1024)}, u32[]{:S(2)}) copy-start(f32[1024]{0:T(1024)} %param.8) | copy-start | bytes 12292
  90.6 36.6 %copy-start.3 = (f32[6]{0:T(128)S(1)}, f32[6]{0:T(128)}, u32[]{:S(2)}) copy-start(f32[6]{0:T(128)} %param.9) | copy-start | bytes 76
  90.7 6.2 %collective-permute-start.23 = (f32[384,128]{1,0:T(8,128)S(1)}, f32[384,128]{1,0:T(8,128)S(1)}, u32[]{:S(2)}, u32[]{:S(2)}) collective-permute-start(f32[384,128]{1,0:T(8,128)S(1)} %get-tuple-element.38), channel_id=1, source_target_pairs={{0,4},{1,17},{2,6},{3,19},{4,0},{5,21},{6,2},{7,23},{8,12},{9,25},... | collective-permute-start | bytes 589832 | tf_op jit(solution)/shard_map/ppermute | solution.py:263
  92.3 6.6 %collective-permute-start.24 = (f32[384,128]{1,0:T(8,128)S(1)}, f32[384,128]{1,0:T(8,128)S(1)}, u32[]{:S(2)}, u32[]{:S(2)}) collective-permute-start(f32[384,128]{1,0:T(8,128)S(1)} %get-tuple-element.36), channel_id=1, source_target_pairs={{0,2},{1,9},{2,4},{3,11},{4,6},{5,13},{6,0},{7,15},{8,10},{9,17},{... | collective-permute-start | bytes 589832 | tf_op jit(solution)/shard_map/ppermute | solution.py:263
  93.7 5.2 %collective-permute-start.25 = (f32[384,128]{1,0:T(8,128)S(1)}, f32[384,128]{1,0:T(8,128)S(1)}, u32[]{:S(2)}, u32[]{:S(2)}) collective-permute-start(f32[384,128]{1,0:T(8,128)S(1)} %get-tuple-element.37), channel_id=1, source_target_pairs={{0,6},{1,25},{2,0},{3,27},{4,2},{5,29},{6,4},{7,31},{8,14},{9,1},{... | collective-permute-start | bytes 589832 | tf_op jit(solution)/shard_map/ppermute | solution.py:263
  119.4 6.5 %collective-permute-start.26 = (f32[4,12,128]{2,1,0:T(8,128)S(1)}, f32[4,12,128]{2,1,0:T(8,128)S(1)}, u32[]{:S(2)}, u32[]{:S(2)}) collective-permute-start(f32[4,12,128]{2,1,0:T(8,128)S(1)} %reduce_sum.9.own), channel_id=1, source_target_pairs={{0,1},{1,0},{2,3},{3,2},{4,5},{5,4},{6,7},{7,6},{8,9},{9,8},{10,11... | collective-permute-start | bytes 73736 | tf_op jit(solution)/shard_map/ppermute | solution.py:263
